TPU v7x, 32 devices: a whole 2x2x4 slice. The times are simulated.
32 devices in a mesh: row: 4 (over z), col: 8 (over y, x, core).
Axes of the slice: x: 2, y: 2, z: 4, core: 2. Of those that a mesh axis runs over, the one named last changes fastest.
Arguments:
- inputs: bfloat16 [2, 8192, 2048], P(None, 'row', 'col'), may hold values from -6 to 6
- cotangent: bfloat16 [2, 8192, 2048], P(None, 'row', 'col'), may hold values from -6 to 6
- segment: int32 [2, 8192], P(None, 'row'), may hold values from 0 to 31, never falling along the last dimension, each value on 1 to 800 neighbouring positions
- norm_gain: bfloat16 [2048], P(('col', 'row')), may hold values from 0.099609375 to 1.8984375
- w_query: bfloat16 [2048, 2048], P('row', 'col'), may hold values from -0.125 to 0.125
- w_key: bfloat16 [2048, 2048], P('row', 'col'), may hold values from -0.125 to 0.125
- w_value: bfloat16 [2048, 2048], P('row', 'col'), may hold values from -0.125 to 0.125
- w_beta: bfloat16 [2048, 16], P('row', 'col'), may hold values from -0.125 to 0.125
- conv_query: bfloat16 [2048, 4], P(('col', 'row')), may hold values from -3 to 3
- conv_key: bfloat16 [2048, 4], P(('col', 'row')), may hold values from -3 to 3
- conv_value: bfloat16 [2048, 4], P(('col', 'row')), may hold values from -3 to 3
- head_gain: bfloat16 [128], P('row'), may hold values from 0.099609375 to 1.8984375
- w_out: bfloat16 [2048, 2048], P('col', 'row'), may hold values from -0.125 to 0.125
- ffn_gain: bfloat16 [2048], P(('col', 'row')), may hold values from 0.099609375 to 1.8984375
- w_gate: bfloat16 [2048, 5632], P('row', 'col'), may hold values from -0.125 to 0.125
- w_up: bfloat16 [2048, 5632], P('row', 'col'), may hold values from -0.125 to 0.125
- w_down: bfloat16 [5632, 2048], P('col', 'row'), may hold values from -0.078125 to 0.078125
Outputs:
- output: bfloat16 [2, 8192, 2048], P(None, 'row', 'col')
- input_grad: float32 [2, 8192, 2048], P(None, 'row', 'col')
- grad_norm_gain: float32 [2048], P(('col', 'row'))
- grad_w_query: float32 [2048, 2048], P('row', 'col')
- grad_w_key: float32 [2048, 2048], P('row', 'col')
- grad_w_value: float32 [2048, 2048], P('row', 'col')
- grad_w_beta: float32 [2048, 16], P('row', 'col')
- grad_conv_query: float32 [2048, 4], P(('col', 'row'))
- grad_conv_key: float32 [2048, 4], P(('col', 'row'))
- grad_conv_value: float32 [2048, 4], P(('col', 'row'))
- grad_head_gain: float32 [128], P('row')
- grad_w_out: float32 [2048, 2048], P('col', 'row')
- grad_ffn_gain: float32 [2048], P(('col', 'row'))
- grad_w_gate: float32 [2048, 5632], P('row', 'col')
- grad_w_up: float32 [2048, 5632], P('row', 'col')
- grad_w_down: float32 [5632, 2048], P('col', 'row')
Inputs may be any that keep to these rules, and one draw needn't show every extreme that they name: `segment`: along each micro-batch's 8192 tokens the numbers never fall, and each number covers 1 to 800 consecutive tokens.
All inputs are finite; a program needn't handle non-finite values.
Results may differ from a plain program's by a relative error of at most 0.014.
Values may be sent and summed in bfloat16 or wider, within the bound.
No kernel may reach another device: no remote copies, remote signals or barrier semaphores. Data moves between devices by JAX's collectives and lax.ppermute only.
A program may use at most 384 MiB of HBM per device.

v0:
```python
from functools import partial

import jax
import jax.numpy as jnp
from jax import lax
from jax.sharding import PartitionSpec as P

GROUP = 64
SEQ = 2048


EPSILON = 1e-06
HEAD_FLOOR = 0.002
HIGHEST = lax.Precision.HIGHEST


def product(left, right):
    return jnp.dot(left, right, preferred_element_type=jnp.float32)


def cross_rows(left, right):
    return lax.dot_general(
        left, right, (((0,), (0,)), ((), ())), preferred_element_type=jnp.float32
    )


def cross_cols(left, right):
    return lax.dot_general(
        left, right, (((1,), (1,)), ((), ())), preferred_element_type=jnp.float32
    )


def row_total(values):
    return lax.psum(jnp.sum(values, axis=1), "col")


def spread_act(values):
    return lax.all_gather(values, "col", axis=1, tiled=True)


def spread_grad(values):
    return lax.all_gather(values, "col", axis=1, tiled=True)


def share_grad(values):
    return lax.psum_scatter(values, "col", scatter_dimension=1, tiled=True)


def short_conv(pre_values, taps, labels, seq_len):
    token_count = pre_values.shape[0]
    position = lax.iota(jnp.int32, token_count) % seq_len
    total = pre_values * taps[:, 0]
    for offset in range(1, taps.shape[1]):
        shifted = jnp.concatenate(
            [jnp.zeros((offset, pre_values.shape[1]), jnp.float32), pre_values[:-offset]], axis=0
        )
        earlier = jnp.concatenate([jnp.full((offset,), -1, jnp.int32), labels[:-offset]], axis=0)
        keep_mask = ((earlier == labels) & (position >= offset)).astype(jnp.float32)
        total = total + keep_mask[:, None] * shifted * taps[:, offset]
    return total


def block_step(memory, items):
    queries, keys, values, betas, labels, prior = items
    block_len = keys.shape[1]
    same_doc = (labels[:, :, None] == labels[:, None, :]).astype(jnp.float32)
    strict_low = jnp.tril(jnp.ones((block_len, block_len), jnp.float32), -1)
    within_low = jnp.tril(jnp.ones((block_len, block_len), jnp.float32))
    carried = (labels == prior[:, None]).astype(jnp.float32)
    key_key = jnp.einsum("bid,bjd->bij", keys, keys, precision=HIGHEST)
    system = (
        jnp.eye(block_len, dtype=jnp.float32) + betas[:, :, None] * key_key * same_doc * strict_low
    )
    key_state = jnp.einsum("bid,bde->bie", keys, memory, precision=HIGHEST)
    right_side = betas[:, :, None] * (values - carried[:, :, None] * key_state)
    updates = lax.linalg.triangular_solve(
        system, right_side, left_side=True, lower=True, unit_diagonal=True
    )
    query_key = jnp.einsum("bid,bjd->bij", queries, keys, precision=HIGHEST) * same_doc * within_low
    outputs = carried[:, :, None] * jnp.einsum("bid,bde->bie", queries, memory, precision=HIGHEST)
    outputs = outputs + jnp.einsum("bij,bje->bie", query_key, updates, precision=HIGHEST)
    last_doc = (labels == labels[:, -1:]).astype(jnp.float32)
    carry_out = (labels[:, -1] == prior).astype(jnp.float32)
    memory = carry_out[:, None, None] * memory + jnp.einsum(
        "bid,bie->bde", keys, last_doc[:, :, None] * updates, precision=HIGHEST
    )
    return (memory, outputs)


def delta_blocks(queries, keys, values, betas, labels, seq_len, block_len):
    token_count, heads_here, head_size = queries.shape
    sequences = token_count // seq_len
    blocks = seq_len // block_len

    def arrange(array_in):
        shaped = array_in.reshape((sequences, blocks, block_len, heads_here) + array_in.shape[2:])
        moved = jnp.moveaxis(shaped, (1, 3), (0, 2))
        return moved.reshape((blocks, sequences * heads_here, block_len) + array_in.shape[2:])

    label_heads = jnp.broadcast_to(labels[:, None], (token_count, heads_here))
    label_grid = labels.reshape(sequences, blocks, block_len)
    prior = jnp.concatenate(
        [jnp.full((sequences, 1), -1, jnp.int32), label_grid[:, :-1, -1]], axis=1
    )
    prior = jnp.repeat(jnp.transpose(prior), heads_here, axis=1)
    start = jnp.zeros((sequences * heads_here, head_size, head_size), jnp.float32)
    items = (
        arrange(queries),
        arrange(keys),
        arrange(values),
        arrange(betas),
        arrange(label_heads),
        prior,
    )
    memory, outputs = lax.scan(jax.checkpoint(block_step), start, items)
    outputs = outputs.reshape(blocks, sequences, heads_here, block_len, head_size)
    outputs = jnp.moveaxis(outputs, (0, 2), (1, 3))
    return outputs.reshape(token_count, heads_here, head_size)


def local_mixer(labels, query_pre, key_pre, value_pre, beta_pre, conv_q, conv_k, conv_v, gain_head):
    token_count = query_pre.shape[0]
    head_size = gain_head.shape[0]
    heads_here = beta_pre.shape[1]
    shape_heads = (token_count, heads_here, head_size)
    query_act = jax.nn.silu(short_conv(query_pre, conv_q, labels, SEQ)).reshape(shape_heads)
    key_act = jax.nn.silu(short_conv(key_pre, conv_k, labels, SEQ)).reshape(shape_heads)
    value_act = jax.nn.silu(short_conv(value_pre, conv_v, labels, SEQ)).reshape(shape_heads)
    query_unit = (
        query_act
        * lax.rsqrt(jnp.sum(query_act * query_act, axis=-1, keepdims=True) + EPSILON)
        * head_size ** (-0.5)
    )
    key_unit = key_act * lax.rsqrt(jnp.sum(key_act * key_act, axis=-1, keepdims=True) + EPSILON)
    mixed = delta_blocks(
        query_unit, key_unit, value_act, jax.nn.sigmoid(beta_pre), labels, SEQ, GROUP
    )
    head_scale = lax.rsqrt(jnp.maximum(jnp.mean(mixed * mixed, axis=-1, keepdims=True), HEAD_FLOOR))
    normed = mixed * head_scale * gain_head
    return normed.reshape(token_count, heads_here * head_size)


def local(
    inputs,
    cotangent,
    segment,
    norm_gain,
    w_query,
    w_key,
    w_value,
    w_beta,
    conv_query,
    conv_key,
    conv_value,
    head_gain,
    w_out,
    ffn_gain,
    w_gate,
    w_up,
    w_down,
):
    (
        gain_one,
        query_full,
        key_full,
        value_full,
        beta_full,
        convq_full,
        convk_full,
        convv_full,
        head_full,
        gain_two,
        gate_full,
        up_full,
    ) = (
        lax.all_gather(norm_gain, "row", axis=0, tiled=True),
        lax.all_gather(w_query, "row", axis=0, tiled=True),
        lax.all_gather(w_key, "row", axis=0, tiled=True),
        lax.all_gather(w_value, "row", axis=0, tiled=True),
        lax.all_gather(w_beta, "row", axis=0, tiled=True),
        lax.all_gather(conv_query, "row", axis=0, tiled=True),
        lax.all_gather(conv_key, "row", axis=0, tiled=True),
        lax.all_gather(conv_value, "row", axis=0, tiled=True),
        lax.all_gather(head_gain, "row", axis=0, tiled=True),
        lax.all_gather(ffn_gain, "row", axis=0, tiled=True),
        lax.all_gather(w_gate, "row", axis=0, tiled=True),
        lax.all_gather(w_up, "row", axis=0, tiled=True),
    )
    out_full, down_full = (
        lax.all_gather(w_out, "row", axis=1, tiled=True),
        lax.all_gather(w_down, "row", axis=1, tiled=True),
    )
    model_width = query_full.shape[0]
    gain_one_f = gain_one.astype(jnp.float32)
    gain_two_f = gain_two.astype(jnp.float32)
    taps_f = (
        convq_full.astype(jnp.float32),
        convk_full.astype(jnp.float32),
        convv_full.astype(jnp.float32),
        head_full.astype(jnp.float32),
    )
    gain_one_acc = jnp.zeros(gain_one.shape, jnp.float32)
    gain_two_acc = jnp.zeros(gain_two.shape, jnp.float32)
    query_acc = jnp.zeros(query_full.shape, jnp.float32)
    key_acc = jnp.zeros(key_full.shape, jnp.float32)
    value_acc = jnp.zeros(value_full.shape, jnp.float32)
    beta_acc = jnp.zeros(beta_full.shape, jnp.float32)
    convq_acc = jnp.zeros(convq_full.shape, jnp.float32)
    convk_acc = jnp.zeros(convk_full.shape, jnp.float32)
    convv_acc = jnp.zeros(convv_full.shape, jnp.float32)
    head_acc = jnp.zeros(head_full.shape, jnp.float32)
    gate_acc = jnp.zeros(gate_full.shape, jnp.float32)
    up_acc = jnp.zeros(up_full.shape, jnp.float32)
    out_acc = jnp.zeros(out_full.shape, jnp.float32)
    down_acc = jnp.zeros(down_full.shape, jnp.float32)
    outputs_list = []
    grads_list = []
    for batch_index in range(inputs.shape[0]):
        shard_in = inputs[batch_index].astype(jnp.float32)
        labels = segment[batch_index]
        inv_one = lax.rsqrt(row_total(shard_in * shard_in) / model_width + EPSILON)
        norm_one = shard_in * inv_one[:, None]
        act_one = spread_act((norm_one * gain_one_f).astype(jnp.bfloat16))
        query_pre = product(act_one, query_full)
        key_pre = product(act_one, key_full)
        value_pre = product(act_one, value_full)
        beta_pre = product(act_one, beta_full)
        mixed, mixer_back = jax.vjp(
            partial(local_mixer, labels),
            query_pre,
            key_pre,
            value_pre,
            beta_pre,
            taps_f[0],
            taps_f[1],
            taps_f[2],
            taps_f[3],
        )
        mixed_low = mixed.astype(jnp.bfloat16)
        attn_shard = lax.psum_scatter(
            product(mixed_low, out_full), "col", scatter_dimension=1, tiled=True
        )
        resid = shard_in + attn_shard
        inv_two = lax.rsqrt(row_total(resid * resid) / model_width + EPSILON)
        norm_two = resid * inv_two[:, None]
        act_two = spread_act((norm_two * gain_two_f).astype(jnp.bfloat16))
        gate_pre = product(act_two, gate_full)
        up_pre = product(act_two, up_full)
        gate_sig = jax.nn.sigmoid(gate_pre)
        gate_act = gate_pre * gate_sig
        hidden_low = (gate_act * up_pre).astype(jnp.bfloat16)
        ffn_shard = lax.psum_scatter(
            product(hidden_low, down_full).astype(jnp.bfloat16),
            "col",
            scatter_dimension=1,
            tiled=True,
        ).astype(jnp.float32)
        outputs_list.append((resid + ffn_shard).astype(jnp.bfloat16))
        cot_low = cotangent[batch_index]
        cot_full = spread_grad(cot_low)
        down_acc = down_acc + cross_rows(hidden_low, cot_full)
        hidden_grad = cross_cols(cot_full, down_full)
        gate_grad = (hidden_grad * up_pre * gate_sig * (1.0 + gate_pre * (1.0 - gate_sig))).astype(
            jnp.bfloat16
        )
        up_grad = (hidden_grad * gate_act).astype(jnp.bfloat16)
        gate_acc = gate_acc + cross_rows(act_two, gate_grad)
        up_acc = up_acc + cross_rows(act_two, up_grad)
        act_two_grad = share_grad(cross_cols(gate_grad, gate_full) + cross_cols(up_grad, up_full))
        gain_two_acc = gain_two_acc + jnp.sum(act_two_grad * norm_two, axis=0)
        scaled_two = act_two_grad * gain_two_f
        mean_two = row_total(scaled_two * norm_two) / model_width
        resid_grad = cot_low.astype(jnp.float32) + inv_two[:, None] * (
            scaled_two - norm_two * mean_two[:, None]
        )
        attn_full = spread_grad(resid_grad.astype(jnp.bfloat16))
        out_acc = out_acc + cross_rows(mixed_low, attn_full)
        mixed_grad = cross_cols(attn_full, out_full)
        (
            query_grad,
            key_grad,
            value_grad,
            beta_grad,
            convq_grad,
            convk_grad,
            convv_grad,
            head_grad,
        ) = mixer_back(mixed_grad)
        query_low = query_grad.astype(jnp.bfloat16)
        key_low = key_grad.astype(jnp.bfloat16)
        value_low = value_grad.astype(jnp.bfloat16)
        beta_low = beta_grad.astype(jnp.bfloat16)
        query_acc = query_acc + cross_rows(act_one, query_low)
        key_acc = key_acc + cross_rows(act_one, key_low)
        value_acc = value_acc + cross_rows(act_one, value_low)
        beta_acc = beta_acc + cross_rows(act_one, beta_low)
        convq_acc = convq_acc + convq_grad
        convk_acc = convk_acc + convk_grad
        convv_acc = convv_acc + convv_grad
        head_acc = head_acc + head_grad
        act_one_grad = share_grad(
            cross_cols(query_low, query_full)
            + cross_cols(key_low, key_full)
            + cross_cols(value_low, value_full)
            + cross_cols(beta_low, beta_full)
        )
        gain_one_acc = gain_one_acc + jnp.sum(act_one_grad * norm_one, axis=0)
        scaled_one = act_one_grad * gain_one_f
        mean_one = row_total(scaled_one * norm_one) / model_width
        grads_list.append(
            resid_grad + inv_one[:, None] * (scaled_one - norm_one * mean_one[:, None])
        )
    (
        grad_gain_one,
        grad_query,
        grad_key,
        grad_value,
        grad_beta,
        grad_convq,
        grad_convk,
        grad_convv,
        grad_head_part,
        grad_gain_two,
        grad_gate,
        grad_up,
    ) = (
        lax.psum_scatter(
            gain_one_acc.astype(jnp.bfloat16), "row", scatter_dimension=0, tiled=True
        ).astype(jnp.float32),
        lax.psum_scatter(
            query_acc.astype(jnp.bfloat16), "row", scatter_dimension=0, tiled=True
        ).astype(jnp.float32),
        lax.psum_scatter(
            key_acc.astype(jnp.bfloat16), "row", scatter_dimension=0, tiled=True
        ).astype(jnp.float32),
        lax.psum_scatter(
            value_acc.astype(jnp.bfloat16), "row", scatter_dimension=0, tiled=True
        ).astype(jnp.float32),
        lax.psum_scatter(
            beta_acc.astype(jnp.bfloat16), "row", scatter_dimension=0, tiled=True
        ).astype(jnp.float32),
        lax.psum_scatter(
            convq_acc.astype(jnp.bfloat16), "row", scatter_dimension=0, tiled=True
        ).astype(jnp.float32),
        lax.psum_scatter(
            convk_acc.astype(jnp.bfloat16), "row", scatter_dimension=0, tiled=True
        ).astype(jnp.float32),
        lax.psum_scatter(
            convv_acc.astype(jnp.bfloat16), "row", scatter_dimension=0, tiled=True
        ).astype(jnp.float32),
        lax.psum_scatter(
            head_acc.astype(jnp.bfloat16), "row", scatter_dimension=0, tiled=True
        ).astype(jnp.float32),
        lax.psum_scatter(
            gain_two_acc.astype(jnp.bfloat16), "row", scatter_dimension=0, tiled=True
        ).astype(jnp.float32),
        lax.psum_scatter(
            gate_acc.astype(jnp.bfloat16), "row", scatter_dimension=0, tiled=True
        ).astype(jnp.float32),
        lax.psum_scatter(
            up_acc.astype(jnp.bfloat16), "row", scatter_dimension=0, tiled=True
        ).astype(jnp.float32),
    )
    grad_out, grad_down = (
        lax.psum_scatter(
            out_acc.astype(jnp.bfloat16), "row", scatter_dimension=1, tiled=True
        ).astype(jnp.float32),
        lax.psum_scatter(
            down_acc.astype(jnp.bfloat16), "row", scatter_dimension=1, tiled=True
        ).astype(jnp.float32),
    )
    grad_head = lax.psum(grad_head_part, "col")
    return (
        jnp.stack(outputs_list),
        jnp.stack(grads_list),
        grad_gain_one,
        grad_query,
        grad_key,
        grad_value,
        grad_beta,
        grad_convq,
        grad_convk,
        grad_convv,
        grad_head,
        grad_out,
        grad_gain_two,
        grad_gate,
        grad_up,
        grad_down,
    )


def solution(mesh):
    in_specs = (
        P(None, "row", "col"),
        P(None, "row", "col"),
        P(None, "row"),
        P(("col", "row")),
        P("row", "col"),
        P("row", "col"),
        P("row", "col"),
        P("row", "col"),
        P(("col", "row"), None),
        P(("col", "row"), None),
        P(("col", "row"), None),
        P("row"),
        P("col", "row"),
        P(("col", "row")),
        P("row", "col"),
        P("row", "col"),
        P("col", "row"),
    )
    out_specs = (
        P(None, "row", "col"),
        P(None, "row", "col"),
        P(("col", "row")),
        P("row", "col"),
        P("row", "col"),
        P("row", "col"),
        P("row", "col"),
        P(("col", "row"), None),
        P(("col", "row"), None),
        P(("col", "row"), None),
        P("row"),
        P("col", "row"),
        P(("col", "row")),
        P("row", "col"),
        P("row", "col"),
        P("col", "row"),
    )
    return jax.shard_map(local, mesh=mesh, in_specs=in_specs, out_specs=out_specs, check_vma=False)
```

profile of v0, /device:TPU:0, one launch (start us, length us, event | category | flops | bytes accessed | tf_op | source)
XLA Modules:
  0.0 4861.2 jit_solution(419051070172942538)
XLA Ops:
  113.8 23.5 all-gather.23.cloned.1.call-done
  179.0 45.0 all-gather.21.cloned.1.call-done
  255.5 661.1 %while.77 = (s32[]{:T(128)}, f32[2,128,128]{2,1,0:T(8,128)S(1)}, f32[32,2,64,128]{3,2,1,0:T(8,128)S(1)}, f32[32,2,128,128]{3,2,1,0:T(8,128)}, s32[32,2,64]{2,1,0...) while((s32[]{:T(128)}, f32[2,128,128]{2,1,0:T(8,128)S(1)}, ...), condition=%wide.region_16.18_spmd.clone, body=%wide.region_15.17_spmd.clone.sunk | while | flops 126243400 | bytes 2158054 | solution.py:115
  986.4 595.8 %while.76 = (s32[]{:T(128)}, f32[2,128,128]{2,1,0:T(8,128)S(1)}, f32[32,2,64,128]{3,2,1,0:T(8,128)}, f32[32,2,128,128]{3,2,1,0:T(8,128)}, s32[32,2,64]{2,1,0:T(2...) while((s32[]{:T(128)}, f32[2,128,128]{2,1,0:T(8,128)S(1)}, ...), condition=%wide.region_5.7_spmd.clone, body=%wide.region_4.6_spmd.clone.sunk | while | flops 126243400 | bytes 2125794 | solution.py:115
  1625.8 103.6 %reduce-scatter.28.cloned.1.call-done = f32[2048,256]{1,0:T(8,128)} async-done(((f32[2048,2048]{1,0:T(8,128)}), f32[2048,256]{1,0:T(8,128)}) %reduce-scatter.28.cloned.1.call-update) | async-done | bytes 2097168 | tf_op jit(solution)/shard_map/reduce_scatter | solution.py:240
  1729.4 119.6 %reduce-scatter.32.cloned.1.call-done = f32[2048,256]{1,0:T(8,128)} async-done(((f32[2048,2048]{1,0:T(8,128)}), f32[2048,256]{1,0:T(8,128)}) %reduce-scatter.32.cloned.1.call-update) | async-done | bytes 2097168 | tf_op jit(solution)/shard_map/reduce_scatter | solution.py:240
  1853.4 23.9 all-reduce.72
  1883.5 26.2 all-gather.33.cloned.1.call-done
  1909.7 57.0 %all-gather.31.cloned.1.call-done = bf16[2048,2048]{1,0:T(8,128)(2,1)} async-done(((bf16[2048,256]{1,0:T(8,128)(2,1)}), bf16[2048,2048]{1,0:T(8,128)(2,1)}) %all-gather.31.cloned.1.call-update) | async-done | bytes 8388624 | tf_op jit(solution)/shard_map/all_gather | solution.py:38
  1977.7 49.8 %all-gather.35.cloned.1.call-done = bf16[2048,704]{0,1:T(8,128)(2,1)} async-done(((bf16[512,704]{0,1:T(8,128)(2,1)}), bf16[2048,704]{0,1:T(8,128)(2,1)}) %all-gather.35.cloned.1.call-update) | async-done | bytes 2883600 | tf_op jit(solution)/shard_map/all_gather | solution.py:187
  2038.5 48.3 all-gather.37.cloned.1.call-done
  2086.8 57.2 %all-gather.47.cloned.1.call-done = bf16[1,2048,2048]{2,1,0:T(8,128)(2,1)} async-done(((bf16[1,2048,256]{2,1,0:T(8,128)(2,1)}), bf16[1,2048,2048]{2,1,0:T(8,128)(2,1)}) %all-gather.47.cloned.1.call-update) | async-done | bytes 8388624 | tf_op jit(solution)/shard_map/all_gather | solution.py:42
  2187.5 116.0 %reduce-scatter.36.cloned.1.call-done = f32[2048,256]{1,0:T(8,128)} async-done(((f32[2048,2048]{1,0:T(8,128)}), f32[2048,256]{1,0:T(8,128)}) %reduce-scatter.36.cloned.1.call-update) | async-done | bytes 2097168 | tf_op jit(solution)/shard_map/reduce_scatter | solution.py:46
  2308.0 55.5 %all-gather.41.cloned.1.call-done = bf16[2048,2048]{1,0:T(8,128)(2,1)} async-done(((bf16[2048,256]{1,0:T(8,128)(2,1)}), bf16[2048,2048]{1,0:T(8,128)(2,1)}) %all-gather.41.cloned.1.call-update) | async-done | bytes 8388624 | tf_op jit(solution)/shard_map/all_gather | solution.py:38
  2382.7 39.2 all-gather.49.cloned.1.call-done
  2473.3 104.5 %reduce-scatter.40.cloned.1.call-done = f32[2048,256]{1,0:T(8,128)} async-done(((f32[2048,2048]{1,0:T(8,128)}), f32[2048,256]{1,0:T(8,128)}) %reduce-scatter.40.cloned.1.call-update) | async-done | bytes 2097168 | tf_op jit(solution)/shard_map/reduce_scatter | solution.py:46
  2581.3 23.3 all-reduce.71
  2604.6 47.7 reduce-scatter.34.cloned.1.call-done
  2748.8 23.7 all-gather.43.cloned.1.call-done
  2796.6 717.2 %while.79 = (s32[]{:T(128)}, f32[2,128,128]{2,1,0:T(8,128)S(1)}, f32[32,2,64,128]{3,2,1,0:T(8,128)S(1)}, f32[32,2,64,128]{3,2,0,1:T(8,128)}, f32[32,2,64,128]{3,...) while((s32[]{:T(128)}, f32[2,128,128]{2,1,0:T(8,128)S(1)}, ...), condition=%wide.region_42.46_spmd.clone, body=%wide.region_39.45_spmd.clone.sunk | while | flops 321573312 | bytes 5961259 | solution.py:115
  3518.6 717.7 %while.78 = (s32[]{:T(128)}, f32[2,128,128]{2,1,0:T(8,128)S(1)}, f32[32,2,64,128]{3,2,1,0:T(8,128)S(1)}, f32[32,2,64,128]{3,2,0,1:T(8,128)}, f32[32,2,64,128]{3,...) while((s32[]{:T(128)}, f32[2,128,128]{2,1,0:T(8,128)S(1)}, ...), condition=%wide.region_29.33_spmd.clone, body=%wide.region_26.32_spmd.clone.sunk | while | flops 321573312 | bytes 5961259 | solution.py:115
  4567.1 84.1 %reduce-scatter.42.cloned.1.call-done = f32[2048,256]{1,0:T(8,128)} async-done(((f32[2048,2048]{1,0:T(8,128)}), f32[2048,256]{1,0:T(8,128)}) %reduce-scatter.42.cloned.1.call-update) | async-done | bytes 2097168 | tf_op jit(solution)/shard_map/reduce_scatter | solution.py:46
  4651.3 119.4 %reduce-scatter.38.cloned.1.call-done = f32[2048,256]{1,0:T(8,128)} async-done(((f32[2048,2048]{1,0:T(8,128)}), f32[2048,256]{1,0:T(8,128)}) %reduce-scatter.38.cloned.1.call-update) | async-done | bytes 2097168 | tf_op jit(solution)/shard_map/reduce_scatter | solution.py:46
  4816.3 29.1 reduce-scatter.30.cloned.1.call-done
  (4421 shorter events, 3624.7 us)
Async XLA Ops:
  56.3 1546.8 %all-gather.29.cloned.1.call-start = ((), (), s32[]{:S(2)}) async-start(), calls=%async_computation.23 | async-start | bytes 1310720 | tf_op jit(solution)/shard_map/all_gather | solution.py:190
  56.9 1672.5 %reduce-scatter.28.cloned.1.call-start = ((), (), s32[]{:S(2)}) async-start(), calls=%async_computation.24 | async-start | bytes 18874368 | tf_op jit(solution)/shard_map/reduce_scatter | solution.py:240
  1613.3 235.7 %reduce-scatter.32.cloned.1.call-start = ((), (), s32[]{:S(2)}) async-start(), calls=%async_computation.31 | async-start | bytes 18874368 | tf_op jit(solution)/shard_map/reduce_scatter | solution.py:240
  1625.0 284.7 %all-gather.33.cloned.1.call-start = ((), (), s32[]{:S(2)}) async-start(), calls=%async_computation.26 | async-start | bytes 3604480 | tf_op jit(solution)/shard_map/all_gather | solution.py:186
  1625.7 341.0 %all-gather.31.cloned.1.call-start = ((), (), s32[]{:S(2)}) async-start(), calls=%async_computation.25 | async-start | bytes 9437184 | tf_op jit(solution)/shard_map/all_gather | solution.py:38
  1881.1 205.7 %all-gather.37.cloned.1.call-start = ((), (), s32[]{:S(2)}) async-start(), calls=%async_computation.28 | async-start | bytes 3604480 | tf_op jit(solution)/shard_map/all_gather | solution.py:191
  1881.7 262.2 %all-gather.47.cloned.1.call-start = ((), (), s32[]{:S(2)}) async-start(), calls=%async_computation.47 | async-start | bytes 9437184 | tf_op jit(solution)/shard_map/all_gather | solution.py:42
  1883.2 420.3 %reduce-scatter.36.cloned.1.call-start = ((), (), s32[]{:S(2)}) async-start(), calls=%async_computation.34 | async-start | bytes 18874368 | tf_op jit(solution)/shard_map/reduce_scatter | solution.py:46
  2187.4 176.1 %all-gather.41.cloned.1.call-start = ((), (), s32[]{:S(2)}) async-start(), calls=%async_computation.32 | async-start | bytes 9437184 | tf_op jit(solution)/shard_map/all_gather | solution.py:38
  2308.0 269.8 %reduce-scatter.40.cloned.1.call-start = ((), (), s32[]{:S(2)}) async-start(), calls=%async_computation.37 | async-start | bytes 18874368 | tf_op jit(solution)/shard_map/reduce_scatter | solution.py:46
  2461.7 190.7 %reduce-scatter.34.cloned.1.call-start = ((), (), s32[]{:S(2)}) async-start(), calls=%async_computation.33 | async-start | bytes 9437184 | tf_op jit(solution)/shard_map/reduce_scatter | solution.py:252
  2473.3 261.6 %all-gather.45.cloned.1.call-start = ((), (), s32[]{:S(2)}) async-start(), calls=%async_computation.38 | async-start | bytes 9437184 | tf_op jit(solution)/shard_map/all_gather | solution.py:42
  2658.6 1887.5 %reduce-scatter.54.cloned.1.call-start = ((), (), s32[]{:S(2)}) async-start(), calls=%async_computation.45 | async-start | bytes 3604480 | tf_op jit(solution)/shard_map/reduce_scatter | solution.py:360
  2679.2 1869.5 %reduce-scatter.52.cloned.1.call-start = ((), (), s32[]{:S(2)}) async-start(), calls=%async_computation.44 | async-start | bytes 3604480 | tf_op jit(solution)/shard_map/reduce_scatter | solution.py:357
  2700.7 1850.4 %reduce-scatter.56.cloned.1.call-start = ((), (), s32[]{:S(2)}) async-start(), calls=%async_computation.46 | async-start | bytes 3604480 | tf_op jit(solution)/shard_map/reduce_scatter | solution.py:368
  2734.8 1819.1 %reduce-scatter.64.cloned.1.call-start = ((), (), s32[]{:S(2)}) async-start(), calls=%async_computation.52 | async-start | bytes 81920
  4338.9 216.6 %reduce-scatter.62.cloned.1.call-start = ((), (), s32[]{:S(2)}) async-start(), calls=%async_computation.51 | async-start | bytes 81920
  4339.7 217.2 %reduce-scatter.60.cloned.1.call-start = ((), (), s32[]{:S(2)}) async-start(), calls=%async_computation.50 | async-start | bytes 81920
  4340.8 217.5 %reduce-scatter.58.cloned.1.call-start = ((), (), s32[]{:S(2)}) async-start(), calls=%async_computation.49 | async-start | bytes 655360
  4351.1 208.8 %reduce-scatter.50.cloned.1.call-start = ((), (), s32[]{:S(2)}) async-start(), calls=%async_computation.43 | async-start | bytes 1310720 | tf_op jit(solution)/shard_map/reduce_scatter | solution.py:365
  4372.2 189.6 %reduce-scatter.48.cloned.1.call-start = ((), (), s32[]{:S(2)}) async-start(), calls=%async_computation.42 | async-start | bytes 1310720 | tf_op jit(solution)/shard_map/reduce_scatter | solution.py:336
  4458.2 193.0 %reduce-scatter.42.cloned.1.call-start = ((), (), s32[]{:S(2)}) async-start(), calls=%async_computation.39 | async-start | bytes 18874368 | tf_op jit(solution)/shard_map/reduce_scatter | solution.py:46
  4494.6 276.1 %reduce-scatter.38.cloned.1.call-start = ((), (), s32[]{:S(2)}) async-start(), calls=%async_computation.36 | async-start | bytes 18874368 | tf_op jit(solution)/shard_map/reduce_scatter | solution.py:46
  4531.7 313.7 %reduce-scatter.30.cloned.1.call-start = ((), (), s32[]{:S(2)}) async-start(), calls=%async_computation.29 | async-start | bytes 9437184 | tf_op jit(solution)/shard_map/reduce_scatter | solution.py:252
  (220 other events, 10701.8 us)
Sparse Core Ops, SparseCore 0:
  9.6 30.6 all-gather.26
  54.5 53.2 all-gather.38
  109.4 27.9 all-gather.22
  168.5 55.4 all-gather.20
  1613.4 115.9 reduce-scatter.27
  1732.9 115.9 reduce-scatter.31
  1850.5 59.1 all-gather.32
  1912.0 54.6 all-gather.30
  1968.3 59.1 all-gather.34
  2028.9 57.8 all-gather.36
  2089.2 54.6 all-gather.46
  2187.5 115.9 reduce-scatter.35
  2307.5 55.9 all-gather.40
  2365.8 55.9 all-gather.48
  2461.8 115.9 reduce-scatter.39
  2581.1 71.2 reduce-scatter.33
  2658.1 55.9 all-gather.44
  2716.5 55.9 all-gather.42
  2774.9 56.1 reduce-scatter.53
  2833.6 56.0 reduce-scatter.51
  2892.1 56.1 reduce-scatter.55
  4536.6 114.6 reduce-scatter.41
  4654.7 115.9 reduce-scatter.37
  4774.1 71.3 reduce-scatter.29
  (10 shorter events, 231.0 us)
where the time goes:
time: 4900 us; the launch traced here: 4860 us
  other arithmetic  1630 us (33%)
  matrix products  1300 us (27%)
  waiting for transfers between devices  1170 us (24%)
  local copies, waits for them, and re-layouts  569 us (12%)
  blocking collectives  156 us (3%)
    another operation x512, other arithmetic, block_step(): lax.linalg.triangular_solve(system, right_side, left_side=True, lower=Tru...  1280 us
    reduce_scatter x4, waiting for transfers between devices, share_grad(): return lax.psum_scatter(values, 'col', scatter_dimension=1, tiled=True)  424 us
    squeeze x448, local copies, waits for them, and re-layouts, delta_blocks(): memory, outputs = lax.scan(jax.checkpoint(block_step), start, items)  326 us
    reduce_scatter x2, waiting for transfers between devices, local(): lax.psum_scatter(product(mixed_low, out_full), 'col', scatter_dimension=1...  223 us
    dot_general x16, matrix products, cross_cols(): lax.dot_general(left, right, (((1,), (1,)), ((), ())), preferred_element_...  181 us
    dot_general x256, matrix products, block_step(): key_key = jnp.einsum('bid,bjd->bij', keys, keys, precision=HIGHEST)  169 us
    all_gather x4, waiting for transfers between devices, spread_act(): return lax.all_gather(values, 'col', axis=1, tiled=True)  167 us
    dot_general x256, matrix products, block_step(): key_state = jnp.einsum('bid,bde->bie', keys, memory, precision=HIGHEST)  140 us

commit v1 on v0

v1 whole, which is shorter than its diff:
```python
from functools import partial

import jax
import jax.numpy as jnp
from jax import lax
from jax.experimental import pallas as pl
from jax.experimental.pallas import tpu as pltpu
from jax.sharding import PartitionSpec as P

SEQ = 2048
CHUNK = 128
FWD_SUB = 4
BWD_SUB = 2
TILE = 512
HALO = 8
EPSILON = 1e-06
HEAD_FLOOR = 0.002
BF = jnp.bfloat16
F32 = jnp.float32
FFN_TILE = 256
PER_MICRO = 4.0e8


def dot_nn(a, b):
    return lax.dot_general(a, b, (((1,), (0,)), ((), ())), preferred_element_type=F32)


def dot_nt(a, b):
    return lax.dot_general(a, b, (((1,), (1,)), ((), ())), preferred_element_type=F32)


def dot_tn(a, b):
    return lax.dot_general(a, b, (((0,), (0,)), ((), ())), preferred_element_type=F32)


def token_marks(labels, chunk):
    seqs, length = labels.shape
    padded_back = jnp.pad(labels, ((0, 0), (4, 0)), constant_values=-1)
    padded_fore = jnp.pad(labels, ((0, 0), (0, 4)), constant_values=-2)
    marks = [labels]
    for lag in (1, 2, 3):
        marks.append(padded_back[:, 4 - lag : 4 - lag + length] == labels)
    for lag in (1, 2, 3):
        marks.append(padded_fore[:, lag : lag + length] == labels)
    grid = labels.reshape(seqs, length // chunk, chunk)
    prior = jnp.pad(grid[:, :-1, -1], ((0, 0), (1, 0)), constant_values=-1)
    marks.append((grid == prior[:, :, None]).reshape(seqs, length))
    marks.append((grid == grid[:, :, -1:]).reshape(seqs, length))
    marks.append(
        jnp.broadcast_to((grid[:, :, -1] == prior)[:, :, None], grid.shape).reshape(seqs, length)
    )
    marks += [jnp.zeros_like(labels)] * (16 - len(marks))
    marks = [mark.astype(F32).reshape(seqs, length // chunk, 1, chunk) for mark in marks]
    return jnp.concatenate(marks, axis=2)


LABEL, BACK, FORE, CARRIED, LAST, KEEP = 0, 0, 3, 7, 8, 9


def sigmoid(x):
    return 1.0 / (1.0 + jnp.exp(-x))


def level_marks(size):
    row = lax.broadcasted_iota(jnp.int32, (size, size), 0)
    col = lax.broadcasted_iota(jnp.int32, (size, size), 1)
    return row == col, row ^ col


def unit_lower_inverses(systems):
    size = systems[0].shape[0]
    diagonal, differ = level_marks(size)
    inverses = [
        (jnp.where(diagonal, 1.0, 0.0) - jnp.where(differ == 1, system, 0.0)).astype(BF)
        for system in systems
    ]
    block = 2
    while block < size:
        level = (differ >= block) & (differ < 2 * block)
        offs = [jnp.where(level, system, 0.0).astype(BF) for system in systems]
        lefts = [dot_nn(inverse, off).astype(BF) for inverse, off in zip(inverses, offs)]
        inverses = [
            inverse - dot_nn(left, inverse).astype(BF) for inverse, left in zip(inverses, lefts)
        ]
        block *= 2
    return inverses


def conv_rows(ext, taps, marks, lane, first, chunk):
    here = ext[pl.ds(HALO + first, chunk), lane]
    shifted = [here]
    total = here * taps[0:1, lane]
    for lag in (1, 2, 3):
        moved = ext[pl.ds(HALO + first - lag, chunk), lane] * marks[:, BACK + lag : BACK + lag + 1]
        shifted.append(moved)
        total = total + moved * taps[lag : lag + 1, lane]
    return total, shifted


def chunk_marks(marks_ref, seq, part, chunk):
    by_row = marks_ref[seq, part]
    marks = jnp.transpose(by_row)
    row = lax.broadcasted_iota(jnp.int32, (chunk, chunk), 0)
    col = lax.broadcasted_iota(jnp.int32, (chunk, chunk), 1)
    same = marks[:, LABEL : LABEL + 1] == by_row[LABEL : LABEL + 1, :]
    return (
        marks,
        same & (row > col),
        same & (row >= col),
        marks[:, CARRIED : CARRIED + 1],
        marks[:, LAST : LAST + 1],
        marks[0:1, KEEP : KEEP + 1],
    )


def mix_fwd_kernel(
    heads, chunk, sub, marks_ref, taps_ref, gain_ref, pre_ref,
    ao_ref, o_ref, u_ref, w_ref, state_ref, inv_ref, ext, memory,
):
    seqs = pre_ref.shape[0]
    wide = 3 * heads * 128
    size = sub * chunk

    @pl.when(pl.program_id(0) == 0)
    def _():
        ext[:, 0:HALO, :] = jnp.zeros((seqs, HALO, wide), F32)
        memory[...] = jnp.zeros_like(memory)

    ext[:, HALO : HALO + size, :] = pre_ref[:, :, 0:wide]
    kept = {
        (seq, part): chunk_marks(marks_ref, seq, part, chunk)
        for seq in range(seqs)
        for part in range(sub)
    }
    chains = [(seq, head) for seq in range(seqs) for head in range(heads)]
    units = [(seq, head, part) for part in range(sub) for seq, head in chains]
    boths, values, betas, attns, keys_list, systems = {}, {}, {}, {}, {}, {}
    for unit in units:
        seq, head, part = unit
        marks = kept[seq, part][0]
        acts = []
        for kind in range(3):
            lane = pl.ds((kind * heads + head) * 128, 128)
            cv, _ = conv_rows(ext.at[seq], taps_ref, marks, lane, part * chunk, chunk)
            acts.append(cv * sigmoid(cv))
        q1, k1, values[unit] = acts
        qn = q1 * (lax.rsqrt(jnp.sum(q1 * q1, axis=1, keepdims=True) + EPSILON) * 128 ** (-0.5))
        kn = k1 * lax.rsqrt(jnp.sum(k1 * k1, axis=1, keepdims=True) + EPSILON)
        betas[unit] = sigmoid(
            pre_ref[seq, part * chunk : (part + 1) * chunk, wide + head : wide + head + 1]
        )
        boths[unit] = jnp.concatenate([qn.astype(BF), kn.astype(BF)], axis=0)
    for unit in units:
        _, strict, within, _, _, _ = kept[unit[0], unit[2]]
        scores = dot_nt(boths[unit], boths[unit][chunk:])
        attns[unit] = jnp.where(within, scores[:chunk], 0.0).astype(BF)
        keys = jnp.where(strict, scores[chunk:], 0.0)
        keys_list[unit] = keys.astype(BF)
        systems[unit] = keys * betas[unit]
    inverses = dict(zip(units, unit_lower_inverses([systems[unit] for unit in units])))
    for part in range(sub):
        here = [(seq, head, part) for seq, head in chains]
        states = [memory[index] for index in range(len(here))]
        lows = [state.astype(BF) for state in states]
        seens = [dot_nn(boths[unit], low) for unit, low in zip(here, lows)]
        rights = [
            values[unit] - kept[unit[0], part][3] * seen[chunk:]
            for unit, seen in zip(here, seens)
        ]
        updates = [
            dot_nn(inverses[unit], (betas[unit] * right).astype(BF))
            for unit, right in zip(here, rights)
        ]
        for index, unit in enumerate(here):
            last, keep = kept[unit[0], part][4:]
            memory[index] = keep * states[index] + dot_tn(
                boths[unit][chunk:], (last * updates[index]).astype(BF)
            )
        for index, unit in enumerate(here):
            seq, head, _ = unit
            carried = kept[seq, part][3]
            rows = slice(part * chunk, (part + 1) * chunk)
            ub = updates[index].astype(BF)
            mixed = dot_nn(jnp.concatenate([attns[unit], keys_list[unit]], axis=0), ub)
            out = carried * seens[index][:chunk] + mixed[:chunk]
            wrong = rights[index] - mixed[chunk:]
            lane = pl.ds(head * 128, 128)
            scale = lax.rsqrt(jnp.maximum(jnp.mean(out * out, axis=1, keepdims=True), HEAD_FLOOR))
            ao_ref[seq, rows, lane] = (out * scale * gain_ref[...]).astype(BF)
            o_ref[seq, rows, lane] = out
            u_ref[seq, rows, lane] = ub
            w_ref[seq, rows, lane] = wrong.astype(BF)
            inv_ref[part, index] = inverses[unit]
            state_ref[part, index] = lows[index]
    ext[:, 0:HALO, :] = ext[:, size : size + HALO, :]


def mix_bwd_kernel(
    heads, chunk, sub, marks_ref, taps_ref, gain_ref,
    o_ref, u_ref, w_ref, state_ref, inv_ref, pre_ref, halo_ref, dao_ref,
    dpre_ref, stat_ref, dconv_ref, dgain_ref, ext, dext, memory,
):
    seqs = pre_ref.shape[0]
    wide = 3 * heads * 128
    size = sub * chunk

    @pl.when(pl.program_id(0) == 0)
    def _():
        dext[:, size : size + HALO, :] = jnp.zeros((seqs, HALO, wide), F32)
        memory[...] = jnp.zeros_like(memory)
        dconv_ref[...] = jnp.zeros_like(dconv_ref)
        dgain_ref[...] = jnp.zeros_like(dgain_ref)

    ext[:, 0:HALO, :] = halo_ref[:, :, 0:wide]
    ext[:, HALO : HALO + size, :] = pre_ref[:, :, 0:wide]
    gain = gain_ref[...]

    def fold(rows):
        return jnp.sum(rows.reshape(chunk // 8, 8, 128), axis=0)

    kept = {
        (seq, part): chunk_marks(marks_ref, seq, part, chunk)
        for seq in range(seqs)
        for part in range(sub)
    }
    chains = [(seq, head) for seq in range(seqs) for head in range(heads)]
    units = [(seq, head, part) for part in reversed(range(sub)) for seq, head in chains]

    def rows_of(unit):
        return slice(unit[2] * chunk, (unit[2] + 1) * chunk)

    def lane_of(unit, kind=0):
        return pl.ds((kind * heads + unit[1]) * 128, 128)

    acts, scales, norms, betas, boths, dobs, cdos = {}, {}, {}, {}, {}, {}, {}
    for unit in units:
        seq, head, part = unit
        marks, _, _, carried, _, _ = kept[seq, part]
        for kind in range(3):
            cv, _ = conv_rows(
                ext.at[seq], taps_ref, marks, lane_of(unit, kind), part * chunk, chunk
            )
            sg = sigmoid(cv)
            acts[unit, kind] = cv * sg
            scales[unit, kind] = sg * (1.0 + cv * (1.0 - sg))
        q1, k1 = acts[unit, 0], acts[unit, 1]
        rq = lax.rsqrt(jnp.sum(q1 * q1, axis=1, keepdims=True) + EPSILON)
        rk = lax.rsqrt(jnp.sum(k1 * k1, axis=1, keepdims=True) + EPSILON)
        norms[unit] = rq, rk
        boths[unit] = jnp.concatenate(
            [(q1 * (rq * 128 ** (-0.5))).astype(BF), (k1 * rk).astype(BF)], axis=0
        )
        betas[unit] = sigmoid(pre_ref[seq, rows_of(unit), wide + head : wide + head + 1])
        out = o_ref[seq, rows_of(unit), lane_of(unit)]
        square = jnp.mean(out * out, axis=1, keepdims=True)
        scale = lax.rsqrt(jnp.maximum(square, HEAD_FLOOR))
        ro = out * scale
        dao = dao_ref[seq, rows_of(unit), lane_of(unit)]
        dgain_ref[...] += fold(dao * ro)
        eo = dao * gain
        inner = jnp.mean(eo * ro, axis=1, keepdims=True)
        inner = jnp.where(square > HEAD_FLOOR, inner, 0.0)
        do = scale * (eo - ro * inner)
        dobs[unit] = do.astype(BF)
        cdos[unit] = (carried * do).astype(BF)
    firsts, grows, crosses = {}, {}, {}
    for unit in units:
        _, _, within, _, _, _ = kept[unit[0], unit[2]]
        both = boths[unit]
        attn = jnp.where(within, dot_nt(both[:chunk], both[chunk:]), 0.0).astype(BF)
        firsts[unit] = dot_tn(attn, dobs[unit])
        grows[unit] = dot_tn(both[:chunk], cdos[unit])
    drs, seconds, dbetas = {}, {}, {}
    for part in reversed(range(sub)):
        here = [(seq, head, part) for seq, head in chains]
        olds = [memory[index] for index in range(len(here))]
        lows = [old.astype(BF) for old in olds]
        fromstate = [dot_nn(boths[unit][chunk:], low) for unit, low in zip(here, lows)]
        dus = [
            (firsts[unit] + kept[unit[0], part][4] * term).astype(BF)
            for unit, term in zip(here, fromstate)
        ]
        drhs = [dot_tn(inv_ref[part, index], du) for index, du in enumerate(dus)]
        for index, unit in enumerate(here):
            drs[unit] = betas[unit] * drhs[index]
            carried, _, keep = kept[unit[0], part][3:]
            memory[index] = (
                keep * olds[index]
                + grows[unit]
                - dot_tn(boths[unit][chunk:], (carried * drs[unit]).astype(BF))
            )
        for index, unit in enumerate(here):
            wrong = w_ref[unit[0], rows_of(unit), lane_of(unit)].astype(F32)
            dbetas[unit] = jnp.sum(drhs[index] * wrong, axis=1, keepdims=True)
            seconds[unit] = dot_nt(u_ref[unit[0], rows_of(unit), lane_of(unit)], lows[index])
    shares = {}
    for unit in units:
        seq, head, part = unit
        marks, strict, within, carried, last, _ = kept[seq, part]
        both, kb = boths[unit], boths[unit][chunk:]
        index = seq * heads + head
        stack = jnp.concatenate([dobs[unit], drs[unit].astype(BF)], axis=0)
        right = jnp.concatenate(
            [u_ref[seq, rows_of(unit), lane_of(unit)], state_ref[part, index]], axis=0
        )
        cross = dot_nt(stack, right)
        dattn = jnp.where(within, cross[:chunk, :chunk], 0.0).astype(BF)
        dkeys = jnp.where(strict, -cross[chunk:, :chunk], 0.0).astype(BF)
        dboth = jnp.concatenate([dattn, dkeys], axis=0)
        by_row = dot_nn(dboth, kb)
        dqn = carried * cross[:chunk, chunk:] + by_row[:chunk]
        dkn = (
            dot_tn(dboth, both)
            + last * seconds[unit]
            + by_row[chunk:]
            - carried * cross[chunk:, chunk:]
        )
        (rq, rk), q1, k1 = norms[unit], acts[unit, 0], acts[unit, 1]
        dq1 = 128 ** (-0.5) * rq * (
            dqn - (rq * rq) * q1 * jnp.sum(q1 * dqn, axis=1, keepdims=True)
        )
        dk1 = rk * (dkn - (rk * rk) * k1 * jnp.sum(k1 * dkn, axis=1, keepdims=True))
        for kind, dact in enumerate((dq1, dk1, drs[unit])):
            dext[seq, rows_of(unit), lane_of(unit, kind)] = dact * scales[unit, kind]
    for unit in units:
        seq, head, part = unit
        marks = kept[seq, part][0]
        share = shares.get((seq, part), 0.0)
        for kind in range(3):
            lane = lane_of(unit, kind)
            _, shifts = conv_rows(ext.at[seq], taps_ref, marks, lane, part * chunk, chunk)
            dc = dext[seq, rows_of(unit), lane]
            back = dc * taps_ref[0:1, lane]
            dconv_ref[0:8, lane] += fold(dc * shifts[0])
            for lag in (1, 2, 3):
                dconv_ref[8 * lag : 8 * lag + 8, lane] += fold(dc * shifts[lag])
                back = back + (
                    dext[seq, pl.ds(part * chunk + lag, chunk), lane]
                    * marks[:, FORE + lag : FORE + lag + 1]
                    * taps_ref[lag : lag + 1, lane]
                )
            dpre_ref[seq, rows_of(unit), lane] = back.astype(BF)
            share = share + back * shifts[0]
        shares[seq, part] = share
    column = lax.broadcasted_iota(jnp.int32, (chunk, 128), 1)
    for seq, part in kept:
        rows = slice(part * chunk, (part + 1) * chunk)
        total = jnp.zeros((chunk, 128), F32)
        for head in range(heads):
            unit = seq, head, part
            grad = dbetas[unit] * betas[unit] * (1.0 - betas[unit])
            total = jnp.where(column == head, grad, total)
        dpre_ref[seq, rows, pl.ds(wide, 128)] = total.astype(BF)
        share = shares[seq, part] + total * pre_ref[seq, rows, pl.ds(wide, 128)]
        stat_ref[seq, rows] = jnp.broadcast_to(
            jnp.sum(share, axis=1, keepdims=True), (chunk, 128)
        )
    dext[:, size : size + HALO, :] = dext[:, 0:HALO, :]


def params():
    return pltpu.CompilerParams(dimension_semantics=("arbitrary",), vmem_limit_bytes=60 * 2**20)


def fixed(array):
    zeros = (0,) * array.ndim
    return pl.BlockSpec(array.shape, lambda n: zeros, pipeline_mode=pl.Buffered(1))


def cost(micros):
    return pl.CostEstimate(flops=int(micros * PER_MICRO), bytes_accessed=0, transcendentals=0)


def shape(dims, dtype):
    return jax.ShapeDtypeStruct(dims, dtype)


def mix_forward(pre, marks, taps, gain, heads, chunk=CHUNK, sub=FWD_SUB):
    seqs, length, cols = pre.shape
    chains, parts = seqs * heads, length // chunk
    steps = parts // sub
    wide, hw = 3 * heads * 128, heads * 128

    def tok(width):
        return pl.BlockSpec((seqs, sub * chunk, width), lambda n: (0, n, 0))

    out_shape = [
        shape((seqs, length, hw), BF),
        shape((seqs, length, hw), F32),
        shape((seqs, length, hw), BF),
        shape((seqs, length, hw), BF),
        shape((parts, chains, 128, 128), BF),
        shape((parts, chains, chunk, chunk), BF),
    ]
    mixed, *saved = pl.pallas_call(
        partial(mix_fwd_kernel, heads, chunk, sub),
        grid=(steps,),
        in_specs=[
            pl.BlockSpec((seqs, sub, 16, chunk), lambda n: (0, n, 0, 0)),
            fixed(taps), fixed(gain), tok(cols),
        ],
        out_specs=[tok(hw)] * 4 + [
            pl.BlockSpec((sub, chains, 128, 128), lambda n: (n, 0, 0, 0)),
            pl.BlockSpec((sub, chains, chunk, chunk), lambda n: (n, 0, 0, 0)),
        ],
        out_shape=out_shape,
        scratch_shapes=[
            pltpu.VMEM((seqs, HALO + sub * chunk, wide), F32),
            pltpu.VMEM((chains, 128, 128), F32),
        ],
        compiler_params=params(),
        cost_estimate=cost(24),
        name="mix_forward",
    )(marks, taps, gain, pre)
    return mixed, saved


def mix_backward(pre, marks, taps, gain, saved, dao, heads, chunk=CHUNK, sub=BWD_SUB):
    seqs, length, cols = pre.shape
    chains, parts = seqs * heads, length // chunk
    steps = parts // sub
    wide, hw = 3 * heads * 128, heads * 128
    end, groups = steps - 1, sub * chunk // HALO

    def tok(width):
        return pl.BlockSpec((seqs, sub * chunk, width), lambda n: (0, end - n, 0))

    halo = pl.BlockSpec(
        (seqs, HALO, cols), lambda n: (0, jnp.maximum((end - n) * groups - 1, 0), 0)
    )
    out_shape = [
        shape((seqs, length, cols), BF), shape((seqs, length, 128), F32),
        shape((32, wide), F32), shape((8, 128), F32),
    ]
    return pl.pallas_call(
        partial(mix_bwd_kernel, heads, chunk, sub),
        grid=(steps,),
        in_specs=[
            pl.BlockSpec((seqs, sub, 16, chunk), lambda n: (0, end - n, 0, 0)),
            fixed(taps), fixed(gain),
        ] + [tok(hw)] * 3 + [
            pl.BlockSpec((sub, chains, 128, 128), lambda n: (end - n, 0, 0, 0)),
            pl.BlockSpec((sub, chains, chunk, chunk), lambda n: (end - n, 0, 0, 0)),
            tok(cols), halo, tok(hw),
        ],
        out_specs=[
            tok(cols), tok(128),
            pl.BlockSpec((32, wide), lambda n: (0, 0)),
            pl.BlockSpec((8, 128), lambda n: (0, 0)),
        ],
        out_shape=out_shape,
        scratch_shapes=[
            pltpu.VMEM((seqs, HALO + sub * chunk, wide), F32),
            pltpu.VMEM((seqs, HALO + sub * chunk, wide), F32),
            pltpu.VMEM((chains, 128, 128), F32),
        ],
        compiler_params=params(),
        cost_estimate=cost(34),
        name="mix_backward",
    )(marks, taps, gain, *saved, pre, pre, dao)


def swap(values, bit, ways):
    return lax.ppermute(values, "col", [(i, i ^ bit) for i in range(ways)])


def gather_cols(values, ways, way="direct"):
    base = [(0, 0, values)]
    if ways == 8:
        half = values.shape[-1] // 2
        along, across = swap(values, 2, ways), swap(values, 4, ways)
        base += [(2, 0, along), (4, 0, across)]
        if way == "direct":
            base.append((6, 0, swap(values, 6, ways)))
        elif way == "along":
            base.append((6, 0, swap(across, 2, ways)))
        elif way == "across":
            base.append((6, 0, swap(along, 4, ways)))
        else:
            base += [
                (6, 0, swap(across[..., :half], 2, ways)),
                (6, half, swap(along[..., half:], 4, ways)),
            ]
    else:
        bit = 2
        while bit < ways:
            base += [(far ^ bit, lane, swap(array, bit, ways)) for far, lane, array in base]
            bit *= 2
    return base


def other_core(base, ways):
    return base + [(far ^ 1, lane, swap(array, 1, ways)) for far, lane, array in base]


def after(values, *others):
    return lax.optimization_barrier((values, others))[0]


def arrays_of(pieces):
    return [array for _, _, array in pieces]


def pieces_after(pieces, *others):
    arrays = after(arrays_of(pieces), *others)
    return [(far, lane, array) for (far, lane, _), array in zip(pieces, arrays)]


def covered(results, pieces):
    results, arrays = lax.optimization_barrier((results, arrays_of(pieces)))
    return results, [(far, lane, array) for (far, lane, _), array in zip(pieces, arrays)]


def add_low(*terms):
    return sum(term.astype(F32) for term in terms).astype(BF)


def send_pairs(pieces, ways):
    return [(far, 0, swap(pieces[far | 1], 1, ways)) for far in range(0, ways, 2)]


def add_pairs(pieces, arrived):
    sums = [(far, 0, add_low(pieces[far], array)) for far, _, array in arrived if far]
    return (pieces[0], arrived[0][2]), sums


def scatter_cols(sums, ways, way="direct"):
    held = {far: array for far, _, array in sums}
    if ways == 8 and way == "direct":
        return [(far, 0, swap(held[far], far, ways)) for far in (2, 4, 6)]
    if ways == 8:
        half = held[2].shape[-1] // 2
        left = swap(held[6][..., :half], 2, ways)
        right = swap(held[6][..., half:], 4, ways)
        four = jnp.concatenate(
            [add_low(left, held[4][..., :half]), held[4][..., half:]], axis=-1
        )
        two = jnp.concatenate(
            [held[2][..., :half], add_low(right, held[2][..., half:])], axis=-1
        )
        return [(2, 0, swap(two, 2, ways)), (4, 0, swap(four, 4, ways))]
    terms = {far: (array,) for far, array in held.items()}
    terms[0] = ()
    bit = 2
    while bit < ways:
        terms = {
            far: terms[far] + (swap(add_low(*terms[far | bit]), bit, ways),)
            for far in terms
            if not far & bit
        }
        bit *= 2
    return [(0, 0, array) for array in terms[0]]


def total_of(own, arrived):
    return sum(array.astype(F32) for array in (*own, *arrays_of(arrived)))


def sum_over(values, axis, ways, bit=1, size=None):
    size = ways if size is None else size
    while bit < ways:
        values = values + lax.ppermute(values, axis, [(i, i ^ bit) for i in range(size)])
        bit *= 2
    return values


def place(spot_ref, layout, block):
    return [
        pl.multiple_of((spot_ref[0] ^ far) * block + lane, 128 if block % 128 == 0 else 1)
        for far, lane in layout
    ]


def norm_into(pieces, starts, gain_ref, act_ref):
    width = act_ref.shape[1]
    total = 0.0
    for piece in pieces:
        rows = piece[...].astype(F32)
        total = total + jnp.sum(rows * rows, axis=1, keepdims=True)
    inverse = lax.rsqrt(total / width + EPSILON)
    for start, piece in zip(starts, pieces):
        lanes = pl.ds(start, piece.shape[1])
        act_ref[:, lanes] = (piece[...].astype(F32) * inverse * gain_ref[0:1, lanes]).astype(BF)
    return inverse


def project_kernel(layout, block, spot_ref, gain_ref, weight_ref, *refs):
    count = len(layout)
    pieces, (pre_ref, act_ref, stat_ref) = refs[:count], refs[count:]
    starts = place(spot_ref, layout, block)
    inverse = norm_into(pieces, starts, gain_ref, act_ref)
    stat_ref[...] = jnp.broadcast_to(inverse, stat_ref.shape)
    pre_ref[...] = dot_nn(act_ref[...], weight_ref[...])


def spread_kernel(transposed, layout, block, spot_ref, weight_ref, rows_ref, *refs):
    outs, whole = refs[: len(layout)], refs[-1]
    parts, step = weight_ref.shape[0], whole.shape[1] // weight_ref.shape[0]
    rows = rows_ref[...]
    for part in range(parts):
        product = (dot_nt if transposed else dot_nn)(rows, weight_ref[part])
        whole[:, part * step : (part + 1) * step] = product.astype(BF)
    for start, out in zip(place(spot_ref, layout, block), outs):
        out[...] = whole[:, pl.ds(start, block)]


def collect_kernel(layout, block, spot_ref, weight_ref, *refs):
    count = len(layout)
    pieces, (whole_ref, out_ref) = refs[:count], refs[count:]
    for start, piece in zip(place(spot_ref, layout, block), pieces):
        whole_ref[:, pl.ds(start, piece.shape[1])] = piece[...]
    parts = weight_ref.shape[0]
    step = whole_ref.shape[1] // parts
    total = 0.0
    for part in range(parts):
        total = total + dot_nt(
            whole_ref[:, part * step : (part + 1) * step], weight_ref[part]
        )
    out_ref[...] = total


def ffn_kernel(layout, cot_layout, block, ways, spot_ref, gain_ref, gates_ref, ups_ref, down_ref, *refs):
    count, total = len(layout), len(layout) + len(cot_layout)
    acts, cots, refs = refs[:count], refs[count:total], refs[total:]
    act_ref, cot_ref, hid_ref, dgate_ref, dup_ref, stat_ref = refs[:6]
    grads, outs, whole = refs[6 : 6 + ways], refs[6 + ways : 6 + 2 * ways], refs[-1]
    starts = place(spot_ref, layout, block)
    inverse = norm_into(acts, starts, gain_ref, act_ref)
    for start, piece in zip(place(spot_ref, cot_layout, block), cots):
        cot_ref[:, pl.ds(start, piece.shape[1])] = piece[...]
    parts = gates_ref.shape[0]
    step = act_ref.shape[1] // parts
    gate, up, dhid = 0.0, 0.0, 0.0
    for part in range(parts):
        lanes = pl.ds(part * step, step)
        gate = gate + dot_nt(act_ref[:, lanes], gates_ref[part])
        up = up + dot_nt(act_ref[:, lanes], ups_ref[part])
        dhid = dhid + dot_nt(cot_ref[:, lanes], down_ref[part])
    sig = sigmoid(gate)
    swish = gate * sig
    hid = (swish * up).astype(BF)
    dgate = (dhid * up * sig * (1.0 + gate * (1.0 - sig))).astype(BF)
    dup = (dhid * swish).astype(BF)
    hid_ref[...] = hid
    dgate_ref[...] = dgate
    dup_ref[...] = dup
    inner = jnp.sum(dgate.astype(F32) * gate + dup.astype(F32) * up, axis=1, keepdims=True)
    lane = lax.broadcasted_iota(jnp.int32, stat_ref.shape, 1)
    stat_ref[...] = jnp.where(lane == 0, inverse, inner)
    spots = place(spot_ref, [(far, 0) for far in range(ways)], block)
    for part in range(parts):
        product = dot_nn(dgate, gates_ref[part]) + dot_nn(dup, ups_ref[part])
        whole[:, part * step : (part + 1) * step] = product.astype(BF)
    for start, out in zip(spots, grads):
        out[...] = whole[:, pl.ds(start, block)]
    for part in range(parts):
        whole[:, part * step : (part + 1) * step] = dot_nn(hid, down_ref[part]).astype(BF)
    for start, out in zip(spots, outs):
        out[...] = whole[:, pl.ds(start, block)]


SPOT = pl.BlockSpec(memory_space=pltpu.SMEM)


def rows_spec(width, tile):
    return pl.BlockSpec((tile, width), lambda n: (n, 0))


def tiled(kernel, name, fixed_args, row_args, out_shape, tile, micros, spot, scratch=()):
    rows = row_args[0].shape[0]
    return pl.pallas_call(
        kernel,
        grid=(rows // tile,),
        in_specs=[SPOT]
        + [fixed(a) for a in fixed_args]
        + [rows_spec(a.shape[1], tile) for a in row_args],
        out_specs=[rows_spec(a.shape[1], tile) for a in out_shape],
        out_shape=out_shape,
        scratch_shapes=list(scratch),
        compiler_params=params(),
        cost_estimate=cost(micros),
        name=name,
    )(spot, *fixed_args, *row_args)


def layout_of(pieces):
    return tuple((far, lane) for far, lane, _ in pieces), [array for _, _, array in pieces]


def project(pieces, gain, weight, spot, block):
    layout, arrays = layout_of(pieces)
    rows, (width, cols) = arrays[0].shape[0], weight.shape
    out = [shape((rows, cols), F32), shape((rows, width), BF), shape((rows, 128), F32)]
    return tiled(
        partial(project_kernel, layout, block), "project", [gain, weight], arrays, out,
        TILE, 19, spot,
    )


def spread(rows_in, weight, spot, block, ways, transposed):
    rows = rows_in.shape[0]
    width = block * ways
    layout = tuple((far, 0) for far in range(ways))
    return tiled(
        partial(spread_kernel, transposed, layout, block), "spread", [weight], [rows_in],
        [shape((rows, block), BF)] * ways, TILE, 14 if transposed else 7, spot,
        [pltpu.VMEM((TILE, width), BF)],
    )


def collect(pieces, weight, spot, block, ways):
    layout, arrays = layout_of(pieces)
    rows = arrays[0].shape[0]
    out = [shape((rows, block * ways), BF), shape((rows, weight.shape[1]), F32)]
    return tiled(
        partial(collect_kernel, layout, block), "collect", [weight], arrays, out,
        TILE, 9, spot,
    )


def feed_forward(acts, cots, gain, gates, ups, down, spot, block, ways):
    layout, act_arrays = layout_of(acts)
    cot_layout, cot_arrays = layout_of(cots)
    rows, width, hidden = act_arrays[0].shape[0], block * ways, down.shape[1]
    out = (
        [shape((rows, width), BF)] * 2
        + [shape((rows, hidden), BF)] * 3
        + [shape((rows, 128), F32)]
        + [shape((rows, block), BF)] * (2 * ways)
    )
    results = tiled(
        partial(ffn_kernel, layout, cot_layout, block, ways), "feed_forward", [gain, gates, ups, down],
        act_arrays + cot_arrays, out, FFN_TILE, 58, spot,
        [pltpu.VMEM((FFN_TILE, width), BF)],
    )
    return results[:6], results[6 : 6 + ways], results[6 + ways :]


def outer(lefts, rights):
    total = None
    for left, right in zip(lefts, rights):
        term = dot_tn(left, right)
        total = term if total is None else total + term
    return total


def scatter_row(values, dim):
    return lax.psum_scatter(
        values.astype(BF), "row", scatter_dimension=dim, tiled=True
    )


def local(
    ways, rows_ways, inputs, cotangent, segment, norm_gain, w_query, w_key, w_value, w_beta,
    conv_query, conv_key, conv_value, head_gain, w_out, ffn_gain, w_gate, w_up, w_down,
):
    micro, tokens, block = inputs.shape
    width = block * ways
    heads = w_beta.shape[1]
    hw = heads * 128
    per = tokens // SEQ
    here = lax.axis_index("col")
    spot = here.astype(jnp.int32)[None]

    share, taps_share = norm_gain.shape[0], conv_query.size
    packed = jnp.concatenate(
        [norm_gain, ffn_gain]
        + [taps.reshape(-1) for taps in (conv_query, conv_key, conv_value)]
        + [head_gain]
    )
    row = lax.axis_index("row")
    packed = lax.dynamic_update_slice(
        jnp.zeros((ways * rows_ways, packed.shape[0]), BF), packed[None], (here * rows_ways + row, 0)
    )
    packed = sum_over(packed, "col", ways, 2)
    first_share = after(inputs[0], packed)
    packed = sum_over(sum_over(packed, "col", 2, 1, ways), "row", rows_ways)
    gain_one = packed[:, :share].reshape(1, width).astype(F32)
    gain_two = packed[:, share : 2 * share].reshape(1, width).astype(F32)
    mine = lax.dynamic_slice_in_dim(packed, here * rows_ways, rows_ways, axis=0).astype(F32)
    taps = mine[:, 2 * share : 2 * share + 3 * taps_share]
    taps = taps.reshape(rows_ways, 3, share, 4).transpose(3, 1, 0, 2).reshape(4, 3 * hw)
    taps = jnp.pad(taps, ((0, 4), (0, 0)))
    gain_head = mine[:, 2 * share + 3 * taps_share :].reshape(1, 128)
    own_one = lax.dynamic_slice_in_dim(gain_one, here * block, block, axis=1)
    own_two = lax.dynamic_slice_in_dim(gain_two, here * block, block, axis=1)

    beta_wide = jnp.pad(w_beta, ((0, 0), (0, 128 - heads)))
    qkv_share = jnp.concatenate([w_query, w_key, w_value, beta_wide], axis=1)
    qkv = lax.all_gather(qkv_share, "row", axis=0, tiled=False)
    out_parts = lax.all_gather(w_out, "row", axis=0, tiled=False)
    gates = lax.all_gather(w_gate.T, "row", axis=0, tiled=False)
    ups = lax.all_gather(w_up.T, "row", axis=0, tiled=False)
    down = lax.all_gather(w_down, "row", axis=0, tiled=False)

    data = [token_marks(segment[m].reshape(per, SEQ), CHUNK) for m in range(micro)]
    x_base, cot_base, mine = [], [], first_share
    for m in range(micro):
        x_base.append(gather_cols(mine, ways, "split"))
        if m < micro - 1:
            mine = after(inputs[m + 1], arrays_of(x_base[m])[:3])
    for m in range(micro):
        mine = after(cotangent[m], arrays_of(x_base[m]))
        cot_base.append(gather_cols(mine, ways, "split"))
    weight = qkv.reshape(width, -1)
    pres, act_ones, inv_ones, mixed, saved = [], [], [], [], []
    resids, act_base = [], []

    def add_residual(m, own, arrived):
        resids.append(inputs[m].astype(F32) + total_of(own, arrived))
        act_base.append(gather_cols(resids[m].astype(BF), ways, "direct" if m else "split"))

    flying = None
    for m in range(micro):
        pieces = other_core(x_base[m], ways)
        if m:
            pieces = pieces_after(pieces, sums)
        pre, act, stat = project(pieces, gain_one, weight, spot, block)
        if m:
            pre, arrived = covered(pre, send_pairs(sums, ways))
            own, pairs = add_pairs(sums, arrived)
            flying = own, scatter_cols(pairs, ways)
            pre, cot_base[m] = covered(after(pre, arrays_of(pairs)), cot_base[m])
            if m == micro - 1:
                pre, gates, ups = lax.optimization_barrier((pre, gates, ups))
        elif micro > 1:
            pre, x_base[m + 1] = covered(pre, x_base[m + 1])
        pres.append(pre.reshape(per, SEQ, -1))
        act_ones.append(act)
        inv_ones.append(stat[:, 0:1])
        array, rest = mix_forward(pres[m], data[m], taps, gain_head, heads)
        if m == 0:
            array, cot_base[m] = covered(array, cot_base[m])
        mixed.append(array.reshape(tokens, hw))
        saved.append(rest)
        sums = spread(mixed[m], out_parts, spot, block, ways, False)
        if flying:
            sums, arrived = covered(sums, flying[1])
            add_residual(m - 1, flying[0], arrived)
            sums = after(sums, resids[m - 1])
        if m == micro - 1:
            sums, down = lax.optimization_barrier((sums, down))
    own, pairs = add_pairs(sums, send_pairs(sums, ways))
    flying = own, scatter_cols(pairs, ways)
    cots = [other_core(base, ways) for base in cot_base]

    ffn_saved, ffn_outs, inners, resid_grads, grad_base = [], [], [], [], []
    down_terms, gate_terms, up_terms, gain_two_grad = [], [], [], 0.0

    def finish_ffn(m, own, arrived):
        inverse = ffn_saved[m][5][:, 0:1]
        act_grad = total_of(own, arrived)
        unit = resids[m] * inverse
        resid_grads.append(
            cotangent[m].astype(F32) + inverse * (act_grad * own_two - unit * inners[m])
        )
        grad_base.append(gather_cols(resid_grads[m].astype(BF), ways))
        return jnp.sum(act_grad * unit, axis=0)

    for m in range(micro):
        pieces = other_core(act_base[m], ways)
        if m:
            pieces = pieces_after(pieces, up_terms, inners)
        else:
            pieces = pieces_after(pieces, arrays_of(pairs))
        kept, grads, outs = feed_forward(
            pieces, cots[m], gain_two, gates, ups, down, spot, block, ways
        )
        (kept, grads, outs), arrived = covered((kept, grads, outs), flying[1])
        if m < micro - 1:
            add_residual(m + 1, flying[0], arrived)
            kept, grads = after((kept, grads), resids[m + 1])
        else:
            gain_two_grad = gain_two_grad + finish_ffn(m - 1, flying[0], arrived)
            kept, grads = after((kept, grads), resid_grads[m - 1])
        ffn_saved.append(kept)
        inners.append(sum_over(kept[5][:, 1], "col", ways)[:, None] / width)
        term, arrived = covered(dot_tn(kept[2], kept[1]), send_pairs(grads, ways))
        down_terms.append(term)
        own, pairs = add_pairs(grads, arrived)
        flying = own, scatter_cols(pairs, ways)
        gate_term = dot_tn(kept[3], after(kept[0], arrays_of(pairs)))
        base = act_base[m + 1] if m < micro - 1 else grad_base[0]
        gate_term, arrived = covered(gate_term, send_pairs(outs, ways))
        gate_terms.append(gate_term)
        ffn_outs.append(add_pairs(outs, arrived))
        up_term = dot_tn(kept[4], after(kept[0], gate_term, arrays_of(ffn_outs[m][1])))
        up_term, base = covered(up_term, base)
        if m < micro - 1:
            act_base[m + 1] = base
        up_terms.append(up_term)
    pieces = other_core(base, ways)
    grad_down = scatter_row(sum(down_terms), 1)
    grad_gate = scatter_row(sum(gate_terms), 1)
    grad_up = scatter_row(sum(up_terms), 1)
    qkv_terms, out_terms, means, firsts, dconv, dgain = [], [], [], [], 0.0, 0.0
    behind, outputs = None, []
    for m in range(micro):
        whole, dao = collect(pieces, out_parts, spot, block, ways)
        own, sums = ffn_outs[m]
        out_flying = scatter_cols(pieces_after(sums, arrays_of(pieces)), ways)
        dpre, stat, dconv_part, dgain_part = mix_backward(
            pres[m], data[m], taps, gain_head, saved[m], dao.reshape(per, SEQ, hw), heads
        )
        dpre = dpre.reshape(tokens, -1)
        if m == micro - 1:
            dpre, grad_down, grad_gate = lax.optimization_barrier((dpre, grad_down, grad_gate))
        dconv, dgain = dconv + dconv_part, dgain + dgain_part
        if flying:
            dpre, arrived = covered(dpre, flying[1])
            gain_two_grad = gain_two_grad + finish_ffn(micro - 1, flying[0], arrived)
            dpre, flying = after(dpre, resid_grads[-1]), None
        dpre, arrived = covered(dpre, out_flying)
        outputs.append((resids[m] + total_of(own, arrived)).astype(BF))
        if behind:
            dpre, arrived = covered(dpre, behind[1])
            firsts.append(total_of(behind[0], arrived))
        if m < micro - 1:
            sums = spread(dpre, qkv, spot, block, ways, True)
            term, arrived = covered(
                dot_tn(act_ones[m], after(dpre, sums)), send_pairs(sums, ways)
            )
            own, pairs = add_pairs(sums, arrived)
            behind = own, scatter_cols(pairs, ways)
            out_term = dot_tn(mixed[m], after(whole, arrays_of(pairs)))
            out_term, grad_base[m + 1] = covered(out_term, grad_base[m + 1])
            pieces = pieces_after(other_core(grad_base[m + 1], ways), out_term)
        else:
            term = dot_tn(act_ones[m], dpre)
            sums = spread(after(dpre, term), qkv, spot, block, ways, True)
            out_term = dot_tn(mixed[m], after(whole, sums))
            out_term, arrived = covered(out_term, send_pairs(sums, ways))
            own, pairs = add_pairs(sums, arrived)
            firsts.append(total_of(own, scatter_cols(pairs, ways, "direct")))
        qkv_terms.append(term)
        out_terms.append(out_term)
        means.append(sum_over(stat.reshape(tokens, 128)[:, 0], "col", ways)[:, None] / width)
    grad_qkv = scatter_row(sum(qkv_terms), 0)
    grad_out = scatter_row(sum(out_terms), 1)
    input_grads, gain_one_grad = [], 0.0
    for m in range(micro):
        unit = inputs[m].astype(F32) * inv_ones[m]
        gain_one_grad = gain_one_grad + jnp.sum(firsts[m] * unit, axis=0)
        input_grads.append(
            resid_grads[m] + inv_ones[m] * (firsts[m] * own_one - unit * means[m])
        )

    grad_qkv, grad_out, grad_gate, grad_up, grad_down = (
        grad.astype(F32) for grad in (grad_qkv, grad_out, grad_gate, grad_up, grad_down)
    )
    head_sum = sum_over(jnp.sum(dgain, axis=0), "col", ways)
    conv_sum = dconv.reshape(4, 8, 3, hw).sum(axis=1).transpose(1, 2, 0)
    early = sum_over(
        jnp.concatenate([conv_sum.reshape(-1), head_sum, gain_two_grad]), "row", rows_ways
    )
    late = sum_over(gain_one_grad, "row", rows_ways)
    conv_grads = lax.dynamic_slice_in_dim(
        early[: 12 * hw].reshape(3, hw, 4), row * share, share, axis=1
    )
    grad_head = lax.dynamic_slice_in_dim(
        early[12 * hw : 12 * hw + 128], row * head_gain.shape[0], head_gain.shape[0]
    )
    grad_two = lax.dynamic_slice_in_dim(early[12 * hw + 128 :], row * share, share)
    grad_one = lax.dynamic_slice_in_dim(late, row * share, share)
    return (
        jnp.stack(outputs),
        jnp.stack(input_grads),
        grad_one,
        grad_qkv[:, :hw],
        grad_qkv[:, hw : 2 * hw],
        grad_qkv[:, 2 * hw : 3 * hw],
        grad_qkv[:, 3 * hw : 3 * hw + heads],
        conv_grads[0],
        conv_grads[1],
        conv_grads[2],
        grad_head,
        grad_out,
        grad_two,
        grad_gate.T,
        grad_up.T,
        grad_down,
    )


def solution(mesh):
    both = P(("col", "row"))
    taps = P(("col", "row"), None)
    rows_cols, cols_rows = P("row", "col"), P("col", "row")
    tokens = P(None, "row", "col")
    in_specs = (
        tokens, tokens, P(None, "row"), both, rows_cols, rows_cols, rows_cols, rows_cols,
        taps, taps, taps, P("row"), cols_rows, both, rows_cols, rows_cols, cols_rows,
    )
    out_specs = (
        tokens, tokens, both, rows_cols, rows_cols, rows_cols, rows_cols,
        taps, taps, taps, P("row"), cols_rows, both, rows_cols, rows_cols, cols_rows,
    )
    body = partial(local, mesh.shape["col"], mesh.shape["row"])
    return jax.shard_map(body, mesh=mesh, in_specs=in_specs, out_specs=out_specs, check_vma=False)
```

time: 4900 us -> 1050 us (0.21)
  other arithmetic: 1630 us -> 114 us
  matrix products: 1300 us -> 95.9 us
  waiting for transfers between devices: 1170 us -> 328 us
  local copies, waits for them, and re-layouts: 569 us -> 48.3 us
  Pallas kernels: 0 us -> 334 us
  blocking collectives: 156 us -> 0 us
  starting transfers between devices: 3.01 us -> 103 us
    another operation x580 -> x5, other arithmetic: 1290 us -> 13.7 us  [the longest x3 8.65 us: local(): jnp.stack(outputs)]
    dot_general x1456 -> x10, matrix products: 1190 us -> 95.9 us  [dot_tn(): lax.dot_general(a, b, (((0,), (0,)), ((), ())), preferred_element_type=F32)]
    reduce_scatter x15 -> x5, waiting for transfers between devices: 724 us -> 0.04 us  [scatter_row(): lax.psum_scatter(values.astype(BF), 'row', scatter_dimension=dim, tiled=T...]
    all_gather x15 -> x5, waiting for transfers between devices: 435 us -> 5.82 us  [the longest x1 5.79 us: local(): down = lax.all_gather(w_down, 'row', axis=0, tiled=False)]
    pallas_call x0 -> x14, Pallas kernels: none -> 334 us  [the longest x10 217 us: tiled(): pl.pallas_call(kernel, grid=(rows // tile,), in_specs=[SPOT] + [fixed(a)...]
    squeeze x448 -> x3, local copies, waits for them, and re-layouts: 326 us -> 4.11 us  [the longest x1 2.65 us: local(): mine = after(cotangent[m], arrays_of(x_base[m]))]
    ppermute x0 -> x146, waiting for transfers between devices: none -> 321 us  [the longest x122 282 us: swap(): return lax.ppermute(values, 'col', [(i, i ^ bit) for i in range(ways)])]
    another operation x256 -> x0, matrix products: 114 us -> none  [block_step(): lax.linalg.triangular_solve(system, right_side, left_side=True, lower=Tru...]
where the time goes in v1:
time: 1050 us; the launch traced here: 1040 us
  Pallas kernels  334 us (32%)
  waiting for transfers between devices  328 us (31%)
  other arithmetic  114 us (11%)
  starting transfers between devices  103 us (10%)
  matrix products  95.9 us (9%)
  local copies, waits for them, and re-layouts  48.3 us (5%)
  between operations  16 us (2%)
    ppermute x122, waiting for transfers between devices, swap(): return lax.ppermute(values, 'col', [(i, i ^ bit) for i in range(ways)])  282 us
    pallas_call x10, Pallas kernels, tiled(): pl.pallas_call(kernel, grid=(rows // tile,), in_specs=[SPOT] + [fixed(a)...  217 us
    dot_general x10, matrix products, dot_tn(): lax.dot_general(a, b, (((0,), (0,)), ((), ())), preferred_element_type=F32)  95.9 us
    ppermute x122, starting transfers between devices, swap(): return lax.ppermute(values, 'col', [(i, i ^ bit) for i in range(ways)])  81.1 us
    pallas_call x2, Pallas kernels, mix_backward(): pl.pallas_call(partial(mix_bwd_kernel, heads, chunk, sub), grid=(steps,),...  68.4 us
    convert_element_type x24, other arithmetic, add_low(): return sum((term.astype(F32) for term in terms)).astype(BF)  48.6 us
    pallas_call x2, Pallas kernels, mix_forward(): pl.pallas_call(partial(mix_fwd_kernel, heads, chunk, sub), grid=(steps,),...  48.4 us
    ppermute x24, waiting for transfers between devices, sum_over(): lax.ppermute(values, axis, [(i, i ^ bit) for i in range(size)])  38.7 us
  transfers between devices with their start and end apart: 156, of which 52 were waited for; matrix products, arithmetic and copies ran while one was open for 22% of the time, Pallas kernels for 32%

profile of v1, /device:TPU:0, one launch (start us, length us, event | category | flops | bytes accessed | tf_op | source)
XLA Modules:
  0.0 1039.5 jit_solution(4852650437111989631)
XLA Ops:
  26.2 19.6 %collective-permute-done.6.refs_2_ = bf16[2048,256]{1,0:T(8,128)(2,1)S(1)} collective-permute-done((bf16[2048,256]{1,0:T(8,128)(2,1)}, bf16[2048,256]{1,0:T(8,128)(2,1)S(1)}, u32[]{:S(2)}, u32[]{:S(2)}) %collective-permute-start.6) | collective-permute-done | bytes 1048608 | tf_op jit(solution)/shard_map/ppermute | solution.py:464
  68.8 11.8 %collective-permute-done.8.refs_4_ = bf16[2048,128]{1,0:T(8,128)(2,1)S(1)} collective-permute-done((bf16[2048,128]{1,0:T(8,128)(2,1)S(1)}, bf16[2048,128]{1,0:T(8,128)(2,1)S(1)}, u32[]{:S(2)}, u32[]{:S(2)}) %collective-permute-start.8) | collective-permute-done | bytes 524320 | tf_op jit(solution)/shard_map/ppermute | solution.py:464
  88.9 27.2 %collective-permute-done.16.refs_3_ = bf16[2048,128]{1,0:T(8,128)(2,1)} collective-permute-done((bf16[2048,128]{1,0:T(8,128)(2,1)}, bf16[2048,128]{1,0:T(8,128)(2,1)}, u32[]{:S(2)}, u32[]{:S(2)}) %collective-permute-start.16) | collective-permute-done | bytes 524320 | tf_op jit(solution)/shard_map/ppermute | solution.py:464
  137.5 19.8 %project.2 = (f32[2048,896]{1,0:T(8,128)}, bf16[2048,2048]{1,0:T(8,128)(2,1)}, f32[2048,128]{1,0:T(8,128)}) custom-call(s32[1]{0:T(128)} %bitcast.1.spot_ref, f32[1,2048]{1,0:T(1,128)} %reshape.399.gain_ref, bf16[2048,896]{1,0:T(8,128)(2,1)} %all-gather.13.cloned.1.call-done.weight_ref, bf16[2048,256]{1,0:T(8,128)(2,1)} %get-tuple-element.374.refs_0_, ...), custom_call_target="tpu_custom_call" | custom-call | flops 7600000000 | tf_op jit(solution)/shard_map/project/pallas_call | solution.py:671
  166.8 24.2 %mix_forward.2 = (bf16[1,2048,256]{2,1,0:T(8,128)(2,1)}, f32[1,2048,256]{2,1,0:T(8,128)}, bf16[1,2048,256]{2,1,0:T(8,128)(2,1)}, bf16[1,2048,256]{2,1,0:T(8,128)...) custom-call(f32[1,16,16,128]{3,2,1,0:T(8,128)} %concatenate.15.marks_ref, ...), custom_call_target="tpu_custom_call" | custom-call | flops 9600000000 | tf_op jit(solution)/shard_map/mix_forward/pallas_call | solution.py:395
  205.3 19.8 %project.3 = (f32[2048,896]{1,0:T(8,128)}, bf16[2048,2048]{1,0:T(8,128)(2,1)}, f32[2048,128]{1,0:T(8,128)}) custom-call(s32[1]{0:T(128)} %bitcast.1.spot_ref, f32[1,2048]{1,0:T(1,128)} %reshape.399.gain_ref, bf16[2048,896]{1,0:T(8,128)(2,1)} %all-gather.13.cloned.1.call-done.weight_ref, bf16[2048,256]{1,0:T(8,128)(2,1)} %get-tuple-element.394.refs_0_, ...), custom_call_target="tpu_custom_call" | custom-call | flops 7600000000 | tf_op jit(solution)/shard_map/project/pallas_call | solution.py:671
  240.2 24.2 %mix_forward.3 = (bf16[1,2048,256]{2,1,0:T(8,128)(2,1)}, f32[1,2048,256]{2,1,0:T(8,128)}, bf16[1,2048,256]{2,1,0:T(8,128)(2,1)}, bf16[1,2048,256]{2,1,0:T(8,128)...) custom-call(f32[1,16,16,128]{3,2,1,0:T(8,128)} %concatenate.18.marks_ref, ...), custom_call_target="tpu_custom_call" | custom-call | flops 9600000000 | tf_op jit(solution)/shard_map/mix_forward/pallas_call | solution.py:395
  271.4 12.5 %collective-permute-done.36 = bf16[2048,256]{1,0:T(8,128)(2,1)} collective-permute-done((bf16[2048,256]{1,0:T(8,128)(2,1)}, bf16[2048,256]{1,0:T(8,128)(2,1)}, u32[]{:S(2)}, u32[]{:S(2)}) %collective-permute-start.36) | collective-permute-done | bytes 1048608 | tf_op jit(solution)/shard_map/ppermute | solution.py:464
  298.8 22.1 %collective-permute-done.39.refs_2_ = bf16[2048,256]{1,0:T(8,128)(2,1)} collective-permute-done((bf16[2048,256]{1,0:T(8,128)(2,1)S(1)}, bf16[2048,256]{1,0:T(8,128)(2,1)}, u32[]{:S(2)}, u32[]{:S(2)}) %collective-permute-start.39) | collective-permute-done | bytes 1048608 | tf_op jit(solution)/shard_map/ppermute | solution.py:464
  329.0 10.7 %collective-permute-done.40.refs_3_ = bf16[2048,128]{1,0:T(8,128)(2,1)S(1)} collective-permute-done((bf16[2048,128]{1,0:T(8,128)(2,1)S(1)}, bf16[2048,128]{1,0:T(8,128)(2,1)S(1)}, u32[]{:S(2)}, u32[]{:S(2)}) %collective-permute-start.40) | collective-permute-done | bytes 524320 | tf_op jit(solution)/shard_map/ppermute | solution.py:464
  353.0 59.4 %feed_forward.2 = (bf16[2048,2048]{1,0:T(8,128)(2,1)}, bf16[2048,2048]{1,0:T(8,128)(2,1)}, bf16[2048,704]{1,0:T(8,128)(2,1)}, bf16[2048,704]{1,0:T(8,128)(2,1)},...) custom-call(s32[1]{0:T(128)} %bitcast.1.spot_ref, ...), custom_call_target="tpu_custom_call" | custom-call | flops 23200000000 | tf_op jit(solution)/shard_map/feed_forward/pallas_call | solution.py:671
  419.6 10.7 %fusion.47 = f32[704,2048]{1,0:T(8,128)} fusion(bf16[2048,704]{1,0:T(8,128)(2,1)S(1)} %copy-done.105, bf16[2048,2048]{1,0:T(8,128)(2,1)} %get-tuple-element.512), kind=kOutput, calls=%fused_computation.144 | convolution fusion | flops 5905580032 | bytes 17039360 | tf_op jit(solution)/shard_map/dot_general | solution.py:33
  458.8 10.9 %collective-permute-done.68.refs_2_ = bf16[2048,256]{1,0:T(8,128)(2,1)S(1)} collective-permute-done((bf16[2048,256]{1,0:T(8,128)(2,1)S(1)}, bf16[2048,256]{1,0:T(8,128)(2,1)S(1)}, u32[]{:S(2)}, u32[]{:S(2)}) %collective-permute-start.68) | collective-permute-done | bytes 1048608 | tf_op jit(solution)/shard_map/ppermute | solution.py:464
  495.8 58.5 %feed_forward.3 = (bf16[2048,2048]{1,0:T(8,128)(2,1)}, bf16[2048,2048]{1,0:T(8,128)(2,1)}, bf16[2048,704]{1,0:T(8,128)(2,1)}, bf16[2048,704]{1,0:T(8,128)(2,1)},...) custom-call(s32[1]{0:T(128)} %bitcast.1.spot_ref, ...), custom_call_target="tpu_custom_call" | custom-call | flops 23200000000 | tf_op jit(solution)/shard_map/feed_forward/pallas_call | solution.py:671
  652.6 34.2 %mix_backward.2 = (bf16[1,2048,896]{2,1,0:T(8,128)(2,1)}, f32[1,2048,128]{2,1,0:T(8,128)}, f32[32,768]{1,0:T(8,128)}, f32[8,128]{1,0:T(8,128)}) custom-call(f32[1,16,16,128]{3,2,1,0:T(8,128)} %concatenate.15.marks_ref, f32[8,768]{1,0:T(8,128)} %pad.37.taps_ref, f32[1,128]{1,0:T(1,128)} %reshape.350.gain_ref, f32[1,2048,256]{2,1,0:T(8,128)} %get-tuple-element.528.o_ref, ...), custom_call_target="tpu_custom_call" | custom-call | flops 13600000000 | tf_op jit(solution)/shard_map/mix_backward/pallas_call | solution.py:435
  699.5 23.0 %collective-permute-done.108 = bf16[2048,256]{1,0:T(8,128)(2,1)} collective-permute-done((bf16[2048,256]{1,0:T(8,128)(2,1)S(1)}, bf16[2048,256]{1,0:T(8,128)(2,1)}, u32[]{:S(2)}, u32[]{:S(2)}) %collective-permute-start.108) | collective-permute-done | bytes 1048608 | tf_op jit(solution)/shard_map/ppermute | solution.py:464
  722.5 14.2 %spread.6 = (bf16[2048,256]{1,0:T(8,128)(2,1)}, bf16[2048,256]{1,0:T(8,128)(2,1)}, bf16[2048,256]{1,0:T(8,128)(2,1)}, bf16[2048,256]{1,0:T(8,128)(2,1)}, bf16[20...) custom-call(s32[1]{0:T(128)} %bitcast.1.spot_ref, ...), custom_call_target="tpu_custom_call" | custom-call | flops 5600000000 | tf_op jit(solution)/shard_map/spread/pallas_call | solution.py:671
  737.7 14.7 %fusion.53 = f32[2048,896]{1,0:T(8,128)} fusion(bf16[2048,2048]{1,0:T(8,128)(2,1)} %get-tuple-element.660, bf16[2048,896]{1,0:T(8,128)(2,1)} %bitcast.203), kind=kOutput, calls=%fused_computation.150 | convolution fusion | flops 7516192768 | bytes 19398656 | tf_op jit(solution)/shard_map/dot_general | solution.py:33
  766.0 11.8 %collective-permute-done.114.refs_2_ = bf16[2048,256]{1,0:T(8,128)(2,1)S(1)} collective-permute-done((bf16[2048,256]{1,0:T(8,128)(2,1)}, bf16[2048,256]{1,0:T(8,128)(2,1)S(1)}, u32[]{:S(2)}, u32[]{:S(2)}) %collective-permute-start.114) | collective-permute-done | bytes 1048608 | tf_op jit(solution)/shard_map/ppermute | solution.py:464
  814.3 34.2 %mix_backward.3 = (bf16[1,2048,896]{2,1,0:T(8,128)(2,1)}, f32[1,2048,128]{2,1,0:T(8,128)}, f32[32,768]{1,0:T(8,128)}, f32[8,128]{1,0:T(8,128)}) custom-call(f32[1,16,16,128]{3,2,1,0:T(8,128)} %concatenate.18.marks_ref, f32[8,768]{1,0:T(8,128)} %pad.37.taps_ref, f32[1,128]{1,0:T(1,128)} %reshape.350.gain_ref, f32[1,2048,256]{2,1,0:T(8,128)} %get-tuple-element.652.o_ref, ...), custom_call_target="tpu_custom_call" | custom-call | flops 13600000000 | tf_op jit(solution)/shard_map/mix_backward/pallas_call | solution.py:435
  848.6 34.1 %collective-permute-done.121 = bf16[2048,256]{1,0:T(8,128)(2,1)} collective-permute-done((bf16[2048,256]{1,0:T(8,128)(2,1)}, bf16[2048,256]{1,0:T(8,128)(2,1)}, u32[]{:S(2)}, u32[]{:S(2)}) %collective-permute-start.121) | collective-permute-done | bytes 1048608 | tf_op jit(solution)/shard_map/ppermute | solution.py:464
  883.7 14.3 %fusion.54 = f32[2048,896]{1,0:T(8,128)} fusion(bf16[2048,2048]{1,0:T(8,128)(2,1)} %get-tuple-element.706, bf16[2048,896]{1,0:T(8,128)(2,1)} %bitcast.204), kind=kOutput, calls=%fused_computation.151 | convolution fusion | flops 7516192768 | bytes 19398656 | tf_op jit(solution)/shard_map/dot_general | solution.py:33
  898.0 14.3 %spread.7 = (bf16[2048,256]{1,0:T(8,128)(2,1)}, bf16[2048,256]{1,0:T(8,128)(2,1)}, bf16[2048,256]{1,0:T(8,128)(2,1)}, bf16[2048,256]{1,0:T(8,128)(2,1)}, bf16[20...) custom-call(s32[1]{0:T(128)} %bitcast.1.spot_ref, ...), custom_call_target="tpu_custom_call" | custom-call | flops 5600000000 | tf_op jit(solution)/shard_map/spread/pallas_call | solution.py:671
  992.9 18.9 %collective-permute-done.135 = bf16[2048,256]{1,0:T(8,128)(2,1)} collective-permute-done((bf16[2048,256]{1,0:T(8,128)(2,1)}, bf16[2048,256]{1,0:T(8,128)(2,1)}, u32[]{:S(2)}, u32[]{:S(2)}) %collective-permute-start.135) | collective-permute-done | bytes 1048608 | tf_op jit(solution)/shard_map/ppermute | solution.py:464
  (722 shorter events, 478.4 us)
Async XLA Ops:
  7.3 130.2 %all-gather.13.cloned.1.call-start = ((), (), s32[]{:S(2)}) async-start(), calls=%async_computation.11 | async-start | bytes 4587520 | tf_op jit(solution)/shard_map/all_gather | solution.py:790
  10.4 180.6 %all-gather.11.cloned.1.call-start = ((), (), s32[]{:S(2)}) async-start(), calls=%async_computation.10 | async-start | bytes 1310720 | tf_op jit(solution)/shard_map/all_gather | solution.py:791
  11.2 229.0 %all-gather.15.cloned.1.call-start = ((), (), s32[]{:S(2)}) async-start(), calls=%async_computation.12 | async-start | bytes 3604480 | tf_op jit(solution)/shard_map/all_gather | solution.py:792
  11.9 228.2 %all-gather.17.cloned.1.call-start = ((), (), s32[]{:S(2)}) async-start(), calls=%async_computation.13 | async-start | bytes 3604480 | tf_op jit(solution)/shard_map/all_gather | solution.py:793
  50.6 244.6 %all-gather.19.cloned.1.call-start = ((), (), s32[]{:S(2)}) async-start(), calls=%async_computation.14 | async-start | bytes 3604480 | tf_op jit(solution)/shard_map/all_gather | solution.py:794
  198.8 649.8 %reduce-scatter.6.cloned.1.call-start = ((), (), s32[]{:S(2)}) async-start(), calls=%async_computation.5 | async-start | bytes 3604480 | tf_op jit(solution)/shard_map/reduce_scatter | solution.py:748
  348.1 64.4 %collective-permute-start.58 = (bf16[2048,256]{1,0:T(8,128)(2,1)}, bf16[2048,256]{1,0:T(8,128)(2,1)}, u32[]{:S(2)}, u32[]{:S(2)}) collective-permute-start(bf16[2048,256]{1,0:T(8,128)(2,1)} %get-tuple-element.504), channel_id=1, source_target_pairs={{0,1},{1,0},{2,3},{3,2},{4,5},{5,4},{6,7},{7,6},{8,9},{9,8},{10,11... | collective-permute-start | bytes 3145736 | tf_op jit(solution)/shard_map/ppermute | solution.py:464
  348.4 63.9 %collective-permute-start.55 = (bf16[2048,256]{1,0:T(8,128)(2,1)}, bf16[2048,256]{1,0:T(8,128)(2,1)}, u32[]{:S(2)}, u32[]{:S(2)}) collective-permute-start(bf16[2048,256]{1,0:T(8,128)(2,1)} %add_convert_fusion.27), channel_id=1, source_target_pairs={{0,2},{1,3},{2,0},{3,1},{4,6},{5,7},{6,4},{7,5},{8,10},{9,11},{10,... | collective-permute-start | bytes 3145736 | tf_op jit(solution)/shard_map/ppermute | solution.py:464
  350.9 61.5 %collective-permute-start.56 = (bf16[2048,256]{1,0:T(8,128)(2,1)}, bf16[2048,256]{1,0:T(8,128)(2,1)}, u32[]{:S(2)}, u32[]{:S(2)}) collective-permute-start(bf16[2048,256]{1,0:T(8,128)(2,1)} %add_convert_fusion.26), channel_id=1, source_target_pairs={{0,4},{1,5},{2,6},{3,7},{4,0},{5,1},{6,2},{7,3},{8,12},{9,13},{10,... | collective-permute-start | bytes 3145736 | tf_op jit(solution)/shard_map/ppermute | solution.py:464
  492.3 62.0 %collective-permute-start.80 = (bf16[2048,256]{1,0:T(8,128)(2,1)}, bf16[2048,256]{1,0:T(8,128)(2,1)}, u32[]{:S(2)}, u32[]{:S(2)}) collective-permute-start(bf16[2048,256]{1,0:T(8,128)(2,1)} %add_convert_fusion.23), channel_id=1, source_target_pairs={{0,4},{1,5},{2,6},{3,7},{4,0},{5,1},{6,2},{7,3},{8,12},{9,13},{10,... | collective-permute-start | bytes 3145736 | tf_op jit(solution)/shard_map/ppermute | solution.py:464
  493.0 61.3 %collective-permute-start.79 = (bf16[2048,256]{1,0:T(8,128)(2,1)}, bf16[2048,256]{1,0:T(8,128)(2,1)}, u32[]{:S(2)}, u32[]{:S(2)}) collective-permute-start(bf16[2048,256]{1,0:T(8,128)(2,1)} %add_convert_fusion.24), channel_id=1, source_target_pairs={{0,2},{1,3},{2,0},{3,1},{4,6},{5,7},{6,4},{7,5},{8,10},{9,11},{10,... | collective-permute-start | bytes 3145736 | tf_op jit(solution)/shard_map/ppermute | solution.py:464
  575.7 272.9 %reduce-scatter.8.cloned.1.call-start = ((), (), s32[]{:S(2)}) async-start(), calls=%async_computation.6 | async-start | bytes 3604480 | tf_op jit(solution)/shard_map/reduce_scatter | solution.py:748
  628.0 350.4 %reduce-scatter.14.cloned.1.call-start = ((), (), s32[]{:S(2)}) async-start(), calls=%async_computation.9 | async-start | bytes 3604480 | tf_op jit(solution)/shard_map/reduce_scatter | solution.py:748
  630.7 68.8 %collective-permute-start.106 = (bf16[2048,256]{1,0:T(8,128)(2,1)}, bf16[2048,256]{1,0:T(8,128)(2,1)}, u32[]{:S(2)}, u32[]{:S(2)}) collective-permute-start(bf16[2048,256]{1,0:T(8,128)(2,1)} %add_convert_fusion.21), channel_id=1, source_target_pairs={{0,2},{1,3},{2,0},{3,1},{4,6},{5,7},{6,4},{7,5},{8,10},{9,11},{10,... | collective-permute-start | bytes 3145736 | tf_op jit(solution)/shard_map/ppermute | solution.py:464
  632.3 67.2 %collective-permute-start.107 = (bf16[2048,256]{1,0:T(8,128)(2,1)}, bf16[2048,256]{1,0:T(8,128)(2,1)}, u32[]{:S(2)}, u32[]{:S(2)}) collective-permute-start(bf16[2048,256]{1,0:T(8,128)(2,1)} %add_convert_fusion.20), channel_id=1, source_target_pairs={{0,4},{1,5},{2,6},{3,7},{4,0},{5,1},{6,2},{7,3},{8,12},{9,13},{10,... | collective-permute-start | bytes 3145736 | tf_op jit(solution)/shard_map/ppermute | solution.py:464
  650.9 71.6 %collective-permute-start.108 = (bf16[2048,256]{1,0:T(8,128)(2,1)S(1)}, bf16[2048,256]{1,0:T(8,128)(2,1)}, u32[]{:S(2)}, u32[]{:S(2)}) collective-permute-start(bf16[2048,256]{1,0:T(8,128)(2,1)S(1)} %add_convert_fusion.19), channel_id=1, source_target_pairs={{0,6},{1,7},{2,4},{3,5},{4,2},{5,3},{6,0},{7,1},{8,14},{9,15},{10,... | collective-permute-start | bytes 3145736 | tf_op jit(solution)/shard_map/ppermute | solution.py:464
  692.1 73.9 %collective-permute-start.115 = (bf16[2048,256]{1,0:T(8,128)(2,1)}, bf16[2048,256]{1,0:T(8,128)(2,1)}, u32[]{:S(2)}, u32[]{:S(2)}) collective-permute-start(bf16[2048,256]{1,0:T(8,128)(2,1)} %get-tuple-element.678.refs_0_), channel_id=1, source_target_pairs={{0,6},{1,7},{2,4},{3,5},{4,2},{5,3},{6,0},{7,1},{8,14},{9,15},{10,... | collective-permute-start | bytes 3145736 | tf_op jit(solution)/shard_map/ppermute | solution.py:464
  789.9 236.9 %reduce-scatter.12.cloned.1.call-start = ((), (), s32[]{:S(2)}) async-start(), calls=%async_computation.8 | async-start | bytes 1310720 | tf_op jit(solution)/shard_map/reduce_scatter | solution.py:748
  789.9 92.8 %collective-permute-start.124 = (bf16[2048,256]{1,0:T(8,128)(2,1)}, bf16[2048,256]{1,0:T(8,128)(2,1)S(1)}, u32[]{:S(2)}, u32[]{:S(2)}) collective-permute-start(bf16[2048,256]{1,0:T(8,128)(2,1)} %add_convert_fusion.10), channel_id=1, source_target_pairs={{0,4},{1,5},{2,6},{3,7},{4,0},{5,1},{6,2},{7,3},{8,12},{9,13},{10,... | collective-permute-start | bytes 3145736 | tf_op jit(solution)/shard_map/ppermute | solution.py:464
  791.3 91.3 %collective-permute-start.123 = (bf16[2048,256]{1,0:T(8,128)(2,1)}, bf16[2048,256]{1,0:T(8,128)(2,1)}, u32[]{:S(2)}, u32[]{:S(2)}) collective-permute-start(bf16[2048,256]{1,0:T(8,128)(2,1)} %add_convert_fusion.11), channel_id=1, source_target_pairs={{0,2},{1,3},{2,0},{3,1},{4,6},{5,7},{6,4},{7,5},{8,10},{9,11},{10,... | collective-permute-start | bytes 3145736 | tf_op jit(solution)/shard_map/ppermute | solution.py:464
  792.5 90.2 %collective-permute-start.125 = (bf16[2048,256]{1,0:T(8,128)(2,1)}, bf16[2048,256]{1,0:T(8,128)(2,1)}, u32[]{:S(2)}, u32[]{:S(2)}) collective-permute-start(bf16[2048,256]{1,0:T(8,128)(2,1)} %add_convert_fusion.9), channel_id=1, source_target_pairs={{0,6},{1,7},{2,4},{3,5},{4,2},{5,3},{6,0},{7,1},{8,14},{9,15},{10,... | collective-permute-start | bytes 3145736 | tf_op jit(solution)/shard_map/ppermute | solution.py:464
  793.5 89.2 %collective-permute-start.121 = (bf16[2048,256]{1,0:T(8,128)(2,1)}, bf16[2048,256]{1,0:T(8,128)(2,1)}, u32[]{:S(2)}, u32[]{:S(2)}) collective-permute-start(bf16[2048,256]{1,0:T(8,128)(2,1)} %add_convert_fusion.14), channel_id=1, source_target_pairs={{0,4},{1,5},{2,6},{3,7},{4,0},{5,1},{6,2},{7,3},{8,12},{9,13},{10,... | collective-permute-start | bytes 3145736 | tf_op jit(solution)/shard_map/ppermute | solution.py:464
  812.2 70.5 %collective-permute-start.122 = (bf16[2048,256]{1,0:T(8,128)(2,1)}, bf16[2048,256]{1,0:T(8,128)(2,1)}, u32[]{:S(2)}, u32[]{:S(2)}) collective-permute-start(bf16[2048,256]{1,0:T(8,128)(2,1)} %add_convert_fusion.13), channel_id=1, source_target_pairs={{0,6},{1,7},{2,4},{3,5},{4,2},{5,3},{6,0},{7,1},{8,14},{9,15},{10,... | collective-permute-start | bytes 3145736 | tf_op jit(solution)/shard_map/ppermute | solution.py:464
  921.2 107.4 %reduce-scatter.10.cloned.1.call-start = ((), (), s32[]{:S(2)}) async-start(), calls=%async_computation.7 | async-start | bytes 4587520 | tf_op jit(solution)/shard_map/reduce_scatter | solution.py:748
  (250 other events, 3922.4 us)
Sparse Core Ops, SparseCore 0:
  10.6 77.5 all-gather.12
  89.7 26.5 all-gather.10
  117.8 58.6 all-gather.14
  178.0 57.8 all-gather.16
  237.3 57.8 all-gather.18
  575.8 54.6 reduce-scatter.5
  632.8 56.0 reduce-scatter.7
  790.0 54.6 reduce-scatter.13
  921.3 25.8 reduce-scatter.11
  949.5 67.1 reduce-scatter.9

commit v2 on v1

--- a/solution.py
+++ b/solution.py
@@ -464,29 +464,33 @@
     return lax.ppermute(values, "col", [(i, i ^ bit) for i in range(ways)])
 
 
-def gather_cols(values, ways, way="direct"):
+def gather_near(values, ways):
     base = [(0, 0, values)]
     if ways == 8:
-        half = values.shape[-1] // 2
-        along, across = swap(values, 2, ways), swap(values, 4, ways)
-        base += [(2, 0, along), (4, 0, across)]
-        if way == "direct":
-            base.append((6, 0, swap(values, 6, ways)))
-        elif way == "along":
-            base.append((6, 0, swap(across, 2, ways)))
-        elif way == "across":
-            base.append((6, 0, swap(along, 4, ways)))
-        else:
-            base += [
-                (6, 0, swap(across[..., :half], 2, ways)),
-                (6, half, swap(along[..., half:], 4, ways)),
-            ]
-    else:
-        bit = 2
-        while bit < ways:
-            base += [(far ^ bit, lane, swap(array, bit, ways)) for far, lane, array in base]
-            bit *= 2
+        return base + [(far, 0, swap(values, far, ways)) for far in (2, 4)]
+    bit = 2
+    while bit < ways:
+        base += [(far ^ bit, lane, swap(array, bit, ways)) for far, lane, array in base]
+        bit *= 2
     return base
+
+
+def gather_far(base, ways, *others):
+    if ways != 8:
+        return base
+    along, across = base[1][2], base[2][2]
+    half = along.shape[-1] // 2
+    first, second = across[..., :half], along[..., half:]
+    if others:
+        first, second = after((first, second), others)
+    return base + [(6, 0, swap(first, 2, ways)), (6, half, swap(second, 4, ways))]
+
+
+def gather_cols(values, ways, way="direct"):
+    base = gather_near(values, ways)
+    if ways != 8 or way == "split":
+        return gather_far(base, ways)
+    return base + [(6, 0, swap(values, 6, ways))]
 
 
 def other_core(base, ways):
@@ -564,55 +568,74 @@
     return values
 
 
-def place(spot_ref, layout, block):
-    return [
-        pl.multiple_of((spot_ref[0] ^ far) * block + lane, 128 if block % 128 == 0 else 1)
-        for far, lane in layout
-    ]
-
-
-def norm_into(pieces, starts, gain_ref, act_ref):
+def sum_cols(values, ways):
+    values = values + swap(values, 1, ways)
+    return values + sum(swap(values, far, ways) for far in range(2, ways, 2))
+
+
+def whole_blocks(layout, pieces):
+    blocks = {}
+    for (far, _), piece in zip(layout, pieces):
+        blocks.setdefault(far, []).append(piece[...])
+    return {
+        far: parts[0] if len(parts) == 1 else jnp.concatenate(parts, axis=1)
+        for far, parts in blocks.items()
+    }
+
+
+def lanes_of(spot_ref, far, block):
+    return pl.ds(pl.multiple_of((spot_ref[0] ^ far) * block, block), block)
+
+
+def part_of(spot_ref, far, block, step):
+    index, each = spot_ref[0] ^ far, step // block
+    return index // each, pl.ds(pl.multiple_of((index % each) * block, block), block)
+
+
+def normed(blocks, spot_ref, gain_ref, act_ref, block):
     width = act_ref.shape[1]
     total = 0.0
-    for piece in pieces:
-        rows = piece[...].astype(F32)
+    for rows in blocks.values():
+        rows = rows.astype(F32)
         total = total + jnp.sum(rows * rows, axis=1, keepdims=True)
     inverse = lax.rsqrt(total / width + EPSILON)
-    for start, piece in zip(starts, pieces):
-        lanes = pl.ds(start, piece.shape[1])
-        act_ref[:, lanes] = (piece[...].astype(F32) * inverse * gain_ref[0:1, lanes]).astype(BF)
-    return inverse
+    acts = {}
+    for far, rows in blocks.items():
+        lanes = lanes_of(spot_ref, far, block)
+        acts[far] = (rows.astype(F32) * inverse * gain_ref[0:1, lanes]).astype(BF)
+        act_ref[:, lanes] = acts[far]
+    return acts, inverse
 
 
 def project_kernel(layout, block, spot_ref, gain_ref, weight_ref, *refs):
-    count = len(layout)
-    pieces, (pre_ref, act_ref, stat_ref) = refs[:count], refs[count:]
-    starts = place(spot_ref, layout, block)
-    inverse = norm_into(pieces, starts, gain_ref, act_ref)
+    pieces, (pre_ref, act_ref, stat_ref) = refs[: len(layout)], refs[len(layout) :]
+    blocks = whole_blocks(layout, pieces)
+    acts, inverse = normed(blocks, spot_ref, gain_ref, act_ref, block)
     stat_ref[...] = jnp.broadcast_to(inverse, stat_ref.shape)
-    pre_ref[...] = dot_nn(act_ref[...], weight_ref[...])
-
-
-def spread_kernel(transposed, layout, block, spot_ref, weight_ref, rows_ref, *refs):
-    outs, whole = refs[: len(layout)], refs[-1]
-    parts, step = weight_ref.shape[0], whole.shape[1] // weight_ref.shape[0]
+    total = 0.0
+    for far, act in acts.items():
+        total = total + dot_nn(act, weight_ref[lanes_of(spot_ref, far, block), :])
+    pre_ref[...] = total
+
+
+def spread_kernel(transposed, block, spot_ref, weight_ref, rows_ref, *outs):
     rows = rows_ref[...]
-    for part in range(parts):
-        product = (dot_nt if transposed else dot_nn)(rows, weight_ref[part])
-        whole[:, part * step : (part + 1) * step] = product.astype(BF)
-    for start, out in zip(place(spot_ref, layout, block), outs):
-        out[...] = whole[:, pl.ds(start, block)]
+    step = weight_ref.shape[1 if transposed else 2]
+    for far, out in enumerate(outs):
+        part, lanes = part_of(spot_ref, far, block, step)
+        if transposed:
+            out[...] = dot_nt(rows, weight_ref[part, lanes, :]).astype(BF)
+        else:
+            out[...] = dot_nn(rows, weight_ref[part, :, lanes]).astype(BF)
 
 
 def collect_kernel(layout, block, spot_ref, weight_ref, *refs):
-    count = len(layout)
-    pieces, (whole_ref, out_ref) = refs[:count], refs[count:]
-    for start, piece in zip(place(spot_ref, layout, block), pieces):
-        whole_ref[:, pl.ds(start, piece.shape[1])] = piece[...]
-    parts = weight_ref.shape[0]
-    step = whole_ref.shape[1] // parts
+    pieces, (whole_ref, out_ref) = refs[: len(layout)], refs[len(layout) :]
+    for far, rows in whole_blocks(layout, pieces).items():
+        whole_ref[:, lanes_of(spot_ref, far, block)] = rows
+    step = weight_ref.shape[2]
     total = 0.0
-    for part in range(parts):
+    for part in range(weight_ref.shape[0]):
         total = total + dot_nt(
             whole_ref[:, part * step : (part + 1) * step], weight_ref[part]
         )
@@ -623,19 +646,24 @@
     count, total = len(layout), len(layout) + len(cot_layout)
     acts, cots, refs = refs[:count], refs[count:total], refs[total:]
     act_ref, cot_ref, hid_ref, dgate_ref, dup_ref, stat_ref = refs[:6]
-    grads, outs, whole = refs[6 : 6 + ways], refs[6 + ways : 6 + 2 * ways], refs[-1]
-    starts = place(spot_ref, layout, block)
-    inverse = norm_into(acts, starts, gain_ref, act_ref)
-    for start, piece in zip(place(spot_ref, cot_layout, block), cots):
-        cot_ref[:, pl.ds(start, piece.shape[1])] = piece[...]
-    parts = gates_ref.shape[0]
-    step = act_ref.shape[1] // parts
-    gate, up, dhid = 0.0, 0.0, 0.0
-    for part in range(parts):
-        lanes = pl.ds(part * step, step)
-        gate = gate + dot_nt(act_ref[:, lanes], gates_ref[part])
-        up = up + dot_nt(act_ref[:, lanes], ups_ref[part])
-        dhid = dhid + dot_nt(cot_ref[:, lanes], down_ref[part])
+    grads, outs = refs[6 : 6 + ways], refs[6 + ways : -4]
+    whole, gates, ups, downs = refs[-4:]
+
+    @pl.when(pl.program_id(0) == 0)
+    def _():
+        step = down_ref.shape[2]
+        for part in range(down_ref.shape[0]):
+            lanes = slice(part * step, (part + 1) * step)
+            gates[:, lanes] = gates_ref[part]
+            ups[:, lanes] = ups_ref[part]
+            downs[:, lanes] = down_ref[part]
+
+    for far, rows in whole_blocks(cot_layout, cots).items():
+        cot_ref[:, lanes_of(spot_ref, far, block)] = rows
+    _, inverse = normed(whole_blocks(layout, acts), spot_ref, gain_ref, act_ref, block)
+    dhid = dot_nt(cot_ref[...], downs[...])
+    gate = dot_nt(act_ref[...], gates[...])
+    up = dot_nt(act_ref[...], ups[...])
     sig = sigmoid(gate)
     swish = gate * sig
     hid = (swish * up).astype(BF)
@@ -647,16 +675,15 @@
     inner = jnp.sum(dgate.astype(F32) * gate + dup.astype(F32) * up, axis=1, keepdims=True)
     lane = lax.broadcasted_iota(jnp.int32, stat_ref.shape, 1)
     stat_ref[...] = jnp.where(lane == 0, inverse, inner)
-    spots = place(spot_ref, [(far, 0) for far in range(ways)], block)
-    for part in range(parts):
-        product = dot_nn(dgate, gates_ref[part]) + dot_nn(dup, ups_ref[part])
-        whole[:, part * step : (part + 1) * step] = product.astype(BF)
-    for start, out in zip(spots, grads):
-        out[...] = whole[:, pl.ds(start, block)]
-    for part in range(parts):
-        whole[:, part * step : (part + 1) * step] = dot_nn(hid, down_ref[part]).astype(BF)
-    for start, out in zip(spots, outs):
-        out[...] = whole[:, pl.ds(start, block)]
+    whole[...] = (dot_nn(dgate, gates[...]) + dot_nn(dup, ups[...])).astype(BF)
+    for far, grad in enumerate(grads):
+        grad[...] = whole[:, lanes_of(spot_ref, far, block)]
+    if len(outs) == 1:
+        outs[0][...] = dot_nn(hid, downs[...]).astype(BF)
+    else:
+        whole[...] = dot_nn(hid, downs[...]).astype(BF)
+        for far, out in enumerate(outs):
+            out[...] = whole[:, lanes_of(spot_ref, far, block)]
 
 
 SPOT = pl.BlockSpec(memory_space=pltpu.SMEM)
@@ -699,12 +726,9 @@
 
 def spread(rows_in, weight, spot, block, ways, transposed):
     rows = rows_in.shape[0]
-    width = block * ways
-    layout = tuple((far, 0) for far in range(ways))
     return tiled(
-        partial(spread_kernel, transposed, layout, block), "spread", [weight], [rows_in],
+        partial(spread_kernel, transposed, block), "spread", [weight], [rows_in],
         [shape((rows, block), BF)] * ways, TILE, 14 if transposed else 7, spot,
-        [pltpu.VMEM((TILE, width), BF)],
     )
 
 
@@ -718,7 +742,7 @@
     )
 
 
-def feed_forward(acts, cots, gain, gates, ups, down, spot, block, ways):
+def feed_forward(acts, cots, gain, gates, ups, down, spot, block, ways, split):
     layout, act_arrays = layout_of(acts)
     cot_layout, cot_arrays = layout_of(cots)
     rows, width, hidden = act_arrays[0].shape[0], block * ways, down.shape[1]
@@ -726,12 +750,13 @@
         [shape((rows, width), BF)] * 2
         + [shape((rows, hidden), BF)] * 3
         + [shape((rows, 128), F32)]
-        + [shape((rows, block), BF)] * (2 * ways)
+        + [shape((rows, block), BF)] * ways
+        + ([shape((rows, block), BF)] * ways if split else [shape((rows, width), BF)])
     )
     results = tiled(
         partial(ffn_kernel, layout, cot_layout, block, ways), "feed_forward", [gain, gates, ups, down],
-        act_arrays + cot_arrays, out, FFN_TILE, 58, spot,
-        [pltpu.VMEM((FFN_TILE, width), BF)],
+        act_arrays + cot_arrays, out, FFN_TILE, 54, spot,
+        [pltpu.VMEM((FFN_TILE, width), BF)] + [pltpu.VMEM((hidden, width), BF)] * 3,
     )
     return results[:6], results[6 : 6 + ways], results[6 + ways :]
 
@@ -742,6 +767,12 @@
         term = dot_tn(left, right)
         total = term if total is None else total + term
     return total
+
+
+def grow(total, left, right, last):
+    term = dot_tn(left, right)
+    term = term if total is None else total + term
+    return term.astype(BF) if last else term
 
 
 def scatter_row(values, dim):
@@ -794,58 +825,63 @@
     down = lax.all_gather(w_down, "row", axis=0, tiled=False)
 
     data = [token_marks(segment[m].reshape(per, SEQ), CHUNK) for m in range(micro)]
-    x_base, cot_base, mine = [], [], first_share
+    x_base, cot_near, mine = [], [], first_share
     for m in range(micro):
-        x_base.append(gather_cols(mine, ways, "split"))
+        near = gather_near(mine, ways)
+        x_base.append(gather_far(near, ways))
         if m < micro - 1:
-            mine = after(inputs[m + 1], arrays_of(x_base[m])[:3])
+            mine = after(inputs[m + 1], arrays_of(near))
     for m in range(micro):
-        mine = after(cotangent[m], arrays_of(x_base[m]))
-        cot_base.append(gather_cols(mine, ways, "split"))
+        mine = after(cotangent[m], arrays_of(x_base[-1]))
+        cot_near.append(gather_near(mine, ways))
+    cot_base = []
     weight = qkv.reshape(width, -1)
     pres, act_ones, inv_ones, mixed, saved = [], [], [], [], []
     resids, act_base = [], []
 
     def add_residual(m, own, arrived):
         resids.append(inputs[m].astype(F32) + total_of(own, arrived))
-        act_base.append(gather_cols(resids[m].astype(BF), ways, "direct" if m else "split"))
+        near = gather_near(resids[m].astype(BF), ways)
+        act_base.append(near if m else gather_far(near, ways, down))
 
     flying = None
     for m in range(micro):
         pieces = other_core(x_base[m], ways)
         if m:
-            pieces = pieces_after(pieces, sums)
+            own, pairs = add_pairs(sums, send_pairs(sums, ways))
+            flying = own, scatter_cols(pairs, ways)
+            pieces = pieces_after(pieces, arrays_of(pairs))
         pre, act, stat = project(pieces, gain_one, weight, spot, block)
         if m:
-            pre, arrived = covered(pre, send_pairs(sums, ways))
-            own, pairs = add_pairs(sums, arrived)
-            flying = own, scatter_cols(pairs, ways)
-            pre, cot_base[m] = covered(after(pre, arrays_of(pairs)), cot_base[m])
+            pre, cot_base[m - 1] = covered(pre, cot_base[m - 1])
             if m == micro - 1:
-                pre, gates, ups = lax.optimization_barrier((pre, gates, ups))
-        elif micro > 1:
-            pre, x_base[m + 1] = covered(pre, x_base[m + 1])
+                pre, gates = lax.optimization_barrier((pre, gates))
         pres.append(pre.reshape(per, SEQ, -1))
         act_ones.append(act)
         inv_ones.append(stat[:, 0:1])
         array, rest = mix_forward(pres[m], data[m], taps, gain_head, heads)
-        if m == 0:
+        if m < micro - 1:
+            cot_base.append(gather_far(cot_near[m], ways, array))
+            array, x_base[m + 1] = covered(array, x_base[m + 1])
+        else:
             array, cot_base[m] = covered(array, cot_base[m])
         mixed.append(array.reshape(tokens, hw))
         saved.append(rest)
         sums = spread(mixed[m], out_parts, spot, block, ways, False)
+        if m == micro - 2:
+            cot_base.append(gather_far(cot_near[m + 1], ways, sums))
         if flying:
             sums, arrived = covered(sums, flying[1])
             add_residual(m - 1, flying[0], arrived)
             sums = after(sums, resids[m - 1])
         if m == micro - 1:
-            sums, down = lax.optimization_barrier((sums, down))
+            sums, ups = lax.optimization_barrier((sums, ups))
     own, pairs = add_pairs(sums, send_pairs(sums, ways))
     flying = own, scatter_cols(pairs, ways)
     cots = [other_core(base, ways) for base in cot_base]
 
     ffn_saved, ffn_outs, inners, resid_grads, grad_base = [], [], [], [], []
-    down_terms, gate_terms, up_terms, gain_two_grad = [], [], [], 0.0
+    down_grad, gate_grad, up_grad, gain_two_grad = None, None, None, 0.0
 
     def finish_ffn(m, own, arrived):
         inverse = ffn_saved[m][5][:, 0:1]
@@ -854,17 +890,17 @@
         resid_grads.append(
             cotangent[m].astype(F32) + inverse * (act_grad * own_two - unit * inners[m])
         )
-        grad_base.append(gather_cols(resid_grads[m].astype(BF), ways))
+        grad_base.append(gather_near(resid_grads[m].astype(BF), ways))
         return jnp.sum(act_grad * unit, axis=0)
 
     for m in range(micro):
         pieces = other_core(act_base[m], ways)
         if m:
-            pieces = pieces_after(pieces, up_terms, inners)
+            pieces = pieces_after(pieces, up_grad, inners)
         else:
             pieces = pieces_after(pieces, arrays_of(pairs))
         kept, grads, outs = feed_forward(
-            pieces, cots[m], gain_two, gates, ups, down, spot, block, ways
+            pieces, cots[m], gain_two, gates, ups, down, spot, block, ways, m == micro - 1
         )
         (kept, grads, outs), arrived = covered((kept, grads, outs), flying[1])
         if m < micro - 1:
@@ -873,82 +909,111 @@
         else:
             gain_two_grad = gain_two_grad + finish_ffn(m - 1, flying[0], arrived)
             kept, grads = after((kept, grads), resid_grads[m - 1])
+        if m:
+            kept, ffn_outs[m - 1] = lax.optimization_barrier((kept, ffn_outs[m - 1]))
         ffn_saved.append(kept)
-        inners.append(sum_over(kept[5][:, 1], "col", ways)[:, None] / width)
-        term, arrived = covered(dot_tn(kept[2], kept[1]), send_pairs(grads, ways))
-        down_terms.append(term)
+        inners.append(sum_cols(kept[5][:, 1], ways)[:, None] / width)
+        last = m == micro - 1
+        down_grad, arrived = covered(
+            grow(down_grad, kept[2], kept[1], last), send_pairs(grads, ways)
+        )
         own, pairs = add_pairs(grads, arrived)
-        flying = own, scatter_cols(pairs, ways)
-        gate_term = dot_tn(kept[3], after(kept[0], arrays_of(pairs)))
-        base = act_base[m + 1] if m < micro - 1 else grad_base[0]
-        gate_term, arrived = covered(gate_term, send_pairs(outs, ways))
-        gate_terms.append(gate_term)
-        ffn_outs.append(add_pairs(outs, arrived))
-        up_term = dot_tn(kept[4], after(kept[0], gate_term, arrays_of(ffn_outs[m][1])))
-        up_term, base = covered(up_term, base)
-        if m < micro - 1:
+        gate_grad = grow(gate_grad, kept[3], after(kept[0], arrays_of(pairs)), last)
+        base = grad_base[0] if last else act_base[m + 1]
+        gate_grad, base = covered(gate_grad, base)
+        base = gather_far(base, ways)
+        right = after(kept[0], gate_grad, inners[m])
+        if last:
+            gate_grad, arrived = covered(gate_grad, send_pairs(outs, ways))
+            out_own, out_sums = add_pairs(outs, arrived)
+            right = after(right, arrays_of(out_sums))
+        else:
+            ffn_outs.append(
+                lax.psum_scatter(outs[0], "col", scatter_dimension=1, tiled=True)
+            )
+        up_grad, base = covered(grow(up_grad, kept[4], right, last), base)
+        if not last:
             act_base[m + 1] = base
-        up_terms.append(up_term)
+        flying = own, scatter_cols(pieces_after(pairs, arrays_of(base)), ways)
     pieces = other_core(base, ways)
-    grad_down = scatter_row(sum(down_terms), 1)
-    grad_gate = scatter_row(sum(gate_terms), 1)
-    grad_up = scatter_row(sum(up_terms), 1)
-    qkv_terms, out_terms, means, firsts, dconv, dgain = [], [], [], [], 0.0, 0.0
-    behind, outputs = None, []
+    grad_down = scatter_row(down_grad, 1)
+    grad_gate = scatter_row(gate_grad, 1)
+    grad_up = scatter_row(up_grad, 1)
+
+    qkv_terms, out_terms, firsts, dconv, dgain = [], [], [], 0.0, 0.0
+    behind, stats = None, []
     for m in range(micro):
         whole, dao = collect(pieces, out_parts, spot, block, ways)
-        own, sums = ffn_outs[m]
-        out_flying = scatter_cols(pieces_after(sums, arrays_of(pieces)), ways)
+        if m == micro - 1:
+            out_terms.append(dot_tn(mixed[m], whole))
+            out_flying = scatter_cols(pieces_after(out_sums, arrays_of(pieces)), ways)
+            grad_out = scatter_row(sum(out_terms), 1)
+            dao = after(dao, out_terms)
         dpre, stat, dconv_part, dgain_part = mix_backward(
             pres[m], data[m], taps, gain_head, saved[m], dao.reshape(per, SEQ, hw), heads
         )
         dpre = dpre.reshape(tokens, -1)
-        if m == micro - 1:
-            dpre, grad_down, grad_gate = lax.optimization_barrier((dpre, grad_down, grad_gate))
         dconv, dgain = dconv + dconv_part, dgain + dgain_part
+        if m == 0:
+            dpre, grad_down = lax.optimization_barrier((dpre, grad_down))
         if flying:
             dpre, arrived = covered(dpre, flying[1])
             gain_two_grad = gain_two_grad + finish_ffn(micro - 1, flying[0], arrived)
             dpre, flying = after(dpre, resid_grads[-1]), None
-        dpre, arrived = covered(dpre, out_flying)
-        outputs.append((resids[m] + total_of(own, arrived)).astype(BF))
         if behind:
             dpre, arrived = covered(dpre, behind[1])
-            firsts.append(total_of(behind[0], arrived))
+            firsts.append((behind[0], arrived))
         if m < micro - 1:
             sums = spread(dpre, qkv, spot, block, ways, True)
             term, arrived = covered(
                 dot_tn(act_ones[m], after(dpre, sums)), send_pairs(sums, ways)
             )
+            stats.append(after(stat, sums))
             own, pairs = add_pairs(sums, arrived)
-            behind = own, scatter_cols(pairs, ways)
-            out_term = dot_tn(mixed[m], after(whole, arrays_of(pairs)))
-            out_term, grad_base[m + 1] = covered(out_term, grad_base[m + 1])
-            pieces = pieces_after(other_core(grad_base[m + 1], ways), out_term)
+            term, base = covered(term, grad_base[m + 1])
+            base = gather_far(base, ways)
+            qkv_terms.append(term)
+            out_term = dot_tn(mixed[m], after(whole, term, arrays_of(pairs)))
+            out_term, base = covered(out_term, base)
+            behind = own, scatter_cols(pieces_after(pairs, arrays_of(base)), ways)
+            out_terms.append(out_term)
+            pieces = pieces_after(other_core(base, ways), out_term)
         else:
-            term = dot_tn(act_ones[m], dpre)
-            sums = spread(after(dpre, term), qkv, spot, block, ways, True)
-            out_term = dot_tn(mixed[m], after(whole, sums))
-            out_term, arrived = covered(out_term, send_pairs(sums, ways))
+            dpre, grad_gate, grad_up, grad_out = lax.optimization_barrier(
+                (dpre, grad_gate, grad_up, grad_out)
+            )
+            qkv_grad = (sum(qkv_terms) + dot_tn(act_ones[m], dpre)).astype(BF)
+            dpre = after(dpre, qkv_grad)
+            grad_qkv = scatter_row(qkv_grad, 0)
+            sums = spread(dpre, qkv, spot, block, ways, True)
+            sums, flown = covered(sums, out_flying)
+            arrived = send_pairs(sums, ways)
+            totals = [
+                resid + out.astype(F32) for resid, out in zip(resids[:-1], after(ffn_outs, sums))
+            ] + [resids[-1] + total_of(out_own, flown)]
+            outputs = [total.astype(BF) for total in totals]
+            outputs, arrived = covered(outputs, arrived)
             own, pairs = add_pairs(sums, arrived)
-            firsts.append(total_of(own, scatter_cols(pairs, ways, "direct")))
-        qkv_terms.append(term)
-        out_terms.append(out_term)
-        means.append(sum_over(stat.reshape(tokens, 128)[:, 0], "col", ways)[:, None] / width)
-    grad_qkv = scatter_row(sum(qkv_terms), 0)
-    grad_out = scatter_row(sum(out_terms), 1)
+            firsts.append((own, scatter_cols(pairs, ways, "split")))
+            firsts[0] = after(firsts[0][0], arrays_of(pairs)), firsts[0][1]
+            stat, dconv, dgain = after((stat, dconv, dgain), sums)
+            stats.append(stat)
+    means = [
+        sum_cols(stat.reshape(tokens, 128)[:, 0], ways)[:, None] / width for stat in stats
+    ]
     input_grads, gain_one_grad = [], 0.0
     for m in range(micro):
+        act_grad = total_of(*firsts[m])
         unit = inputs[m].astype(F32) * inv_ones[m]
-        gain_one_grad = gain_one_grad + jnp.sum(firsts[m] * unit, axis=0)
+        gain_one_grad = gain_one_grad + jnp.sum(act_grad * unit, axis=0)
         input_grads.append(
-            resid_grads[m] + inv_ones[m] * (firsts[m] * own_one - unit * means[m])
+            resid_grads[m] + inv_ones[m] * (act_grad * own_one - unit * means[m])
         )
 
     grad_qkv, grad_out, grad_gate, grad_up, grad_down = (
         grad.astype(F32) for grad in (grad_qkv, grad_out, grad_gate, grad_up, grad_down)
     )
-    head_sum = sum_over(jnp.sum(dgain, axis=0), "col", ways)
+    head_sum = sum_cols(jnp.sum(dgain, axis=0), ways)
     conv_sum = dconv.reshape(4, 8, 3, hw).sum(axis=1).transpose(1, 2, 0)
     early = sum_over(
         jnp.concatenate([conv_sum.reshape(-1), head_sum, gain_two_grad]), "row", rows_ways

time: 1050 us -> 1000 us (0.952)
  waiting for transfers between devices: 328 us -> 293 us
  other arithmetic: 114 us -> 97.8 us
  Pallas kernels: 334 us -> 318 us
  local copies, waits for them, and re-layouts: 48.3 us -> 63.7 us
    ppermute x122 -> x142, waiting for transfers between devices: 282 us -> 253 us  [swap(): return lax.ppermute(values, 'col', [(i, i ^ bit) for i in range(ways)])]
    ppermute x24 -> x9, waiting for transfers between devices: 38.7 us -> 21.2 us  [sum_over(): lax.ppermute(values, axis, [(i, i ^ bit) for i in range(size)])]
    pallas_call x10, Pallas kernels: 217 us -> 201 us  [tiled(): pl.pallas_call(kernel, grid=(rows // tile,), in_specs=[SPOT] + [fixed(a)...]
    ppermute x24 -> x9, starting transfers between devices: 21.6 us -> 8.35 us  [sum_over(): lax.ppermute(values, axis, [(i, i ^ bit) for i in range(size)])]
    all_gather x1, waiting for transfers between devices: 5.79 us -> 17.2 us  [local(): down = lax.all_gather(w_down, 'row', axis=0, tiled=False)]
    ppermute x122 -> x142, starting transfers between devices: 81.1 us -> 88.6 us  [swap(): return lax.ppermute(values, 'col', [(i, i ^ bit) for i in range(ways)])]
    convert_element_type x24 -> x23, other arithmetic: 48.6 us -> 42.6 us  [add_low(): return sum((term.astype(F32) for term in terms)).astype(BF)]
    convert_element_type x10 -> x8, other arithmetic: 36.1 us -> 30.4 us  [the longest x2 9.75 us: add_residual(): near = gather_near(resids[m].astype(BF), ways)]
  transfers between devices with their start and end apart: 156 -> 162, of which waited for: 52 -> 62; matrix products, arithmetic and copies ran while one was open for 22% -> 25% of each run, Pallas kernels for 32% -> 32%
where the time goes in v2:
time: 1000 us; the launch traced here: 991 us
  Pallas kernels  318 us (32%)
  waiting for transfers between devices  293 us (29%)
  matrix products  105 us (10%)
  starting transfers between devices  97.9 us (10%)
  other arithmetic  97.8 us (10%)
  local copies, waits for them, and re-layouts  63.7 us (6%)
  between operations  15.5 us (2%)
    ppermute x142, waiting for transfers between devices, swap(): return lax.ppermute(values, 'col', [(i, i ^ bit) for i in range(ways)])  253 us
    pallas_call x10, Pallas kernels, tiled(): pl.pallas_call(kernel, grid=(rows // tile,), in_specs=[SPOT] + [fixed(a)...  201 us
    dot_general x10, matrix products, dot_tn(): lax.dot_general(a, b, (((0,), (0,)), ((), ())), preferred_element_type=F32)  105 us
    ppermute x142, starting transfers between devices, swap(): return lax.ppermute(values, 'col', [(i, i ^ bit) for i in range(ways)])  88.6 us
    pallas_call x2, Pallas kernels, mix_backward(): pl.pallas_call(partial(mix_bwd_kernel, heads, chunk, sub), grid=(steps,),...  68.9 us
    pallas_call x2, Pallas kernels, mix_forward(): pl.pallas_call(partial(mix_fwd_kernel, heads, chunk, sub), grid=(steps,),...  48.4 us
    convert_element_type x23, other arithmetic, add_low(): return sum((term.astype(F32) for term in terms)).astype(BF)  42.6 us
    ppermute x9, waiting for transfers between devices, sum_over(): lax.ppermute(values, axis, [(i, i ^ bit) for i in range(size)])  21.2 us
  transfers between devices with their start and end apart: 162, of which 62 were waited for; matrix products, arithmetic and copies ran while one was open for 25% of the time, Pallas kernels for 32%

profile of v2, /device:TPU:0, one launch (start us, length us, event | category | flops | bytes accessed | tf_op | source)
XLA Modules:
  0.0 990.8 jit_solution(9806913340533035137)
XLA Ops:
  26.3 19.6 %collective-permute-done.6.refs_2_ = bf16[2048,256]{1,0:T(8,128)(2,1)} collective-permute-done((bf16[2048,256]{1,0:T(8,128)(2,1)}, bf16[2048,256]{1,0:T(8,128)(2,1)}, u32[]{:S(2)}, u32[]{:S(2)}) %collective-permute-start.6) | collective-permute-done | bytes 1048608 | tf_op jit(solution)/shard_map/ppermute | solution.py:464
  102.6 17.4 %project.2 = (f32[2048,896]{1,0:T(8,128)}, bf16[2048,2048]{1,0:T(8,128)(2,1)}, f32[2048,128]{1,0:T(8,128)}) custom-call(s32[1]{0:T(128)} %bitcast.1.spot_ref, f32[1,2048]{1,0:T(1,128)} %reshape.399.gain_ref, bf16[2048,896]{1,0:T(8,128)(2,1)} %all-gather.13.cloned.1.call-done.weight_ref, bf16[2048,256]{1,0:T(8,128)(2,1)} %get-tuple-element.401.refs_0_, ...), custom_call_target="tpu_custom_call" | custom-call | flops 7600000000 | tf_op jit(solution)/shard_map/project/pallas_call | solution.py:698
  120.0 24.2 %mix_forward.2 = (bf16[1,2048,256]{2,1,0:T(8,128)(2,1)}, f32[1,2048,256]{2,1,0:T(8,128)}, bf16[1,2048,256]{2,1,0:T(8,128)(2,1)}, bf16[1,2048,256]{2,1,0:T(8,128)...) custom-call(f32[1,16,16,128]{3,2,1,0:T(8,128)} %concatenate.21.marks_ref, ...), custom_call_target="tpu_custom_call" | custom-call | flops 9600000000 | tf_op jit(solution)/shard_map/mix_forward/pallas_call | solution.py:395
  176.1 17.3 %project.3 = (f32[2048,896]{1,0:T(8,128)}, bf16[2048,2048]{1,0:T(8,128)(2,1)}, f32[2048,128]{1,0:T(8,128)}) custom-call(s32[1]{0:T(128)} %bitcast.1.spot_ref, f32[1,2048]{1,0:T(1,128)} %reshape.399.gain_ref, bf16[2048,896]{1,0:T(8,128)(2,1)} %all-gather.13.cloned.1.call-done.weight_ref, bf16[2048,256]{1,0:T(8,128)(2,1)} %copy-done.42, ...), custom_call_target="tpu_custom_call" | custom-call | flops 7600000000 | tf_op jit(solution)/shard_map/project/pallas_call | solution.py:698
  198.7 24.2 %mix_forward.3 = (bf16[1,2048,256]{2,1,0:T(8,128)(2,1)}, f32[1,2048,256]{2,1,0:T(8,128)}, bf16[1,2048,256]{2,1,0:T(8,128)(2,1)}, bf16[1,2048,256]{2,1,0:T(8,128)...) custom-call(f32[1,16,16,128]{3,2,1,0:T(8,128)} %concatenate.24.marks_ref, ...), custom_call_target="tpu_custom_call" | custom-call | flops 9600000000 | tf_op jit(solution)/shard_map/mix_forward/pallas_call | solution.py:395
  229.3 12.6 %collective-permute-done.37 = bf16[2048,256]{1,0:T(8,128)(2,1)} collective-permute-done((bf16[2048,256]{1,0:T(8,128)(2,1)}, bf16[2048,256]{1,0:T(8,128)(2,1)}, u32[]{:S(2)}, u32[]{:S(2)}) %collective-permute-start.37) | collective-permute-done | bytes 1048608 | tf_op jit(solution)/shard_map/ppermute | solution.py:464
  250.0 22.8 %collective-permute-done.39.refs_2_ = bf16[2048,256]{1,0:T(8,128)(2,1)} collective-permute-done((bf16[2048,256]{1,0:T(8,128)(2,1)}, bf16[2048,256]{1,0:T(8,128)(2,1)}, u32[]{:S(2)}, u32[]{:S(2)}) %collective-permute-start.39) | collective-permute-done | bytes 1048608 | tf_op jit(solution)/shard_map/ppermute | solution.py:464
  277.9 17.2 %all-gather.19.cloned.1.call-done = bf16[2816,512]{1,0:T(8,128)(2,1)} async-done(((bf16[704,512]{1,0:T(8,128)(2,1)}), bf16[2816,512]{1,0:T(8,128)(2,1)}) %all-gather.19.cloned.1.call-update) | async-done | bytes 2883600 | tf_op jit(solution)/shard_map/all_gather | solution.py:825
  321.4 53.9 %feed_forward.2 = (bf16[2048,2048]{1,0:T(8,128)(2,1)}, bf16[2048,2048]{1,0:T(8,128)(2,1)}, bf16[2048,704]{1,0:T(8,128)(2,1)}, bf16[2048,704]{1,0:T(8,128)(2,1)},...) custom-call(s32[1]{0:T(128)} %bitcast.1.spot_ref, ...), custom_call_target="tpu_custom_call" | custom-call | flops 21600000000 | tf_op jit(solution)/shard_map/feed_forward/pallas_call | solution.py:698
  390.0 10.8 %fusion.46 = f32[704,2048]{1,0:T(8,128)} fusion(bf16[2048,704]{1,0:T(8,128)(2,1)S(1)} %copy-done.106, bf16[2048,2048]{1,0:T(8,128)(2,1)} %get-tuple-element.531), kind=kOutput, calls=%fused_computation.144 | convolution fusion | flops 5905580032 | bytes 17039360 | tf_op jit(solution)/shard_map/dot_general | solution.py:33
  416.4 31.7 %collective-permute-done.64.refs_2_ = bf16[2048,256]{1,0:T(8,128)(2,1)S(1)} collective-permute-done((bf16[2048,256]{1,0:T(8,128)(2,1)S(1)}, bf16[2048,256]{1,0:T(8,128)(2,1)S(1)}, u32[]{:S(2)}, u32[]{:S(2)}) %collective-permute-start.64) | collective-permute-done | bytes 1048608 | tf_op jit(solution)/shard_map/ppermute | solution.py:464
  458.8 12.6 %collective-permute-done.69.refs_3_ = bf16[2048,128]{1,0:T(8,128)(2,1)S(1)} collective-permute-done((bf16[2048,128]{1,0:T(8,128)(2,1)S(1)}, bf16[2048,128]{1,0:T(8,128)(2,1)S(1)}, u32[]{:S(2)}, u32[]{:S(2)}) %collective-permute-start.69) | collective-permute-done | bytes 524320 | tf_op jit(solution)/shard_map/ppermute | solution.py:464
  489.1 55.2 %feed_forward.3 = (bf16[2048,2048]{1,0:T(8,128)(2,1)}, bf16[2048,2048]{1,0:T(8,128)(2,1)}, bf16[2048,704]{1,0:T(8,128)(2,1)}, bf16[2048,704]{1,0:T(8,128)(2,1)},...) custom-call(s32[1]{0:T(128)} %bitcast.1.spot_ref, ...), custom_call_target="tpu_custom_call" | custom-call | flops 21600000000 | tf_op jit(solution)/shard_map/feed_forward/pallas_call | solution.py:698
  575.5 14.7 %collective-permute-done.89.refs_2_ = bf16[2048,256]{1,0:T(8,128)(2,1)} collective-permute-done((bf16[2048,256]{1,0:T(8,128)(2,1)}, bf16[2048,256]{1,0:T(8,128)(2,1)}, u32[]{:S(2)}, u32[]{:S(2)}) %collective-permute-start.89) | collective-permute-done | bytes 1048608 | tf_op jit(solution)/shard_map/ppermute | solution.py:464
  590.2 12.1 %add_convert_fusion.2 = bf16[704,2048]{1,0:T(8,128)(2,1)} fusion(f32[704,2048]{1,0:T(8,128)} %fusion.47, bf16[2048,704]{1,0:T(8,128)(2,1)S(1)} %copy-done.107, bf16[2048,2048]{1,0:T(8,128)(2,1)} %get-tuple-element.655), kind=kOutput, calls=%fused_computation.2 | convolution fusion | flops 5908463616 | bytes 19922944 | tf_op jit(solution)/shard_map/dot_general | solution.py:33
  615.8 11.9 %add_convert_fusion.1 = bf16[704,2048]{1,0:T(8,128)(2,1)} fusion(f32[704,2048]{1,0:T(8,128)} %fusion.48, bf16[2048,704]{1,0:T(8,128)(2,1)} %get-tuple-element.626, bf16[2048,2048]{1,0:T(8,128)(2,1)} %get-tuple-element.655), kind=kOutput, calls=%fused_computation.1 | convolution fusion | flops 5908463616 | bytes 19922944 | tf_op jit(solution)/shard_map/dot_general | solution.py:33
  655.2 34.3 %mix_backward.2 = (bf16[1,2048,896]{2,1,0:T(8,128)(2,1)}, f32[1,2048,128]{2,1,0:T(8,128)}, f32[32,768]{1,0:T(8,128)}, f32[8,128]{1,0:T(8,128)}) custom-call(f32[1,16,16,128]{3,2,1,0:T(8,128)} %concatenate.21.marks_ref, f32[8,768]{1,0:T(8,128)} %pad.37.taps_ref, f32[1,128]{1,0:T(1,128)} %reshape.350.gain_ref, f32[1,2048,256]{2,1,0:T(8,128)} %get-tuple-element.666.o_ref, ...), custom_call_target="tpu_custom_call" | custom-call | flops 13600000000 | tf_op jit(solution)/shard_map/mix_backward/pallas_call | solution.py:435
  696.8 13.1 %spread.6 = (bf16[2048,256]{1,0:T(8,128)(2,1)}, bf16[2048,256]{1,0:T(8,128)(2,1)}, bf16[2048,256]{1,0:T(8,128)(2,1)}, bf16[2048,256]{1,0:T(8,128)(2,1)}, bf16[20...) custom-call(s32[1]{0:T(128)} %bitcast.1.spot_ref, ...), custom_call_target="tpu_custom_call" | custom-call | flops 5600000000 | tf_op jit(solution)/shard_map/spread/pallas_call | solution.py:698
  712.9 14.8 %fusion.50 = f32[2048,896]{1,0:T(8,128)} fusion(bf16[2048,2048]{1,0:T(8,128)(2,1)} %get-tuple-element.665, bf16[2048,896]{1,0:T(8,128)(2,1)} %bitcast.198), kind=kOutput, calls=%fused_computation.148 | convolution fusion | flops 7516192768 | bytes 19398656 | tf_op jit(solution)/shard_map/dot_general | solution.py:33
  796.7 34.6 %mix_backward.3 = (bf16[1,2048,896]{2,1,0:T(8,128)(2,1)}, f32[1,2048,128]{2,1,0:T(8,128)}, f32[32,768]{1,0:T(8,128)}, f32[8,128]{1,0:T(8,128)}) custom-call(f32[1,16,16,128]{3,2,1,0:T(8,128)} %concatenate.24.marks_ref, f32[8,768]{1,0:T(8,128)} %pad.37.taps_ref, f32[1,128]{1,0:T(1,128)} %reshape.350.gain_ref, f32[1,2048,256]{2,1,0:T(8,128)} %get-tuple-element.621.o_ref, ...), custom_call_target="tpu_custom_call" | custom-call | flops 13600000000 | tf_op jit(solution)/shard_map/mix_backward/pallas_call | solution.py:435
  842.6 14.8 %add_convert_fusion = bf16[2048,896]{1,0:T(8,128)(2,1)} fusion(f32[2048,896]{1,0:T(8,128)} %fusion.50, bf16[2048,2048]{1,0:T(8,128)(2,1)} %get-tuple-element.731, bf16[2048,896]{1,0:T(8,128)(2,1)} %bitcast.199), kind=kOutput, calls=%fused_computation | convolution fusion | flops 7519862784 | bytes 23068672 | tf_op jit(solution)/shard_map/dot_general | solution.py:33
  857.4 13.2 %spread.7 = (bf16[2048,256]{1,0:T(8,128)(2,1)}, bf16[2048,256]{1,0:T(8,128)(2,1)}, bf16[2048,256]{1,0:T(8,128)(2,1)}, bf16[2048,256]{1,0:T(8,128)(2,1)}, bf16[20...) custom-call(s32[1]{0:T(128)} %bitcast.1.spot_ref, ...), custom_call_target="tpu_custom_call" | custom-call | flops 5600000000 | tf_op jit(solution)/shard_map/spread/pallas_call | solution.py:698
  870.7 12.9 %collective-permute-done.126 = bf16[2048,256]{1,0:T(8,128)(2,1)} collective-permute-done((bf16[2048,256]{1,0:T(8,128)(2,1)S(1)}, bf16[2048,256]{1,0:T(8,128)(2,1)}, u32[]{:S(2)}, u32[]{:S(2)}) %collective-permute-start.126) | collective-permute-done | bytes 1048608 | tf_op jit(solution)/shard_map/ppermute | solution.py:464
  929.6 19.0 %collective-permute-done.142 = f32[2048]{0:T(1024)S(1)} collective-permute-done((f32[2048]{0:T(1024)S(1)}, f32[2048]{0:T(1024)S(1)}, u32[]{:S(2)}, u32[]{:S(2)}) %collective-permute-start.142) | collective-permute-done | bytes 8224 | tf_op jit(solution)/shard_map/ppermute | solution.py:464
  (716 shorter events, 460.2 us)
Async XLA Ops:
  7.3 95.4 %all-gather.13.cloned.1.call-start = ((), (), s32[]{:S(2)}) async-start(), calls=%async_computation.13 | async-start | bytes 4587520 | tf_op jit(solution)/shard_map/all_gather | solution.py:821
  10.4 133.8 %all-gather.11.cloned.1.call-start = ((), (), s32[]{:S(2)}) async-start(), calls=%async_computation.12 | async-start | bytes 1310720 | tf_op jit(solution)/shard_map/all_gather | solution.py:822
  11.2 184.2 %all-gather.15.cloned.1.call-start = ((), (), s32[]{:S(2)}) async-start(), calls=%async_computation.14 | async-start | bytes 3604480 | tf_op jit(solution)/shard_map/all_gather | solution.py:823
  11.9 235.0 %all-gather.17.cloned.1.call-start = ((), (), s32[]{:S(2)}) async-start(), calls=%async_computation.15 | async-start | bytes 3604480 | tf_op jit(solution)/shard_map/all_gather | solution.py:824
  26.3 268.9 %all-gather.19.cloned.1.call-start = ((), (), s32[]{:S(2)}) async-start(), calls=%async_computation.16 | async-start | bytes 3604480 | tf_op jit(solution)/shard_map/all_gather | solution.py:825
  99.6 56.7 %collective-permute-start.27 = (bf16[2048,256]{1,0:T(8,128)(2,1)}, bf16[2048,256]{1,0:T(8,128)(2,1)}, u32[]{:S(2)}, u32[]{:S(2)}) collective-permute-start(bf16[2048,256]{1,0:T(8,128)(2,1)} %get-tuple-element.487.refs_10_), channel_id=1, source_target_pairs={{0,2},{1,3},{2,0},{3,1},{4,6},{5,7},{6,4},{7,5},{8,10},{9,11},{10,... | collective-permute-start | bytes 3145736 | tf_op jit(solution)/shard_map/ppermute | solution.py:464
  100.4 56.9 %collective-permute-start.32 = (bf16[2048,256]{1,0:T(8,128)(2,1)}, bf16[2048,256]{1,0:T(8,128)(2,1)}, u32[]{:S(2)}, u32[]{:S(2)}) collective-permute-start(bf16[2048,256]{1,0:T(8,128)(2,1)} %get-tuple-element.564.refs_10_), channel_id=1, source_target_pairs={{0,4},{1,5},{2,6},{3,7},{4,0},{5,1},{6,2},{7,3},{8,12},{9,13},{10,... | collective-permute-start | bytes 3145736 | tf_op jit(solution)/shard_map/ppermute | solution.py:464
  101.5 57.8 %collective-permute-start.31 = (bf16[2048,256]{1,0:T(8,128)(2,1)}, bf16[2048,256]{1,0:T(8,128)(2,1)}, u32[]{:S(2)}, u32[]{:S(2)}) collective-permute-start(bf16[2048,256]{1,0:T(8,128)(2,1)} %get-tuple-element.564.refs_10_), channel_id=1, source_target_pairs={{0,2},{1,3},{2,0},{3,1},{4,6},{5,7},{6,4},{7,5},{8,10},{9,11},{10,... | collective-permute-start | bytes 3145736 | tf_op jit(solution)/shard_map/ppermute | solution.py:464
  152.1 397.6 %reduce-scatter.7.cloned.1.call-start = ((), (), s32[]{:S(2)}) async-start(), calls=%async_computation.6 | async-start | bytes 9437184 | tf_op jit(solution)/shard_map/reduce_scatter | solution.py:932
  170.5 71.4 %collective-permute-start.18 = (bf16[2048,256]{1,0:T(8,128)(2,1)}, bf16[2048,256]{1,0:T(8,128)(2,1)}, u32[]{:S(2)}, u32[]{:S(2)}) collective-permute-start(bf16[2048,256]{1,0:T(8,128)(2,1)} %get-tuple-element.407), channel_id=1, source_target_pairs={{0,1},{1,0},{2,3},{3,2},{4,5},{5,4},{6,7},{7,6},{8,9},{9,8},{10,11... | collective-permute-start | bytes 3145736 | tf_op jit(solution)/shard_map/ppermute | solution.py:464
  317.4 59.0 %collective-permute-start.58 = (bf16[2048,256]{1,0:T(8,128)(2,1)}, bf16[2048,256]{1,0:T(8,128)(2,1)}, u32[]{:S(2)}, u32[]{:S(2)}) collective-permute-start(bf16[2048,256]{1,0:T(8,128)(2,1)} %get-tuple-element.522), channel_id=1, source_target_pairs={{0,1},{1,0},{2,3},{3,2},{4,5},{5,4},{6,7},{7,6},{8,9},{9,8},{10,11... | collective-permute-start | bytes 3145736 | tf_op jit(solution)/shard_map/ppermute | solution.py:464
  317.8 57.5 %collective-permute-start.55 = (bf16[2048,256]{1,0:T(8,128)(2,1)}, bf16[2048,256]{1,0:T(8,128)(2,1)S(1)}, u32[]{:S(2)}, u32[]{:S(2)}) collective-permute-start(bf16[2048,256]{1,0:T(8,128)(2,1)} %add_convert_fusion.24), channel_id=1, source_target_pairs={{0,2},{1,3},{2,0},{3,1},{4,6},{5,7},{6,4},{7,5},{8,10},{9,11},{10,... | collective-permute-start | bytes 3145736 | tf_op jit(solution)/shard_map/ppermute | solution.py:464
  319.3 56.0 %collective-permute-start.56 = (bf16[2048,256]{1,0:T(8,128)(2,1)}, bf16[2048,256]{1,0:T(8,128)(2,1)}, u32[]{:S(2)}, u32[]{:S(2)}) collective-permute-start(bf16[2048,256]{1,0:T(8,128)(2,1)} %add_convert_fusion.23), channel_id=1, source_target_pairs={{0,4},{1,5},{2,6},{3,7},{4,0},{5,1},{6,2},{7,3},{8,12},{9,13},{10,... | collective-permute-start | bytes 3145736 | tf_op jit(solution)/shard_map/ppermute | solution.py:464
  320.9 54.5 %collective-permute-start.57 = (bf16[2048,256]{1,0:T(8,128)(2,1)}, bf16[2048,256]{1,0:T(8,128)(2,1)}, u32[]{:S(2)}, u32[]{:S(2)}) collective-permute-start(bf16[2048,256]{1,0:T(8,128)(2,1)} %add_convert_fusion.22), channel_id=1, source_target_pairs={{0,6},{1,7},{2,4},{3,5},{4,2},{5,3},{6,0},{7,1},{8,14},{9,15},{10,... | collective-permute-start | bytes 3145736 | tf_op jit(solution)/shard_map/ppermute | solution.py:464
  376.4 313.1 %reduce-scatter.9.cloned.1.call-start = ((), (), s32[]{:S(2)}) async-start(), calls=%async_computation.7 | async-start | bytes 3604480 | tf_op jit(solution)/shard_map/reduce_scatter | solution.py:779
  485.0 59.4 %collective-permute-start.81 = (bf16[2048,256]{1,0:T(8,128)(2,1)}, bf16[2048,256]{1,0:T(8,128)(2,1)}, u32[]{:S(2)}, u32[]{:S(2)}) collective-permute-start(bf16[2048,256]{1,0:T(8,128)(2,1)} %add_convert_fusion.21), channel_id=1, source_target_pairs={{0,2},{1,3},{2,0},{3,1},{4,6},{5,7},{6,4},{7,5},{8,10},{9,11},{10,... | collective-permute-start | bytes 3145736 | tf_op jit(solution)/shard_map/ppermute | solution.py:464
  486.9 57.5 %collective-permute-start.82 = (bf16[2048,256]{1,0:T(8,128)(2,1)}, bf16[2048,256]{1,0:T(8,128)(2,1)}, u32[]{:S(2)}, u32[]{:S(2)}) collective-permute-start(bf16[2048,256]{1,0:T(8,128)(2,1)} %add_convert_fusion.20), channel_id=1, source_target_pairs={{0,4},{1,5},{2,6},{3,7},{4,0},{5,1},{6,2},{7,3},{8,12},{9,13},{10,... | collective-permute-start | bytes 3145736 | tf_op jit(solution)/shard_map/ppermute | solution.py:464
  487.2 57.1 %collective-permute-start.83 = (bf16[2048,256]{1,0:T(8,128)(2,1)}, bf16[2048,256]{1,0:T(8,128)(2,1)}, u32[]{:S(2)}, u32[]{:S(2)}) collective-permute-start(bf16[2048,256]{1,0:T(8,128)(2,1)} %add_convert_fusion.19), channel_id=1, source_target_pairs={{0,6},{1,7},{2,4},{3,5},{4,2},{5,3},{6,0},{7,1},{8,14},{9,15},{10,... | collective-permute-start | bytes 3145736 | tf_op jit(solution)/shard_map/ppermute | solution.py:464
  564.6 277.9 %reduce-scatter.11.cloned.1.call-start = ((), (), s32[]{:S(2)}) async-start(), calls=%async_computation.8 | async-start | bytes 3604480 | tf_op jit(solution)/shard_map/reduce_scatter | solution.py:779
  615.7 226.8 %reduce-scatter.13.cloned.1.call-start = ((), (), s32[]{:S(2)}) async-start(), calls=%async_computation.9 | async-start | bytes 3604480 | tf_op jit(solution)/shard_map/reduce_scatter | solution.py:779
  709.9 132.6 %reduce-scatter.15.cloned.1.call-start = ((), (), s32[]{:S(2)}) async-start(), calls=%async_computation.10 | async-start | bytes 1310720 | tf_op jit(solution)/shard_map/reduce_scatter | solution.py:779
  780.0 200.2 %reduce-scatter.17.cloned.1.call-start = ((), (), s32[]{:S(2)}) async-start(), calls=%async_computation.11 | async-start | bytes 4587520 | tf_op jit(solution)/shard_map/reduce_scatter | solution.py:779
  794.8 75.9 %collective-permute-start.124 = (bf16[2048,256]{1,0:T(8,128)(2,1)}, bf16[2048,256]{1,0:T(8,128)(2,1)}, u32[]{:S(2)}, u32[]{:S(2)}) collective-permute-start(bf16[2048,256]{1,0:T(8,128)(2,1)} %add_convert_fusion.15), channel_id=1, source_target_pairs={{0,2},{1,3},{2,0},{3,1},{4,6},{5,7},{6,4},{7,5},{8,10},{9,11},{10,... | collective-permute-start | bytes 3145736 | tf_op jit(solution)/shard_map/ppermute | solution.py:464
  795.5 75.2 %collective-permute-start.125 = (bf16[2048,256]{1,0:T(8,128)(2,1)}, bf16[2048,256]{1,0:T(8,128)(2,1)}, u32[]{:S(2)}, u32[]{:S(2)}) collective-permute-start(bf16[2048,256]{1,0:T(8,128)(2,1)} %add_convert_fusion.14), channel_id=1, source_target_pairs={{0,4},{1,5},{2,6},{3,7},{4,0},{5,1},{6,2},{7,3},{8,12},{9,13},{10,... | collective-permute-start | bytes 3145736 | tf_op jit(solution)/shard_map/ppermute | solution.py:464
  (248 other events, 3838.5 us)
Sparse Core Ops, SparseCore 0:
  10.6 77.5 all-gather.12
  89.7 26.5 all-gather.10
  117.8 58.6 all-gather.14
  178.0 57.8 all-gather.16
  237.3 57.8 all-gather.18
  376.5 99.6 reduce-scatter.6
  564.8 53.2 reduce-scatter.8
  620.5 56.0 reduce-scatter.10
  710.1 52.8 reduce-scatter.12
  780.1 24.8 reduce-scatter.14
  857.6 66.4 reduce-scatter.16

commit v3 on v2

--- a/solution.py
+++ b/solution.py
@@ -841,8 +841,11 @@
 
     def add_residual(m, own, arrived):
         resids.append(inputs[m].astype(F32) + total_of(own, arrived))
+        if m:
+            act_base.append(gather_cols(resids[m].astype(BF), ways))
+            return
         near = gather_near(resids[m].astype(BF), ways)
-        act_base.append(near if m else gather_far(near, ways, down))
+        act_base.append(gather_far(near, ways))
 
     flying = None
     for m in range(micro):
@@ -877,7 +880,8 @@
         if m == micro - 1:
             sums, ups = lax.optimization_barrier((sums, ups))
     own, pairs = add_pairs(sums, send_pairs(sums, ways))
-    flying = own, scatter_cols(pairs, ways)
+    arrived = scatter_cols(pairs, ways, "split")
+    add_residual(micro - 1, own, arrived)
     cots = [other_core(base, ways) for base in cot_base]
 
     ffn_saved, ffn_outs, inners, resid_grads, grad_base = [], [], [], [], []
@@ -893,55 +897,57 @@
         grad_base.append(gather_near(resid_grads[m].astype(BF), ways))
         return jnp.sum(act_grad * unit, axis=0)
 
+    flying = None
     for m in range(micro):
+        last = m == micro - 1
         pieces = other_core(act_base[m], ways)
-        if m:
-            pieces = pieces_after(pieces, up_grad, inners)
-        else:
-            pieces = pieces_after(pieces, arrays_of(pairs))
+        pieces = pieces_after(pieces, resids, down_grad, arrays_of(pairs))
         kept, grads, outs = feed_forward(
-            pieces, cots[m], gain_two, gates, ups, down, spot, block, ways, m == micro - 1
-        )
-        (kept, grads, outs), arrived = covered((kept, grads, outs), flying[1])
-        if m < micro - 1:
-            add_residual(m + 1, flying[0], arrived)
-            kept, grads = after((kept, grads), resids[m + 1])
-        else:
+            pieces, cots[m], gain_two, gates, ups, down, spot, block, ways, last
+        )
+        if not last:
+            (kept, grads, outs), act_base[m + 1] = covered(
+                (kept, grads, outs), act_base[m + 1]
+            )
+        if flying:
+            before = ffn_saved[m - 1]
+            left = after(before[0], kept[5])
+            gate_grad = grow(gate_grad, before[3], left, False)
+            up_grad = grow(up_grad, before[4], after(left, gate_grad), False)
+            (kept, grads, outs, gate_grad, up_grad), arrived = covered(
+                (kept, grads, outs, gate_grad, up_grad), flying[1]
+            )
             gain_two_grad = gain_two_grad + finish_ffn(m - 1, flying[0], arrived)
-            kept, grads = after((kept, grads), resid_grads[m - 1])
-        if m:
-            kept, ffn_outs[m - 1] = lax.optimization_barrier((kept, ffn_outs[m - 1]))
+            kept, grads, ffn_outs[m - 1] = lax.optimization_barrier(
+                (kept, after(grads, resid_grads[m - 1]), ffn_outs[m - 1])
+            )
         ffn_saved.append(kept)
         inners.append(sum_cols(kept[5][:, 1], ways)[:, None] / width)
-        last = m == micro - 1
         down_grad, arrived = covered(
             grow(down_grad, kept[2], kept[1], last), send_pairs(grads, ways)
         )
         own, pairs = add_pairs(grads, arrived)
-        gate_grad = grow(gate_grad, kept[3], after(kept[0], arrays_of(pairs)), last)
-        base = grad_base[0] if last else act_base[m + 1]
-        gate_grad, base = covered(gate_grad, base)
-        base = gather_far(base, ways)
-        right = after(kept[0], gate_grad, inners[m])
-        if last:
-            gate_grad, arrived = covered(gate_grad, send_pairs(outs, ways))
-            out_own, out_sums = add_pairs(outs, arrived)
-            right = after(right, arrays_of(out_sums))
-        else:
+        if not last:
+            flying = own, scatter_cols(pairs, ways)
             ffn_outs.append(
                 lax.psum_scatter(outs[0], "col", scatter_dimension=1, tiled=True)
             )
-        up_grad, base = covered(grow(up_grad, kept[4], right, last), base)
-        if not last:
-            act_base[m + 1] = base
-        flying = own, scatter_cols(pieces_after(pairs, arrays_of(base)), ways)
+    kept = ffn_saved[-1]
+    gate_grad = grow(gate_grad, kept[3], after(kept[0], arrays_of(pairs)), True)
+    gate_grad, arrived = covered(gate_grad, send_pairs(outs, ways))
+    gate_grad, base = covered(gate_grad, grad_base[0])
+    out_own, out_sums = add_pairs(outs, arrived)
+    base = gather_far(base, ways)
+    right = after(kept[0], gate_grad, arrays_of(out_sums))
+    up_grad, base = covered(grow(up_grad, kept[4], right, True), base)
+    flying = own, scatter_cols(pieces_after(pairs, arrays_of(base)), ways)
     pieces = other_core(base, ways)
     grad_down = scatter_row(down_grad, 1)
     grad_gate = scatter_row(gate_grad, 1)
     grad_up = scatter_row(up_grad, 1)
 
     qkv_terms, out_terms, firsts, dconv, dgain = [], [], [], 0.0, 0.0
-    behind, stats = None, []
+    behind, means = None, []
     for m in range(micro):
         whole, dao = collect(pieces, out_parts, spot, block, ways)
         if m == micro - 1:
@@ -968,7 +974,7 @@
             term, arrived = covered(
                 dot_tn(act_ones[m], after(dpre, sums)), send_pairs(sums, ways)
             )
-            stats.append(after(stat, sums))
+            means.append(sum_cols(stat.reshape(tokens, 128)[:, 0], ways)[:, None] / width)
             own, pairs = add_pairs(sums, arrived)
             term, base = covered(term, grad_base[m + 1])
             base = gather_far(base, ways)
@@ -979,28 +985,42 @@
             out_terms.append(out_term)
             pieces = pieces_after(other_core(base, ways), out_term)
         else:
-            dpre, grad_gate, grad_up, grad_out = lax.optimization_barrier(
-                (dpre, grad_gate, grad_up, grad_out)
+            dpre, grad_gate, grad_up, grad_out, means = lax.optimization_barrier(
+                (dpre, grad_gate, grad_up, grad_out, means)
             )
             qkv_grad = (sum(qkv_terms) + dot_tn(act_ones[m], dpre)).astype(BF)
             dpre = after(dpre, qkv_grad)
+            dconv, dgain, gain_two_grad = after((dconv, dgain, gain_two_grad), qkv_grad)
+            conv_sum = dconv.reshape(4, 8, 3, hw).sum(axis=1).transpose(1, 2, 0)
+            early = sum_over(
+                jnp.concatenate(
+                    [conv_sum.reshape(-1), jnp.sum(dgain, axis=0), gain_two_grad]
+                ),
+                "row", rows_ways,
+            )
             grad_qkv = scatter_row(qkv_grad, 0)
             sums = spread(dpre, qkv, spot, block, ways, True)
+            arrived = send_pairs(sums, ways)
             sums, flown = covered(sums, out_flying)
-            arrived = send_pairs(sums, ways)
-            totals = [
-                resid + out.astype(F32) for resid, out in zip(resids[:-1], after(ffn_outs, sums))
-            ] + [resids[-1] + total_of(out_own, flown)]
-            outputs = [total.astype(BF) for total in totals]
-            outputs, arrived = covered(outputs, arrived)
             own, pairs = add_pairs(sums, arrived)
-            firsts.append((own, scatter_cols(pairs, ways, "split")))
+            late_resids = after(resids, arrays_of(pairs))
+            outputs = [
+                (resid + out.astype(F32)).astype(BF)
+                for resid, out in zip(late_resids[:-1], ffn_outs)
+            ] + [(late_resids[-1] + total_of(out_own, flown)).astype(BF)]
+            arrived = scatter_cols(pairs, ways, "split")
             firsts[0] = after(firsts[0][0], arrays_of(pairs)), firsts[0][1]
-            stat, dconv, dgain = after((stat, dconv, dgain), sums)
-            stats.append(stat)
-    means = [
-        sum_cols(stat.reshape(tokens, 128)[:, 0], ways)[:, None] / width for stat in stats
-    ]
+            stat, early = after((stat, early), arrays_of(pairs))
+            means.append(sum_cols(stat.reshape(tokens, 128)[:, 0], ways)[:, None] / width)
+            head_sum = sum_cols(early[12 * hw : 12 * hw + 128], ways)
+    conv_grads = lax.dynamic_slice_in_dim(
+        early[: 12 * hw].reshape(3, hw, 4), row * share, share, axis=1
+    )
+    grad_two = lax.dynamic_slice_in_dim(early[12 * hw + 128 :], row * share, share)
+    output, conv_grads, grad_two = lax.optimization_barrier(
+        (jnp.stack(outputs), [conv_grads[kind] for kind in range(3)], grad_two)
+    )
+    firsts.append((own, pieces_after(arrived, output, conv_grads, grad_two)))
     input_grads, gain_one_grad = [], 0.0
     for m in range(micro):
         act_grad = total_of(*firsts[m])
@@ -1013,22 +1033,13 @@
     grad_qkv, grad_out, grad_gate, grad_up, grad_down = (
         grad.astype(F32) for grad in (grad_qkv, grad_out, grad_gate, grad_up, grad_down)
     )
-    head_sum = sum_cols(jnp.sum(dgain, axis=0), ways)
-    conv_sum = dconv.reshape(4, 8, 3, hw).sum(axis=1).transpose(1, 2, 0)
-    early = sum_over(
-        jnp.concatenate([conv_sum.reshape(-1), head_sum, gain_two_grad]), "row", rows_ways
-    )
     late = sum_over(gain_one_grad, "row", rows_ways)
-    conv_grads = lax.dynamic_slice_in_dim(
-        early[: 12 * hw].reshape(3, hw, 4), row * share, share, axis=1
-    )
     grad_head = lax.dynamic_slice_in_dim(
-        early[12 * hw : 12 * hw + 128], row * head_gain.shape[0], head_gain.shape[0]
-    )
-    grad_two = lax.dynamic_slice_in_dim(early[12 * hw + 128 :], row * share, share)
+        head_sum, row * head_gain.shape[0], head_gain.shape[0]
+    )
     grad_one = lax.dynamic_slice_in_dim(late, row * share, share)
     return (
-        jnp.stack(outputs),
+        output,
         jnp.stack(input_grads),
         grad_one,
         grad_qkv[:, :hw],

time: 1000 us -> 916 us (0.916)
  waiting for transfers between devices: 293 us -> 205 us
    ppermute x142 -> x141, waiting for transfers between devices: 253 us -> 187 us  [swap(): return lax.ppermute(values, 'col', [(i, i ^ bit) for i in range(ways)])]
    all_gather x1, waiting for transfers between devices: 17.2 us -> 0.01 us  [local(): down = lax.all_gather(w_down, 'row', axis=0, tiled=False)]
    convert_element_type x23 -> x25, other arithmetic: 42.6 us -> 36.1 us  [add_low(): return sum((term.astype(F32) for term in terms)).astype(BF)]
    slice x16 -> x14, local copies, waits for them, and re-layouts: 20.6 us -> 16.9 us  [gather_far(): first, second = (across[..., :half], along[..., half:])]
    ppermute x142 -> x141, starting transfers between devices: 88.6 us -> 88.4 us  [swap(): return lax.ppermute(values, 'col', [(i, i ^ bit) for i in range(ways)])]
  transfers between devices with their start and end apart: 162 -> 161, of which waited for: 62 -> 55; matrix products, arithmetic and copies ran while one was open for 25% -> 27% of each run, Pallas kernels for 32% -> 35%
where the time goes in v3:
time: 916 us; the launch traced here: 905 us
  Pallas kernels  317 us (35%)
  waiting for transfers between devices  205 us (22%)
  matrix products  108 us (12%)
  starting transfers between devices  103 us (11%)
  other arithmetic  91.9 us (10%)
  local copies, waits for them, and re-layouts  64.1 us (7%)
  between operations  15.8 us (2%)
    pallas_call x10, Pallas kernels, tiled(): pl.pallas_call(kernel, grid=(rows // tile,), in_specs=[SPOT] + [fixed(a)...  200 us
    ppermute x141, waiting for transfers between devices, swap(): return lax.ppermute(values, 'col', [(i, i ^ bit) for i in range(ways)])  187 us
    dot_general x10, matrix products, dot_tn(): lax.dot_general(a, b, (((0,), (0,)), ((), ())), preferred_element_type=F32)  108 us
    ppermute x141, starting transfers between devices, swap(): return lax.ppermute(values, 'col', [(i, i ^ bit) for i in range(ways)])  88.4 us
    pallas_call x2, Pallas kernels, mix_backward(): pl.pallas_call(partial(mix_bwd_kernel, heads, chunk, sub), grid=(steps,),...  68.8 us
    pallas_call x2, Pallas kernels, mix_forward(): pl.pallas_call(partial(mix_fwd_kernel, heads, chunk, sub), grid=(steps,),...  48.4 us
    convert_element_type x25, other arithmetic, add_low(): return sum((term.astype(F32) for term in terms)).astype(BF)  36.1 us
  transfers between devices with their start and end apart: 161, of which 55 were waited for; matrix products, arithmetic and copies ran while one was open for 27% of the time, Pallas kernels for 35%

profile of v3, /device:TPU:0, one launch (start us, length us, event | category | flops | bytes accessed | tf_op | source)
XLA Modules:
  0.0 905.5 jit_solution(16039269023954972750)
XLA Ops:
  24.8 19.6 %collective-permute-done.6.refs_2_ = bf16[2048,256]{1,0:T(8,128)(2,1)} collective-permute-done((bf16[2048,256]{1,0:T(8,128)(2,1)}, bf16[2048,256]{1,0:T(8,128)(2,1)}, u32[]{:S(2)}, u32[]{:S(2)}) %collective-permute-start.6) | collective-permute-done | bytes 1048608 | tf_op jit(solution)/shard_map/ppermute | solution.py:464
  58.2 9.3 %collective-permute-done.3 = bf16[32,928]{1,0:T(8,128)(2,1)S(1)} collective-permute-done((bf16[32,928]{1,0:T(8,128)(2,1)S(1)}, bf16[32,928]{1,0:T(8,128)(2,1)S(1)}, u32[]{:S(2)}, u32[]{:S(2)}) %collective-permute-start.3) | collective-permute-done | bytes 59424 | tf_op jit(solution)/shard_map/ppermute | solution.py:566
  102.0 17.4 %project.2 = (f32[2048,896]{1,0:T(8,128)}, bf16[2048,2048]{1,0:T(8,128)(2,1)}, f32[2048,128]{1,0:T(8,128)}) custom-call(s32[1]{0:T(128)} %bitcast.1.spot_ref, f32[1,2048]{1,0:T(1,128)} %reshape.398.gain_ref, bf16[2048,896]{1,0:T(8,128)(2,1)} %all-gather.13.cloned.1.call-done.weight_ref, bf16[2048,256]{1,0:T(8,128)(2,1)} %get-tuple-element.374.refs_0_, ...), custom_call_target="tpu_custom_call" | custom-call | flops 7600000000 | tf_op jit(solution)/shard_map/project/pallas_call | solution.py:698
  119.4 24.2 %mix_forward.2 = (bf16[1,2048,256]{2,1,0:T(8,128)(2,1)}, f32[1,2048,256]{2,1,0:T(8,128)}, bf16[1,2048,256]{2,1,0:T(8,128)(2,1)}, bf16[1,2048,256]{2,1,0:T(8,128)...) custom-call(f32[1,16,16,128]{3,2,1,0:T(8,128)} %concatenate.27.marks_ref, ...), custom_call_target="tpu_custom_call" | custom-call | flops 9600000000 | tf_op jit(solution)/shard_map/mix_forward/pallas_call | solution.py:395
  173.1 17.3 %project.3 = (f32[2048,896]{1,0:T(8,128)}, bf16[2048,2048]{1,0:T(8,128)(2,1)}, f32[2048,128]{1,0:T(8,128)}) custom-call(s32[1]{0:T(128)} %bitcast.1.spot_ref, f32[1,2048]{1,0:T(1,128)} %reshape.398.gain_ref, bf16[2048,896]{1,0:T(8,128)(2,1)} %all-gather.13.cloned.1.call-done.weight_ref, bf16[2048,256]{1,0:T(8,128)(2,1)} %copy-done.40, ...), custom_call_target="tpu_custom_call" | custom-call | flops 7600000000 | tf_op jit(solution)/shard_map/project/pallas_call | solution.py:698
  194.9 24.2 %mix_forward.3 = (bf16[1,2048,256]{2,1,0:T(8,128)(2,1)}, f32[1,2048,256]{2,1,0:T(8,128)}, bf16[1,2048,256]{2,1,0:T(8,128)(2,1)}, bf16[1,2048,256]{2,1,0:T(8,128)...) custom-call(f32[1,16,16,128]{3,2,1,0:T(8,128)} %concatenate.30.marks_ref, ...), custom_call_target="tpu_custom_call" | custom-call | flops 9600000000 | tf_op jit(solution)/shard_map/mix_forward/pallas_call | solution.py:395
  225.4 13.5 %collective-permute-done.36 = bf16[2048,256]{1,0:T(8,128)(2,1)} collective-permute-done((bf16[2048,256]{1,0:T(8,128)(2,1)}, bf16[2048,256]{1,0:T(8,128)(2,1)}, u32[]{:S(2)}, u32[]{:S(2)}) %collective-permute-start.36) | collective-permute-done | bytes 1048608 | tf_op jit(solution)/shard_map/ppermute | solution.py:464
  253.1 17.5 %collective-permute-done.47.refs_2_ = bf16[2048,256]{1,0:T(8,128)(2,1)S(1)} collective-permute-done((bf16[2048,256]{1,0:T(8,128)(2,1)S(1)}, bf16[2048,256]{1,0:T(8,128)(2,1)S(1)}, u32[]{:S(2)}, u32[]{:S(2)}) %collective-permute-start.47) | collective-permute-done | bytes 1048608 | tf_op jit(solution)/shard_map/ppermute | solution.py:464
  300.1 15.5 %collective-permute-done.42 = bf16[2048,256]{1,0:T(8,128)(2,1)} collective-permute-done((bf16[2048,256]{1,0:T(8,128)(2,1)}, bf16[2048,256]{1,0:T(8,128)(2,1)}, u32[]{:S(2)}, u32[]{:S(2)}) %collective-permute-start.42) | collective-permute-done | bytes 1048608 | tf_op jit(solution)/shard_map/ppermute | solution.py:464
  325.0 53.8 %feed_forward.2 = (bf16[2048,2048]{1,0:T(8,128)(2,1)}, bf16[2048,2048]{1,0:T(8,128)(2,1)}, bf16[2048,704]{1,0:T(8,128)(2,1)}, bf16[2048,704]{1,0:T(8,128)(2,1)},...) custom-call(s32[1]{0:T(128)} %bitcast.1.spot_ref, ...), custom_call_target="tpu_custom_call" | custom-call | flops 21600000000 | tf_op jit(solution)/shard_map/feed_forward/pallas_call | solution.py:698
  389.8 11.5 %fusion.49 = f32[704,2048]{1,0:T(8,128)} fusion(bf16[2048,704]{1,0:T(8,128)(2,1)} %get-tuple-element.489, bf16[2048,2048]{1,0:T(8,128)(2,1)} %get-tuple-element.490), kind=kOutput, calls=%fused_computation.152 | convolution fusion | flops 5905580032 | bytes 17039360 | tf_op jit(solution)/shard_map/dot_general | solution.py:33
  416.1 54.7 %feed_forward.3 = (bf16[2048,2048]{1,0:T(8,128)(2,1)}, bf16[2048,2048]{1,0:T(8,128)(2,1)}, bf16[2048,704]{1,0:T(8,128)(2,1)}, bf16[2048,704]{1,0:T(8,128)(2,1)},...) custom-call(s32[1]{0:T(128)} %bitcast.1.spot_ref, ...), custom_call_target="tpu_custom_call" | custom-call | flops 21600000000 | tf_op jit(solution)/shard_map/feed_forward/pallas_call | solution.py:698
  470.8 11.8 %fusion.50 = f32[704,2048]{1,0:T(8,128)} fusion(bf16[2048,704]{1,0:T(8,128)(2,1)} %get-tuple-element.537, bf16[2048,2048]{1,0:T(8,128)(2,1)} %get-tuple-element.541), kind=kOutput, calls=%fused_computation.153 | convolution fusion | flops 5905580032 | bytes 17039360 | tf_op jit(solution)/shard_map/dot_general | solution.py:33
  482.6 10.4 %fusion.51 = f32[704,2048]{1,0:T(8,128)} fusion(bf16[2048,704]{1,0:T(8,128)(2,1)S(1)} %copy-done.109, bf16[2048,2048]{1,0:T(8,128)(2,1)} %get-tuple-element.541), kind=kOutput, calls=%fused_computation.154 | convolution fusion | flops 5905580032 | bytes 17039360 | tf_op jit(solution)/shard_map/dot_general | solution.py:33
  498.0 11.5 %add_convert_fusion.3 = bf16[704,2048]{1,0:T(8,128)(2,1)} fusion(f32[704,2048]{1,0:T(8,128)} %fusion.49, bf16[2048,704]{1,0:T(8,128)(2,1)} %get-tuple-element.577, bf16[2048,2048]{1,0:T(8,128)(2,1)} %get-tuple-element.578), kind=kOutput, calls=%fused_computation.3 | convolution fusion | flops 5908463616 | bytes 19922944 | tf_op jit(solution)/shard_map/dot_general | solution.py:33
  550.1 9.9 %fusion.53 = f32[704,2048]{1,0:T(8,128)S(1)} fusion(bf16[2048,704]{1,0:T(8,128)(2,1)} %get-tuple-element.572, bf16[2048,2048]{1,0:T(8,128)(2,1)} %get-tuple-element.601), kind=kOutput, calls=%fused_computation.156 | convolution fusion | flops 5905580032 | bytes 17039360 | tf_op jit(solution)/shard_map/dot_general | solution.py:33
  588.3 34.3 %mix_backward.2 = (bf16[1,2048,896]{2,1,0:T(8,128)(2,1)}, f32[1,2048,128]{2,1,0:T(8,128)}, f32[32,768]{1,0:T(8,128)}, f32[8,128]{1,0:T(8,128)}) custom-call(f32[1,16,16,128]{3,2,1,0:T(8,128)} %concatenate.27.marks_ref, f32[8,768]{1,0:T(8,128)} %pad.37.taps_ref, f32[1,128]{1,0:T(1,128)} %reshape.349.gain_ref, f32[1,2048,256]{2,1,0:T(8,128)} %get-tuple-element.612.o_ref, ...), custom_call_target="tpu_custom_call" | custom-call | flops 13600000000 | tf_op jit(solution)/shard_map/mix_backward/pallas_call | solution.py:435
  630.0 13.1 %spread.6 = (bf16[2048,256]{1,0:T(8,128)(2,1)}, bf16[2048,256]{1,0:T(8,128)(2,1)}, bf16[2048,256]{1,0:T(8,128)(2,1)}, bf16[2048,256]{1,0:T(8,128)(2,1)}, bf16[20...) custom-call(s32[1]{0:T(128)} %bitcast.1.spot_ref, ...), custom_call_target="tpu_custom_call" | custom-call | flops 5600000000 | tf_op jit(solution)/shard_map/spread/pallas_call | solution.py:698
  646.0 15.0 %fusion.54 = f32[2048,896]{1,0:T(8,128)} fusion(bf16[2048,2048]{1,0:T(8,128)(2,1)} %get-tuple-element.611, bf16[2048,896]{1,0:T(8,128)(2,1)} %bitcast.203), kind=kOutput, calls=%fused_computation.157 | convolution fusion | flops 7516192768 | bytes 19398656 | tf_op jit(solution)/shard_map/dot_general | solution.py:33
  728.7 34.6 %mix_backward.3 = (bf16[1,2048,896]{2,1,0:T(8,128)(2,1)}, f32[1,2048,128]{2,1,0:T(8,128)}, f32[32,768]{1,0:T(8,128)}, f32[8,128]{1,0:T(8,128)}) custom-call(f32[1,16,16,128]{3,2,1,0:T(8,128)} %concatenate.30.marks_ref, f32[8,768]{1,0:T(8,128)} %pad.37.taps_ref, f32[1,128]{1,0:T(1,128)} %reshape.349.gain_ref, f32[1,2048,256]{2,1,0:T(8,128)} %get-tuple-element.448.o_ref, ...), custom_call_target="tpu_custom_call" | custom-call | flops 13600000000 | tf_op jit(solution)/shard_map/mix_backward/pallas_call | solution.py:435
  773.2 14.8 %add_convert_fusion = bf16[2048,896]{1,0:T(8,128)(2,1)} fusion(f32[2048,896]{1,0:T(8,128)} %fusion.54, bf16[2048,2048]{1,0:T(8,128)(2,1)} %get-tuple-element.677, bf16[2048,896]{1,0:T(8,128)(2,1)} %bitcast.204), kind=kOutput, calls=%fused_computation | convolution fusion | flops 7519862784 | bytes 23068672 | tf_op jit(solution)/shard_map/dot_general | solution.py:33
  788.1 13.3 %spread.7 = (bf16[2048,256]{1,0:T(8,128)(2,1)}, bf16[2048,256]{1,0:T(8,128)(2,1)}, bf16[2048,256]{1,0:T(8,128)(2,1)}, bf16[2048,256]{1,0:T(8,128)(2,1)}, bf16[20...) custom-call(s32[1]{0:T(128)} %bitcast.1.spot_ref, ...), custom_call_target="tpu_custom_call" | custom-call | flops 5600000000 | tf_op jit(solution)/shard_map/spread/pallas_call | solution.py:698
  830.7 10.0 %collective-permute-done.136 = bf16[2048,128]{1,0:T(8,128)(2,1)S(1)} collective-permute-done((bf16[2048,128]{1,0:T(8,128)(2,1)S(1)}, bf16[2048,128]{1,0:T(8,128)(2,1)S(1)}, u32[]{:S(2)}, u32[]{:S(2)}) %collective-permute-start.136) | collective-permute-done | bytes 524320 | tf_op jit(solution)/shard_map/ppermute | solution.py:464
  852.7 13.8 %collective-permute-done.149 = f32[128]{0:T(128)} collective-permute-done((f32[128]{0:T(128)}, f32[128]{0:T(128)}, u32[]{:S(2)}, u32[]{:S(2)}) %collective-permute-start.149) | collective-permute-done | bytes 544 | tf_op jit(solution)/shard_map/ppermute | solution.py:464
  (732 shorter events, 419.0 us)
Async XLA Ops:
  7.3 94.7 %all-gather.13.cloned.1.call-start = ((), (), s32[]{:S(2)}) async-start(), calls=%async_computation.13 | async-start | bytes 4587520 | tf_op jit(solution)/shard_map/all_gather | solution.py:821
  10.4 133.2 %all-gather.11.cloned.1.call-start = ((), (), s32[]{:S(2)}) async-start(), calls=%async_computation.12 | async-start | bytes 1310720 | tf_op jit(solution)/shard_map/all_gather | solution.py:822
  14.5 177.9 %all-gather.15.cloned.1.call-start = ((), (), s32[]{:S(2)}) async-start(), calls=%async_computation.14 | async-start | bytes 3604480 | tf_op jit(solution)/shard_map/all_gather | solution.py:823
  24.8 218.8 %all-gather.17.cloned.1.call-start = ((), (), s32[]{:S(2)}) async-start(), calls=%async_computation.15 | async-start | bytes 3604480 | tf_op jit(solution)/shard_map/all_gather | solution.py:824
  98.4 56.0 %collective-permute-start.27 = (bf16[2048,256]{1,0:T(8,128)(2,1)}, bf16[2048,256]{1,0:T(8,128)(2,1)}, u32[]{:S(2)}, u32[]{:S(2)}) collective-permute-start(bf16[2048,256]{1,0:T(8,128)(2,1)} %get-tuple-element.465.refs_10_), channel_id=1, source_target_pairs={{0,2},{1,3},{2,0},{3,1},{4,6},{5,7},{6,4},{7,5},{8,10},{9,11},{10,... | collective-permute-start | bytes 3145736 | tf_op jit(solution)/shard_map/ppermute | solution.py:464
  99.3 56.2 %collective-permute-start.32 = (bf16[2048,256]{1,0:T(8,128)(2,1)}, bf16[2048,256]{1,0:T(8,128)(2,1)}, u32[]{:S(2)}, u32[]{:S(2)}) collective-permute-start(bf16[2048,256]{1,0:T(8,128)(2,1)} %get-tuple-element.510.refs_8_), channel_id=1, source_target_pairs={{0,4},{1,5},{2,6},{3,7},{4,0},{5,1},{6,2},{7,3},{8,12},{9,13},{10,... | collective-permute-start | bytes 3145736 | tf_op jit(solution)/shard_map/ppermute | solution.py:464
  100.8 56.6 %collective-permute-start.31 = (bf16[2048,256]{1,0:T(8,128)(2,1)}, bf16[2048,256]{1,0:T(8,128)(2,1)}, u32[]{:S(2)}, u32[]{:S(2)}) collective-permute-start(bf16[2048,256]{1,0:T(8,128)(2,1)} %get-tuple-element.510.refs_8_), channel_id=1, source_target_pairs={{0,2},{1,3},{2,0},{3,1},{4,6},{5,7},{6,4},{7,5},{8,10},{9,11},{10,... | collective-permute-start | bytes 3145736 | tf_op jit(solution)/shard_map/ppermute | solution.py:464
  150.5 174.5 %all-gather.19.cloned.1.call-start = ((), (), s32[]{:S(2)}) async-start(), calls=%async_computation.16 | async-start | bytes 3604480 | tf_op jit(solution)/shard_map/all_gather | solution.py:825
  167.4 71.5 %collective-permute-start.18 = (bf16[2048,256]{1,0:T(8,128)(2,1)}, bf16[2048,256]{1,0:T(8,128)(2,1)}, u32[]{:S(2)}, u32[]{:S(2)}) collective-permute-start(bf16[2048,256]{1,0:T(8,128)(2,1)} %get-tuple-element.380), channel_id=1, source_target_pairs={{0,1},{1,0},{2,3},{3,2},{4,5},{5,4},{6,7},{7,6},{8,9},{9,8},{10,11... | collective-permute-start | bytes 3145736 | tf_op jit(solution)/shard_map/ppermute | solution.py:464
  244.1 252.9 %reduce-scatter.7.cloned.1.call-start = ((), (), s32[]{:S(2)}) async-start(), calls=%async_computation.6 | async-start | bytes 9437184 | tf_op jit(solution)/shard_map/reduce_scatter | solution.py:933
  321.3 57.5 %collective-permute-start.62 = (bf16[2048,256]{1,0:T(8,128)(2,1)S(1)}, bf16[2048,256]{1,0:T(8,128)(2,1)S(1)}, u32[]{:S(2)}, u32[]{:S(2)}) collective-permute-start(bf16[2048,256]{1,0:T(8,128)(2,1)S(1)} %get-tuple-element.502.refs_0_), channel_id=1, source_target_pairs={{0,6},{1,7},{2,4},{3,5},{4,2},{5,3},{6,0},{7,1},{8,14},{9,15},{10,... | collective-permute-start | bytes 3145736 | tf_op jit(solution)/shard_map/ppermute | solution.py:464
  322.9 55.9 %collective-permute-start.61 = (bf16[2048,256]{1,0:T(8,128)(2,1)S(1)}, bf16[2048,256]{1,0:T(8,128)(2,1)S(1)}, u32[]{:S(2)}, u32[]{:S(2)}) collective-permute-start(bf16[2048,256]{1,0:T(8,128)(2,1)S(1)} %get-tuple-element.502.refs_0_), channel_id=1, source_target_pairs={{0,4},{1,5},{2,6},{3,7},{4,0},{5,1},{6,2},{7,3},{8,12},{9,13},{10,... | collective-permute-start | bytes 3145736 | tf_op jit(solution)/shard_map/ppermute | solution.py:464
  380.1 242.5 %reduce-scatter.9.cloned.1.call-start = ((), (), s32[]{:S(2)}) async-start(), calls=%async_computation.7 | async-start | bytes 3604480 | tf_op jit(solution)/shard_map/reduce_scatter | solution.py:779
  411.5 81.6 %collective-permute-start.77 = (bf16[2048,256]{1,0:T(8,128)(2,1)}, bf16[2048,256]{1,0:T(8,128)(2,1)}, u32[]{:S(2)}, u32[]{:S(2)}) collective-permute-start(bf16[2048,256]{1,0:T(8,128)(2,1)} %add_convert_fusion.20), channel_id=1, source_target_pairs={{0,4},{1,5},{2,6},{3,7},{4,0},{5,1},{6,2},{7,3},{8,12},{9,13},{10,... | collective-permute-start | bytes 3145736 | tf_op jit(solution)/shard_map/ppermute | solution.py:464
  413.0 80.1 %collective-permute-start.76 = (bf16[2048,256]{1,0:T(8,128)(2,1)}, bf16[2048,256]{1,0:T(8,128)(2,1)}, u32[]{:S(2)}, u32[]{:S(2)}) collective-permute-start(bf16[2048,256]{1,0:T(8,128)(2,1)} %add_convert_fusion.21), channel_id=1, source_target_pairs={{0,2},{1,3},{2,0},{3,1},{4,6},{5,7},{6,4},{7,5},{8,10},{9,11},{10,... | collective-permute-start | bytes 3145736 | tf_op jit(solution)/shard_map/ppermute | solution.py:464
  414.0 79.1 %collective-permute-start.78 = (bf16[2048,256]{1,0:T(8,128)(2,1)}, bf16[2048,256]{1,0:T(8,128)(2,1)}, u32[]{:S(2)}, u32[]{:S(2)}) collective-permute-start(bf16[2048,256]{1,0:T(8,128)(2,1)} %add_convert_fusion.19), channel_id=1, source_target_pairs={{0,6},{1,7},{2,4},{3,5},{4,2},{5,3},{6,0},{7,1},{8,14},{9,15},{10,... | collective-permute-start | bytes 3145736 | tf_op jit(solution)/shard_map/ppermute | solution.py:464
  509.5 263.7 %reduce-scatter.11.cloned.1.call-start = ((), (), s32[]{:S(2)}) async-start(), calls=%async_computation.8 | async-start | bytes 3604480 | tf_op jit(solution)/shard_map/reduce_scatter | solution.py:779
  544.2 229.0 %reduce-scatter.13.cloned.1.call-start = ((), (), s32[]{:S(2)}) async-start(), calls=%async_computation.9 | async-start | bytes 3604480 | tf_op jit(solution)/shard_map/reduce_scatter | solution.py:779
  643.1 130.2 %reduce-scatter.15.cloned.1.call-start = ((), (), s32[]{:S(2)}) async-start(), calls=%async_computation.10 | async-start | bytes 1310720 | tf_op jit(solution)/shard_map/reduce_scatter | solution.py:779
  713.7 181.1 %reduce-scatter.17.cloned.1.call-start = ((), (), s32[]{:S(2)}) async-start(), calls=%async_computation.11 | async-start | bytes 4587520 | tf_op jit(solution)/shard_map/reduce_scatter | solution.py:779
  726.8 87.0 %collective-permute-start.127 = (bf16[2048,256]{1,0:T(8,128)(2,1)}, bf16[2048,256]{1,0:T(8,128)(2,1)}, u32[]{:S(2)}, u32[]{:S(2)}) collective-permute-start(bf16[2048,256]{1,0:T(8,128)(2,1)} %add_convert_fusion.15), channel_id=1, source_target_pairs={{0,2},{1,3},{2,0},{3,1},{4,6},{5,7},{6,4},{7,5},{8,10},{9,11},{10,... | collective-permute-start | bytes 3145736 | tf_op jit(solution)/shard_map/ppermute | solution.py:464
  727.8 92.0 %collective-permute-start.128 = (bf16[2048,256]{1,0:T(8,128)(2,1)}, bf16[2048,256]{1,0:T(8,128)(2,1)}, u32[]{:S(2)}, u32[]{:S(2)}) collective-permute-start(bf16[2048,256]{1,0:T(8,128)(2,1)} %add_convert_fusion.14), channel_id=1, source_target_pairs={{0,4},{1,5},{2,6},{3,7},{4,0},{5,1},{6,2},{7,3},{8,12},{9,13},{10,... | collective-permute-start | bytes 3145736 | tf_op jit(solution)/shard_map/ppermute | solution.py:464
  763.3 56.5 %collective-permute-start.129 = (bf16[2048,256]{1,0:T(8,128)(2,1)S(1)}, bf16[2048,256]{1,0:T(8,128)(2,1)}, u32[]{:S(2)}, u32[]{:S(2)}) collective-permute-start(bf16[2048,256]{1,0:T(8,128)(2,1)S(1)} %copy-done.13), channel_id=1, source_target_pairs={{0,6},{1,7},{2,4},{3,5},{4,2},{5,3},{6,0},{7,1},{8,14},{9,15},{10,... | collective-permute-start | bytes 3145736 | tf_op jit(solution)/shard_map/ppermute | solution.py:464
  819.8 61.0 %collective-permute-start.135 = (bf16[2048,256]{1,0:T(8,128)(2,1)}, bf16[2048,256]{1,0:T(8,128)(2,1)}, u32[]{:S(2)}, u32[]{:S(2)}) collective-permute-start(bf16[2048,256]{1,0:T(8,128)(2,1)} %get-tuple-element.680), channel_id=1, source_target_pairs={{0,1},{1,0},{2,3},{3,2},{4,5},{5,4},{6,7},{7,6},{8,9},{9,8},{10,11... | collective-permute-start | bytes 3145736 | tf_op jit(solution)/shard_map/ppermute | solution.py:464
  (253 other events, 3383.1 us)
Sparse Core Ops, SparseCore 0:
  10.6 77.5 all-gather.12
  89.7 26.5 all-gather.10
  117.8 58.6 all-gather.14
  178.0 57.8 all-gather.16
  244.2 59.3 all-gather.18
  380.2 108.0 reduce-scatter.6
  509.7 56.8 reduce-scatter.8
  569.0 55.9 reduce-scatter.10
  643.2 56.6 reduce-scatter.12
  713.9 27.2 reduce-scatter.14
  811.0 68.7 reduce-scatter.16

commit v4 on v3

--- a/solution.py
+++ b/solution.py
@@ -990,14 +990,6 @@
             )
             qkv_grad = (sum(qkv_terms) + dot_tn(act_ones[m], dpre)).astype(BF)
             dpre = after(dpre, qkv_grad)
-            dconv, dgain, gain_two_grad = after((dconv, dgain, gain_two_grad), qkv_grad)
-            conv_sum = dconv.reshape(4, 8, 3, hw).sum(axis=1).transpose(1, 2, 0)
-            early = sum_over(
-                jnp.concatenate(
-                    [conv_sum.reshape(-1), jnp.sum(dgain, axis=0), gain_two_grad]
-                ),
-                "row", rows_ways,
-            )
             grad_qkv = scatter_row(qkv_grad, 0)
             sums = spread(dpre, qkv, spot, block, ways, True)
             arrived = send_pairs(sums, ways)
@@ -1009,6 +1001,16 @@
                 for resid, out in zip(late_resids[:-1], ffn_outs)
             ] + [(late_resids[-1] + total_of(out_own, flown)).astype(BF)]
             arrived = scatter_cols(pairs, ways, "split")
+            dconv, dgain, gain_two_grad = after(
+                (dconv, dgain, gain_two_grad), arrays_of(pairs)
+            )
+            conv_sum = dconv.reshape(4, 8, 3, hw).sum(axis=1).transpose(1, 2, 0)
+            early = sum_over(
+                jnp.concatenate(
+                    [conv_sum.reshape(-1), jnp.sum(dgain, axis=0), gain_two_grad]
+                ),
+                "row", rows_ways,
+            )
             firsts[0] = after(firsts[0][0], arrays_of(pairs)), firsts[0][1]
             stat, early = after((stat, early), arrays_of(pairs))
             means.append(sum_cols(stat.reshape(tokens, 128)[:, 0], ways)[:, None] / width)

time: 916 us -> 921 us (level)
  transfers between devices with their start and end apart: 161 -> 161, of which waited for: 55 -> 56; matrix products, arithmetic and copies ran while one was open for 27% -> 27% of each run, Pallas kernels for 35% -> 35%
where the time goes in v4:
time: 921 us; the launch traced here: 911 us
  Pallas kernels  317 us (34%)
  waiting for transfers between devices  200 us (22%)
  starting transfers between devices  110 us (12%)
  matrix products  108 us (12%)
  other arithmetic  93.5 us (10%)
  local copies, waits for them, and re-layouts  66.5 us (7%)
  between operations  15.7 us (2%)
    pallas_call x10, Pallas kernels, tiled(): pl.pallas_call(kernel, grid=(rows // tile,), in_specs=[SPOT] + [fixed(a)...  200 us
    ppermute x141, waiting for transfers between devices, swap(): return lax.ppermute(values, 'col', [(i, i ^ bit) for i in range(ways)])  181 us
    dot_general x10, matrix products, dot_tn(): lax.dot_general(a, b, (((0,), (0,)), ((), ())), preferred_element_type=F32)  108 us
    ppermute x141, starting transfers between devices, swap(): return lax.ppermute(values, 'col', [(i, i ^ bit) for i in range(ways)])  92 us
    pallas_call x2, Pallas kernels, mix_backward(): pl.pallas_call(partial(mix_bwd_kernel, heads, chunk, sub), grid=(steps,),...  68.8 us
    pallas_call x2, Pallas kernels, mix_forward(): pl.pallas_call(partial(mix_fwd_kernel, heads, chunk, sub), grid=(steps,),...  48.4 us
    convert_element_type x25, other arithmetic, add_low(): return sum((term.astype(F32) for term in terms)).astype(BF)  37.8 us
    ppermute x9, waiting for transfers between devices, sum_over(): lax.ppermute(values, axis, [(i, i ^ bit) for i in range(size)])  18.8 us
  transfers between devices with their start and end apart: 161, of which 56 were waited for; matrix products, arithmetic and copies ran while one was open for 27% of the time, Pallas kernels for 35%

profile of v4, /device:TPU:0, one launch (start us, length us, event | category | flops | bytes accessed | tf_op | source)
XLA Modules:
  0.0 911.0 jit_solution(4364819948369184680)
XLA Ops:
  24.8 19.6 %collective-permute-done.6.refs_2_ = bf16[2048,256]{1,0:T(8,128)(2,1)} collective-permute-done((bf16[2048,256]{1,0:T(8,128)(2,1)}, bf16[2048,256]{1,0:T(8,128)(2,1)}, u32[]{:S(2)}, u32[]{:S(2)}) %collective-permute-start.6) | collective-permute-done | bytes 1048608 | tf_op jit(solution)/shard_map/ppermute | solution.py:464
  58.2 9.3 %collective-permute-done.3 = bf16[32,928]{1,0:T(8,128)(2,1)S(1)} collective-permute-done((bf16[32,928]{1,0:T(8,128)(2,1)S(1)}, bf16[32,928]{1,0:T(8,128)(2,1)S(1)}, u32[]{:S(2)}, u32[]{:S(2)}) %collective-permute-start.3) | collective-permute-done | bytes 59424 | tf_op jit(solution)/shard_map/ppermute | solution.py:566
  102.0 17.4 %project.2 = (f32[2048,896]{1,0:T(8,128)}, bf16[2048,2048]{1,0:T(8,128)(2,1)}, f32[2048,128]{1,0:T(8,128)}) custom-call(s32[1]{0:T(128)} %bitcast.1.spot_ref, f32[1,2048]{1,0:T(1,128)} %reshape.398.gain_ref, bf16[2048,896]{1,0:T(8,128)(2,1)} %all-gather.13.cloned.1.call-done.weight_ref, bf16[2048,256]{1,0:T(8,128)(2,1)} %get-tuple-element.374.refs_0_, ...), custom_call_target="tpu_custom_call" | custom-call | flops 7600000000 | tf_op jit(solution)/shard_map/project/pallas_call | solution.py:698
  119.4 24.2 %mix_forward.2 = (bf16[1,2048,256]{2,1,0:T(8,128)(2,1)}, f32[1,2048,256]{2,1,0:T(8,128)}, bf16[1,2048,256]{2,1,0:T(8,128)(2,1)}, bf16[1,2048,256]{2,1,0:T(8,128)...) custom-call(f32[1,16,16,128]{3,2,1,0:T(8,128)} %concatenate.27.marks_ref, ...), custom_call_target="tpu_custom_call" | custom-call | flops 9600000000 | tf_op jit(solution)/shard_map/mix_forward/pallas_call | solution.py:395
  173.1 17.3 %project.3 = (f32[2048,896]{1,0:T(8,128)}, bf16[2048,2048]{1,0:T(8,128)(2,1)}, f32[2048,128]{1,0:T(8,128)}) custom-call(s32[1]{0:T(128)} %bitcast.1.spot_ref, f32[1,2048]{1,0:T(1,128)} %reshape.398.gain_ref, bf16[2048,896]{1,0:T(8,128)(2,1)} %all-gather.13.cloned.1.call-done.weight_ref, bf16[2048,256]{1,0:T(8,128)(2,1)} %copy-done.41, ...), custom_call_target="tpu_custom_call" | custom-call | flops 7600000000 | tf_op jit(solution)/shard_map/project/pallas_call | solution.py:698
  194.8 24.2 %mix_forward.3 = (bf16[1,2048,256]{2,1,0:T(8,128)(2,1)}, f32[1,2048,256]{2,1,0:T(8,128)}, bf16[1,2048,256]{2,1,0:T(8,128)(2,1)}, bf16[1,2048,256]{2,1,0:T(8,128)...) custom-call(f32[1,16,16,128]{3,2,1,0:T(8,128)} %concatenate.30.marks_ref, ...), custom_call_target="tpu_custom_call" | custom-call | flops 9600000000 | tf_op jit(solution)/shard_map/mix_forward/pallas_call | solution.py:395
  225.3 13.5 %collective-permute-done.36 = bf16[2048,256]{1,0:T(8,128)(2,1)} collective-permute-done((bf16[2048,256]{1,0:T(8,128)(2,1)}, bf16[2048,256]{1,0:T(8,128)(2,1)}, u32[]{:S(2)}, u32[]{:S(2)}) %collective-permute-start.36) | collective-permute-done | bytes 1048608 | tf_op jit(solution)/shard_map/ppermute | solution.py:464
  253.0 17.5 %collective-permute-done.47.refs_2_ = bf16[2048,256]{1,0:T(8,128)(2,1)S(1)} collective-permute-done((bf16[2048,256]{1,0:T(8,128)(2,1)S(1)}, bf16[2048,256]{1,0:T(8,128)(2,1)S(1)}, u32[]{:S(2)}, u32[]{:S(2)}) %collective-permute-start.47) | collective-permute-done | bytes 1048608 | tf_op jit(solution)/shard_map/ppermute | solution.py:464
  300.0 15.5 %collective-permute-done.42 = bf16[2048,256]{1,0:T(8,128)(2,1)} collective-permute-done((bf16[2048,256]{1,0:T(8,128)(2,1)}, bf16[2048,256]{1,0:T(8,128)(2,1)}, u32[]{:S(2)}, u32[]{:S(2)}) %collective-permute-start.42) | collective-permute-done | bytes 1048608 | tf_op jit(solution)/shard_map/ppermute | solution.py:464
  324.9 53.8 %feed_forward.2 = (bf16[2048,2048]{1,0:T(8,128)(2,1)}, bf16[2048,2048]{1,0:T(8,128)(2,1)}, bf16[2048,704]{1,0:T(8,128)(2,1)}, bf16[2048,704]{1,0:T(8,128)(2,1)},...) custom-call(s32[1]{0:T(128)} %bitcast.1.spot_ref, ...), custom_call_target="tpu_custom_call" | custom-call | flops 21600000000 | tf_op jit(solution)/shard_map/feed_forward/pallas_call | solution.py:698
  389.7 11.6 %fusion.49 = f32[704,2048]{1,0:T(8,128)} fusion(bf16[2048,704]{1,0:T(8,128)(2,1)} %get-tuple-element.489, bf16[2048,2048]{1,0:T(8,128)(2,1)} %get-tuple-element.490), kind=kOutput, calls=%fused_computation.152 | convolution fusion | flops 5905580032 | bytes 17039360 | tf_op jit(solution)/shard_map/dot_general | solution.py:33
  416.2 54.6 %feed_forward.3 = (bf16[2048,2048]{1,0:T(8,128)(2,1)}, bf16[2048,2048]{1,0:T(8,128)(2,1)}, bf16[2048,704]{1,0:T(8,128)(2,1)}, bf16[2048,704]{1,0:T(8,128)(2,1)},...) custom-call(s32[1]{0:T(128)} %bitcast.1.spot_ref, ...), custom_call_target="tpu_custom_call" | custom-call | flops 21600000000 | tf_op jit(solution)/shard_map/feed_forward/pallas_call | solution.py:698
  470.8 11.8 %fusion.50 = f32[704,2048]{1,0:T(8,128)} fusion(bf16[2048,704]{1,0:T(8,128)(2,1)} %get-tuple-element.537, bf16[2048,2048]{1,0:T(8,128)(2,1)} %get-tuple-element.541), kind=kOutput, calls=%fused_computation.153 | convolution fusion | flops 5905580032 | bytes 17039360 | tf_op jit(solution)/shard_map/dot_general | solution.py:33
  482.6 10.5 %fusion.51 = f32[704,2048]{1,0:T(8,128)} fusion(bf16[2048,704]{1,0:T(8,128)(2,1)S(1)} %copy-done.108, bf16[2048,2048]{1,0:T(8,128)(2,1)} %get-tuple-element.541), kind=kOutput, calls=%fused_computation.154 | convolution fusion | flops 5905580032 | bytes 17039360 | tf_op jit(solution)/shard_map/dot_general | solution.py:33
  498.9 11.5 %add_convert_fusion.3 = bf16[704,2048]{1,0:T(8,128)(2,1)} fusion(f32[704,2048]{1,0:T(8,128)} %fusion.49, bf16[2048,704]{1,0:T(8,128)(2,1)} %get-tuple-element.577, bf16[2048,2048]{1,0:T(8,128)(2,1)} %get-tuple-element.578), kind=kOutput, calls=%fused_computation.3 | convolution fusion | flops 5908463616 | bytes 19922944 | tf_op jit(solution)/shard_map/dot_general | solution.py:33
  550.3 9.9 %fusion.53 = f32[704,2048]{1,0:T(8,128)S(1)} fusion(bf16[2048,704]{1,0:T(8,128)(2,1)} %get-tuple-element.572, bf16[2048,2048]{1,0:T(8,128)(2,1)} %get-tuple-element.601), kind=kOutput, calls=%fused_computation.156 | convolution fusion | flops 5905580032 | bytes 17039360 | tf_op jit(solution)/shard_map/dot_general | solution.py:33
  589.3 34.2 %mix_backward.2 = (bf16[1,2048,896]{2,1,0:T(8,128)(2,1)}, f32[1,2048,128]{2,1,0:T(8,128)}, f32[32,768]{1,0:T(8,128)}, f32[8,128]{1,0:T(8,128)}) custom-call(f32[1,16,16,128]{3,2,1,0:T(8,128)} %concatenate.27.marks_ref, f32[8,768]{1,0:T(8,128)} %pad.37.taps_ref, f32[1,128]{1,0:T(1,128)} %reshape.349.gain_ref, f32[1,2048,256]{2,1,0:T(8,128)} %get-tuple-element.612.o_ref, ...), custom_call_target="tpu_custom_call" | custom-call | flops 13600000000 | tf_op jit(solution)/shard_map/mix_backward/pallas_call | solution.py:435
  630.2 13.1 %spread.6 = (bf16[2048,256]{1,0:T(8,128)(2,1)}, bf16[2048,256]{1,0:T(8,128)(2,1)}, bf16[2048,256]{1,0:T(8,128)(2,1)}, bf16[2048,256]{1,0:T(8,128)(2,1)}, bf16[20...) custom-call(s32[1]{0:T(128)} %bitcast.1.spot_ref, ...), custom_call_target="tpu_custom_call" | custom-call | flops 5600000000 | tf_op jit(solution)/shard_map/spread/pallas_call | solution.py:698
  646.3 14.8 %fusion.54 = f32[2048,896]{1,0:T(8,128)} fusion(bf16[2048,2048]{1,0:T(8,128)(2,1)} %get-tuple-element.611, bf16[2048,896]{1,0:T(8,128)(2,1)} %bitcast.203), kind=kOutput, calls=%fused_computation.157 | convolution fusion | flops 7516192768 | bytes 19398656 | tf_op jit(solution)/shard_map/dot_general | solution.py:33
  697.8 9.1 collect.3
  729.5 34.6 %mix_backward.3 = (bf16[1,2048,896]{2,1,0:T(8,128)(2,1)}, f32[1,2048,128]{2,1,0:T(8,128)}, f32[32,768]{1,0:T(8,128)}, f32[8,128]{1,0:T(8,128)}) custom-call(f32[1,16,16,128]{3,2,1,0:T(8,128)} %concatenate.30.marks_ref, f32[8,768]{1,0:T(8,128)} %pad.37.taps_ref, f32[1,128]{1,0:T(1,128)} %reshape.349.gain_ref, f32[1,2048,256]{2,1,0:T(8,128)} %get-tuple-element.448.o_ref, ...), custom_call_target="tpu_custom_call" | custom-call | flops 13600000000 | tf_op jit(solution)/shard_map/mix_backward/pallas_call | solution.py:435
  773.7 14.8 %add_convert_fusion = bf16[2048,896]{1,0:T(8,128)(2,1)} fusion(f32[2048,896]{1,0:T(8,128)} %fusion.54, bf16[2048,2048]{1,0:T(8,128)(2,1)} %get-tuple-element.677, bf16[2048,896]{1,0:T(8,128)(2,1)} %bitcast.204), kind=kOutput, calls=%fused_computation | convolution fusion | flops 7519862784 | bytes 23068672 | tf_op jit(solution)/shard_map/dot_general | solution.py:33
  788.5 13.2 %spread.7 = (bf16[2048,256]{1,0:T(8,128)(2,1)}, bf16[2048,256]{1,0:T(8,128)(2,1)}, bf16[2048,256]{1,0:T(8,128)(2,1)}, bf16[2048,256]{1,0:T(8,128)(2,1)}, bf16[20...) custom-call(s32[1]{0:T(128)} %bitcast.1.spot_ref, ...), custom_call_target="tpu_custom_call" | custom-call | flops 5600000000 | tf_op jit(solution)/shard_map/spread/pallas_call | solution.py:698
  856.3 14.1 %collective-permute-done.149 = f32[128]{0:T(128)} collective-permute-done((f32[128]{0:T(128)}, f32[128]{0:T(128)}, u32[]{:S(2)}, u32[]{:S(2)}) %collective-permute-start.149) | collective-permute-done | bytes 544 | tf_op jit(solution)/shard_map/ppermute | solution.py:464
  (731 shorter events, 425.3 us)
Async XLA Ops:
  7.3 94.7 %all-gather.13.cloned.1.call-start = ((), (), s32[]{:S(2)}) async-start(), calls=%async_computation.13 | async-start | bytes 4587520 | tf_op jit(solution)/shard_map/all_gather | solution.py:821
  10.4 133.1 %all-gather.11.cloned.1.call-start = ((), (), s32[]{:S(2)}) async-start(), calls=%async_computation.12 | async-start | bytes 1310720 | tf_op jit(solution)/shard_map/all_gather | solution.py:822
  14.5 177.9 %all-gather.15.cloned.1.call-start = ((), (), s32[]{:S(2)}) async-start(), calls=%async_computation.14 | async-start | bytes 3604480 | tf_op jit(solution)/shard_map/all_gather | solution.py:823
  24.8 218.7 %all-gather.17.cloned.1.call-start = ((), (), s32[]{:S(2)}) async-start(), calls=%async_computation.15 | async-start | bytes 3604480 | tf_op jit(solution)/shard_map/all_gather | solution.py:824
  98.4 56.0 %collective-permute-start.27 = (bf16[2048,256]{1,0:T(8,128)(2,1)}, bf16[2048,256]{1,0:T(8,128)(2,1)}, u32[]{:S(2)}, u32[]{:S(2)}) collective-permute-start(bf16[2048,256]{1,0:T(8,128)(2,1)} %get-tuple-element.465.refs_10_), channel_id=1, source_target_pairs={{0,2},{1,3},{2,0},{3,1},{4,6},{5,7},{6,4},{7,5},{8,10},{9,11},{10,... | collective-permute-start | bytes 3145736 | tf_op jit(solution)/shard_map/ppermute | solution.py:464
  99.3 56.2 %collective-permute-start.32 = (bf16[2048,256]{1,0:T(8,128)(2,1)}, bf16[2048,256]{1,0:T(8,128)(2,1)}, u32[]{:S(2)}, u32[]{:S(2)}) collective-permute-start(bf16[2048,256]{1,0:T(8,128)(2,1)} %get-tuple-element.510.refs_8_), channel_id=1, source_target_pairs={{0,4},{1,5},{2,6},{3,7},{4,0},{5,1},{6,2},{7,3},{8,12},{9,13},{10,... | collective-permute-start | bytes 3145736 | tf_op jit(solution)/shard_map/ppermute | solution.py:464
  100.8 56.5 %collective-permute-start.31 = (bf16[2048,256]{1,0:T(8,128)(2,1)}, bf16[2048,256]{1,0:T(8,128)(2,1)}, u32[]{:S(2)}, u32[]{:S(2)}) collective-permute-start(bf16[2048,256]{1,0:T(8,128)(2,1)} %get-tuple-element.510.refs_8_), channel_id=1, source_target_pairs={{0,2},{1,3},{2,0},{3,1},{4,6},{5,7},{6,4},{7,5},{8,10},{9,11},{10,... | collective-permute-start | bytes 3145736 | tf_op jit(solution)/shard_map/ppermute | solution.py:464
  150.4 174.5 %all-gather.19.cloned.1.call-start = ((), (), s32[]{:S(2)}) async-start(), calls=%async_computation.16 | async-start | bytes 3604480 | tf_op jit(solution)/shard_map/all_gather | solution.py:825
  167.3 71.5 %collective-permute-start.18 = (bf16[2048,256]{1,0:T(8,128)(2,1)}, bf16[2048,256]{1,0:T(8,128)(2,1)}, u32[]{:S(2)}, u32[]{:S(2)}) collective-permute-start(bf16[2048,256]{1,0:T(8,128)(2,1)} %get-tuple-element.380), channel_id=1, source_target_pairs={{0,1},{1,0},{2,3},{3,2},{4,5},{5,4},{6,7},{7,6},{8,9},{9,8},{10,11... | collective-permute-start | bytes 3145736 | tf_op jit(solution)/shard_map/ppermute | solution.py:464
  244.0 253.9 %reduce-scatter.7.cloned.1.call-start = ((), (), s32[]{:S(2)}) async-start(), calls=%async_computation.6 | async-start | bytes 9437184 | tf_op jit(solution)/shard_map/reduce_scatter | solution.py:933
  321.3 57.5 %collective-permute-start.62 = (bf16[2048,256]{1,0:T(8,128)(2,1)S(1)}, bf16[2048,256]{1,0:T(8,128)(2,1)S(1)}, u32[]{:S(2)}, u32[]{:S(2)}) collective-permute-start(bf16[2048,256]{1,0:T(8,128)(2,1)S(1)} %get-tuple-element.502.refs_0_), channel_id=1, source_target_pairs={{0,6},{1,7},{2,4},{3,5},{4,2},{5,3},{6,0},{7,1},{8,14},{9,15},{10,... | collective-permute-start | bytes 3145736 | tf_op jit(solution)/shard_map/ppermute | solution.py:464
  322.9 55.9 %collective-permute-start.61 = (bf16[2048,256]{1,0:T(8,128)(2,1)S(1)}, bf16[2048,256]{1,0:T(8,128)(2,1)S(1)}, u32[]{:S(2)}, u32[]{:S(2)}) collective-permute-start(bf16[2048,256]{1,0:T(8,128)(2,1)S(1)} %get-tuple-element.502.refs_0_), channel_id=1, source_target_pairs={{0,4},{1,5},{2,6},{3,7},{4,0},{5,1},{6,2},{7,3},{8,12},{9,13},{10,... | collective-permute-start | bytes 3145736 | tf_op jit(solution)/shard_map/ppermute | solution.py:464
  323.7 55.1 %collective-permute-start.60 = (bf16[2048,256]{1,0:T(8,128)(2,1)S(1)}, bf16[2048,256]{1,0:T(8,128)(2,1)}, u32[]{:S(2)}, u32[]{:S(2)}) collective-permute-start(bf16[2048,256]{1,0:T(8,128)(2,1)S(1)} %get-tuple-element.502.refs_0_), channel_id=1, source_target_pairs={{0,2},{1,3},{2,0},{3,1},{4,6},{5,7},{6,4},{7,5},{8,10},{9,11},{10,... | collective-permute-start | bytes 3145736 | tf_op jit(solution)/shard_map/ppermute | solution.py:464
  380.1 243.5 %reduce-scatter.9.cloned.1.call-start = ((), (), s32[]{:S(2)}) async-start(), calls=%async_computation.7 | async-start | bytes 3604480 | tf_op jit(solution)/shard_map/reduce_scatter | solution.py:779
  411.5 81.6 %collective-permute-start.77 = (bf16[2048,256]{1,0:T(8,128)(2,1)}, bf16[2048,256]{1,0:T(8,128)(2,1)}, u32[]{:S(2)}, u32[]{:S(2)}) collective-permute-start(bf16[2048,256]{1,0:T(8,128)(2,1)} %add_convert_fusion.20), channel_id=1, source_target_pairs={{0,4},{1,5},{2,6},{3,7},{4,0},{5,1},{6,2},{7,3},{8,12},{9,13},{10,... | collective-permute-start | bytes 3145736 | tf_op jit(solution)/shard_map/ppermute | solution.py:464
  413.1 80.0 %collective-permute-start.76 = (bf16[2048,256]{1,0:T(8,128)(2,1)}, bf16[2048,256]{1,0:T(8,128)(2,1)}, u32[]{:S(2)}, u32[]{:S(2)}) collective-permute-start(bf16[2048,256]{1,0:T(8,128)(2,1)} %add_convert_fusion.21), channel_id=1, source_target_pairs={{0,2},{1,3},{2,0},{3,1},{4,6},{5,7},{6,4},{7,5},{8,10},{9,11},{10,... | collective-permute-start | bytes 3145736 | tf_op jit(solution)/shard_map/ppermute | solution.py:464
  414.0 80.0 %collective-permute-start.78 = (bf16[2048,256]{1,0:T(8,128)(2,1)}, bf16[2048,256]{1,0:T(8,128)(2,1)}, u32[]{:S(2)}, u32[]{:S(2)}) collective-permute-start(bf16[2048,256]{1,0:T(8,128)(2,1)} %add_convert_fusion.19), channel_id=1, source_target_pairs={{0,6},{1,7},{2,4},{3,5},{4,2},{5,3},{6,0},{7,1},{8,14},{9,15},{10,... | collective-permute-start | bytes 3145736 | tf_op jit(solution)/shard_map/ppermute | solution.py:464
  510.5 263.2 %reduce-scatter.11.cloned.1.call-start = ((), (), s32[]{:S(2)}) async-start(), calls=%async_computation.8 | async-start | bytes 3604480 | tf_op jit(solution)/shard_map/reduce_scatter | solution.py:779
  544.3 229.4 %reduce-scatter.13.cloned.1.call-start = ((), (), s32[]{:S(2)}) async-start(), calls=%async_computation.9 | async-start | bytes 3604480 | tf_op jit(solution)/shard_map/reduce_scatter | solution.py:779
  643.4 130.3 %reduce-scatter.15.cloned.1.call-start = ((), (), s32[]{:S(2)}) async-start(), calls=%async_computation.10 | async-start | bytes 1310720 | tf_op jit(solution)/shard_map/reduce_scatter | solution.py:779
  714.2 186.2 %reduce-scatter.17.cloned.1.call-start = ((), (), s32[]{:S(2)}) async-start(), calls=%async_computation.11 | async-start | bytes 4587520 | tf_op jit(solution)/shard_map/reduce_scatter | solution.py:779
  727.1 84.0 %collective-permute-start.127 = (bf16[2048,256]{1,0:T(8,128)(2,1)}, bf16[2048,256]{1,0:T(8,128)(2,1)}, u32[]{:S(2)}, u32[]{:S(2)}) collective-permute-start(bf16[2048,256]{1,0:T(8,128)(2,1)} %add_convert_fusion.15), channel_id=1, source_target_pairs={{0,2},{1,3},{2,0},{3,1},{4,6},{5,7},{6,4},{7,5},{8,10},{9,11},{10,... | collective-permute-start | bytes 3145736 | tf_op jit(solution)/shard_map/ppermute | solution.py:464
  728.3 87.5 %collective-permute-start.128 = (bf16[2048,256]{1,0:T(8,128)(2,1)}, bf16[2048,256]{1,0:T(8,128)(2,1)}, u32[]{:S(2)}, u32[]{:S(2)}) collective-permute-start(bf16[2048,256]{1,0:T(8,128)(2,1)} %add_convert_fusion.14), channel_id=1, source_target_pairs={{0,4},{1,5},{2,6},{3,7},{4,0},{5,1},{6,2},{7,3},{8,12},{9,13},{10,... | collective-permute-start | bytes 3145736 | tf_op jit(solution)/shard_map/ppermute | solution.py:464
  810.7 73.9 %collective-permute-start.135 = (bf16[2048,256]{1,0:T(8,128)(2,1)}, bf16[2048,256]{1,0:T(8,128)(2,1)}, u32[]{:S(2)}, u32[]{:S(2)}) collective-permute-start(bf16[2048,256]{1,0:T(8,128)(2,1)} %get-tuple-element.680), channel_id=1, source_target_pairs={{0,1},{1,0},{2,3},{3,2},{4,5},{5,4},{6,7},{7,6},{8,9},{9,8},{10,11... | collective-permute-start | bytes 3145736 | tf_op jit(solution)/shard_map/ppermute | solution.py:464
  (253 other events, 3308.8 us)
Sparse Core Ops, SparseCore 0:
  10.6 77.5 all-gather.12
  89.7 26.5 all-gather.10
  117.8 58.6 all-gather.14
  178.0 57.8 all-gather.16
  244.2 59.4 all-gather.18
  380.2 112.6 reduce-scatter.6
  510.6 57.2 reduce-scatter.8
  570.3 55.9 reduce-scatter.10
  643.5 57.3 reduce-scatter.12
  714.3 28.1 reduce-scatter.14
  809.6 70.2 reduce-scatter.16
